TPU v7x, 32 devices: a whole 2x2x4 slice. The times are simulated.
32 devices in a mesh: dp: 4 (over z), expert: 8 (over y, x, core).
Axes of the slice: x: 2, y: 2, z: 4, core: 2. Of those that a mesh axis runs over, the one named last changes fastest.
Arguments:
- layer_input: bfloat16 [1536, 7168], P('expert', 'dp'), may hold values from -6 to 6
- out_grad: bfloat16 [1536, 7168], P('expert', 'dp'), may hold values from -6 to 6
- routes: int32 [1536, 2], P('expert'), may hold values from 0 to 7, all different within a row; in each aligned block of 192 rows (0 to 191, 192 to 383, ...) at most 96 rows name the same one
- gate_weights: bfloat16 [1536, 2], P('expert'), may hold values from 0.049804688 to 1
- w_gate: bfloat16 [8, 7168, 1024], P('expert', 'dp'), may hold values from -0.0625 to 0.0625
- w_up: bfloat16 [8, 7168, 1024], P('expert', 'dp'), may hold values from -0.0625 to 0.0625
- w_down: bfloat16 [8, 1024, 7168], P('expert', None, 'dp'), may hold values from -0.1875 to 0.1875
Outputs:
- input_grad: bfloat16 [1536, 7168], P('expert', 'dp')
- route_grad: bfloat16 [1536, 2], P('expert')
- grad_gate: bfloat16 [8, 7168, 1024], P('expert', 'dp')
- grad_up: bfloat16 [8, 7168, 1024], P('expert', 'dp')
- grad_down: bfloat16 [8, 1024, 7168], P('expert', None, 'dp')
Inputs may be any that keep to these rules, and one draw needn't show every extreme that they name: `routes`: each row names 2 different experts. Among the 192 rows of one index of the expert axis (aligned blocks of rows), no expert is named by more than 96 rows.
All inputs are finite; a program needn't handle non-finite values.
Results may differ from a plain program's by a relative error of at most 0.024.
Values may be sent and summed in bfloat16 or wider, within the bound.
No kernel may reach another device: no remote copies, remote signals or barrier semaphores. Data moves between devices by JAX's collectives and lax.ppermute only.
A program may use at most 128 MiB of HBM per device.

v0:
```python
import functools

import jax
import jax.numpy as jnp
from jax import lax
from jax.experimental import pallas as pl
from jax.experimental.pallas import tpu as pltpu
from jax.sharding import PartitionSpec as P

BF16 = jnp.bfloat16
F32 = jnp.float32


def line_sum(part, axis, size, place):
    half = size // 2
    total = part
    for k in range(half - 1):
        pairs = [(k, k + 1), (size - 1 - k, size - 2 - k)]
        arrived = lax.ppermute(total, axis, pairs)
        total = (total.astype(F32) + arrived.astype(F32)).astype(BF16)
    arrived = lax.ppermute(total, axis, [(half - 1, half), (half, half - 1)])
    total = (total.astype(F32) + arrived.astype(F32)).astype(BF16)
    depth = jnp.where(place < half, half - 1 - place, place - half)
    for k in range(half - 1):
        pairs = [(half - 1 - k, half - 2 - k), (half + k, half + k + 1)]
        arrived = lax.ppermute(total, axis, pairs)
        total = jnp.where(depth == k + 1, arrived, total)
    return total


def activation_grads(sums, weight):
    pre_gate, pre_up, back_hidden = (one.astype(F32) for one in sums)
    sigmoid_gate = jax.nn.sigmoid(pre_gate)
    silu_gate = pre_gate * sigmoid_gate
    hidden = silu_gate * pre_up
    route_part = jnp.sum(hidden * back_hidden, axis=1, keepdims=True).astype(BF16)
    scale = weight.astype(F32)
    scaled_hidden = (scale * hidden).astype(BF16)
    gate_pre = (
        scale * back_hidden * pre_up * sigmoid_gate * (1.0 + pre_gate * (1.0 - sigmoid_gate))
    ).astype(BF16)
    up_pre = (scale * back_hidden * silu_gate).astype(BF16)
    return (scaled_hidden, gate_pre, up_pre, route_part)


LITTLE = pl.CostEstimate(flops=1, bytes_accessed=1, transcendentals=0)
LANES = 128
BLOCK = 256
OVER_LAST = (((1,), (1,)), ((), ()))


def params(mebibytes):
    return pltpu.CompilerParams(vmem_limit_bytes=mebibytes * 1024 * 1024)


def whole(shape):
    return pl.BlockSpec(shape, lambda *_: (0,) * len(shape))


def forward_kernel(n_rows, width, per_array, scalars, *refs):
    rows, (gate_ref, up_ref, down_ref, out_ref, *joined) = refs[:n_rows], refs[n_rows:]
    step = pl.program_id(0)
    rows_in = jnp.concatenate([ref[:, :width] for ref in rows], axis=0)
    rows_grad = jnp.concatenate([ref[:, width : 2 * width] for ref in rows], axis=0)
    results = (
        jnp.dot(rows_in, gate_ref[0], preferred_element_type=F32),
        jnp.dot(rows_in, up_ref[0], preferred_element_type=F32),
        lax.dot_general(rows_grad, down_ref[0], OVER_LAST, preferred_element_type=F32),
    )
    for a, result in enumerate(results):
        start = pl.multiple_of(a * per_array + step * BLOCK, BLOCK)
        out_ref[:, pl.ds(start, BLOCK)] = result.astype(BF16)
    for ref, value in zip(joined, (rows_in, rows_grad)):
        ref[...] = value


def forward_piece(scalars, rows, height, w_gate, w_up, w_down, half, per_array):
    width = w_gate.shape[1]
    steps = per_array // BLOCK
    total = height * len(rows)
    outs = [(total, 3 * per_array)] + ([(total, width)] * 2 if half == 0 else [])
    across = pl.BlockSpec((1, width, BLOCK), lambda j: (0, 0, half * steps + j))
    down = pl.BlockSpec((1, BLOCK, width), lambda j: (0, half * steps + j, 0))
    return pl.pallas_call(
        functools.partial(forward_kernel, len(rows), width, per_array),
        grid=(steps,),
        in_specs=[pl.BlockSpec(memory_space=pltpu.SMEM)]
        + [whole((height, r.shape[1])) for r in rows]
        + [across, across, down],
        out_specs=[whole(shape) for shape in outs],
        out_shape=[jax.ShapeDtypeStruct(shape, BF16) for shape in outs],
        compiler_params=params(28),
        cost_estimate=LITTLE,
    )(scalars, *rows, w_gate, w_up, w_down)


def add_kernel(a_ref, b_ref, out_ref):
    out_ref[...] = (a_ref[...].astype(F32) + b_ref[...].astype(F32)).astype(BF16)


def add_pieces(a, b):
    return pl.pallas_call(
        add_kernel,
        out_shape=jax.ShapeDtypeStruct(a.shape, BF16),
        compiler_params=params(8),
        cost_estimate=LITTLE,
    )(a, b)


def add_choose_kernel(middle_ref, a_ref, b_ref, other_ref, out_ref, both_ref):
    total = (a_ref[...].astype(F32) + b_ref[...].astype(F32)).astype(BF16)
    out_ref[...] = total
    both_ref[...] = jnp.where(middle_ref[0] == 1, total.astype(F32), other_ref[...].astype(F32)).astype(BF16)


def add_choose(middle, a, b, other):
    spec = pl.BlockSpec(memory_space=pltpu.VMEM)
    return pl.pallas_call(
        add_choose_kernel,
        in_specs=[pl.BlockSpec(memory_space=pltpu.SMEM), spec, spec, spec],
        out_specs=[spec, spec],
        out_shape=[jax.ShapeDtypeStruct(a.shape, BF16)] * 2,
        compiler_params=params(8),
        cost_estimate=LITTLE,
    )(middle, a, b, other)


def backward_kernel(n_rows, width, first, scalars, own_ref, came_ref, *refs):
    extras, refs = refs[:n_rows], refs[n_rows:]
    (gate_ref, up_ref), refs = refs[:2], refs[2:]
    if not first:
        (grad_in, route_in), refs = refs[:2], refs[5:]
    hidden_ref, gate_pre_ref, up_pre_ref = refs[:3]
    per_array = own_ref.shape[1] // 3

    def load(a):
        cols = slice(a * per_array, (a + 1) * per_array)
        return jnp.where(
            scalars[0] == 1, own_ref[:, cols].astype(F32), came_ref[:, cols].astype(F32)
        )

    tail = jnp.concatenate([ref[...] for ref in extras], axis=0).astype(F32)
    weight = jnp.where(tail[:, 2:3] == scalars[1].astype(F32), tail[:, 0:1], tail[:, 1:2])
    pre_gate, pre_up, back_hidden = load(0), load(1), load(2)
    sigmoid_gate = jax.nn.sigmoid(pre_gate)
    silu_gate = pre_gate * sigmoid_gate
    hidden = silu_gate * pre_up
    route = jnp.sum(hidden * back_hidden, axis=1, keepdims=True)
    hidden_ref[...] = (weight * hidden).astype(BF16)
    gate_pre = (
        weight * back_hidden * pre_up * sigmoid_gate * (1.0 + pre_gate * (1.0 - sigmoid_gate))
    ).astype(BF16)
    up_pre = (weight * back_hidden * silu_gate).astype(BF16)
    gate_pre_ref[...] = gate_pre
    up_pre_ref[...] = up_pre
    grad = lax.dot_general(
        gate_pre, gate_ref[0], OVER_LAST, preferred_element_type=F32
    ) + lax.dot_general(up_pre, up_ref[0], OVER_LAST, preferred_element_type=F32)
    if first:
        grad_ref, route_ref = refs[3:]
        grad_ref[...] = grad
        route_ref[...] = jnp.broadcast_to(route, route_ref.shape)
        return
    backs = refs[3:]
    grad = grad + grad_in[...]
    routes = route_in[...] + jnp.broadcast_to(route, route_in.shape)
    rows = backs[0].shape[0]
    for i, ref in enumerate(backs):
        ref[:, :width] = grad[i * rows : (i + 1) * rows, :].astype(BF16)
        ref[:, width:] = routes[i * rows : (i + 1) * rows, :].astype(BF16)


def backward_piece(scalars, own, came, rows, height, w_gate, w_up, half, before):
    width, units = w_gate.shape[1:]
    total = height * len(rows)
    per_array = own.shape[1] // 3
    across = pl.BlockSpec((1, width, per_array), lambda j: (0, 0, half))
    column = pl.BlockSpec((total, per_array), lambda j: (0, half))
    extra = pl.BlockSpec((height, LANES), lambda j: (0, 2 * width // LANES))
    sums = [(total, width), (total, LANES)]
    back = (height, width + LANES)
    in_specs = [pl.BlockSpec(memory_space=pltpu.SMEM), whole(own.shape), whole(came.shape)]
    in_specs += [extra] * len(rows) + [across, across]
    operands = [scalars, own, came, *rows, w_gate, w_up]
    aliases = {}
    if half:
        in_specs += [whole(shape) for shape in sums]
        in_specs += [pl.BlockSpec(memory_space=pl.ANY)] * 3
        operands += [*before[3:], *before[:3]]
        aliases = {len(operands) - 3 + i: i for i in range(3)}
        outs = [whole(back)] * len(rows)
        shapes = [jax.ShapeDtypeStruct(back, BF16)] * len(rows)
    else:
        outs = [whole(shape) for shape in sums]
        shapes = [jax.ShapeDtypeStruct(shape, F32) for shape in sums]
    return pl.pallas_call(
        functools.partial(backward_kernel, len(rows), width, half == 0),
        grid=(1,),
        in_specs=in_specs,
        out_specs=[column] * 3 + outs,
        out_shape=[jax.ShapeDtypeStruct((total, units), BF16)] * 3 + shapes,
        input_output_aliases=aliases,
        compiler_params=params(32),
        cost_estimate=LITTLE,
    )(*operands)


def gradient_kernel(left_ref, right_ref, before_ref, out_ref):
    added = lax.dot_general(
        left_ref[...], right_ref[...], (((0,), (0,)), ((), ())), preferred_element_type=F32
    )
    out_ref[...] = (added + before_ref[...].astype(F32)).astype(BF16)


def gradient_add(left, right, before):
    rows, height = left.shape
    wide = right.shape[1]
    block = pl.BlockSpec((BLOCK, wide), lambda j: (j, 0))
    return pl.pallas_call(
        gradient_kernel,
        grid=(height // BLOCK,),
        in_specs=[pl.BlockSpec((rows, BLOCK), lambda j: (0, j)), whole(right.shape), block],
        out_specs=block,
        out_shape=jax.ShapeDtypeStruct((height, wide), BF16),
        compiler_params=params(16),
        cost_estimate=LITTLE,
    )(left, right, before)


def tie_kernel(*refs):
    refs[-1][...] = jnp.zeros(refs[-1].shape, jnp.int32)


def tie(*arrays):
    return pl.pallas_call(
        tie_kernel,
        in_specs=[pl.BlockSpec(memory_space=pl.ANY)] * len(arrays),
        out_shape=jax.ShapeDtypeStruct((8, LANES), jnp.int32),
        cost_estimate=LITTLE,
    )(*arrays)


def body(layer_input, out_grad, routes, gate_weights, w_gate, w_up, w_down):
    groups = lax.axis_size("expert")
    n_dp = lax.axis_size("dp")
    me = lax.axis_index("expert")
    place = lax.axis_index("dp")
    tokens, width = layer_input.shape
    choose = routes.shape[1]
    capacity = 2 * tokens * choose // groups
    per_chunk = max(1, groups // 4)
    offsets = list(range(groups))
    chunks = [offsets[i : i + per_chunk] for i in range(0, groups, per_chunk)]

    partner = me ^ jnp.arange(groups, dtype=jnp.int32)
    named = routes[:, :, None] == partner[None, None, :]
    chosen = jnp.any(named, axis=1)
    rank = jnp.cumsum(chosen.astype(jnp.int32), axis=0) - 1
    rank = jnp.where(chosen, rank, -1).T
    slot = jnp.arange(capacity, dtype=jnp.int32)
    pick = (rank[:, None, :] == slot[None, :, None]).astype(BF16)

    lanes = 128
    extra = jnp.concatenate([gate_weights, routes[:, :1].astype(BF16)], axis=1)
    extra = jnp.pad(extra, ((0, 0), (0, lanes - choose - 1)))
    packed = jnp.concatenate([layer_input, out_grad, extra], axis=1)

    gate_mat, up_mat, down_mat = w_gate[0], w_up[0], w_down[0]
    over_units = (((1,), (1,)), ((), ()))
    over_rows = (((0,), (0,)), ((), ()))

    middle = (place == n_dp // 2 - 1) | (place == n_dp // 2)

    last = [None]

    def gate(*values):
        if last[0] is None:
            return values
        return lax.optimization_barrier((*values, last[0]))[:-1]

    def mark(value):
        last[0] = value
        return value

    def fetch(r):
        (one,) = gate(pick[r])
        rows = jnp.dot(one, packed, preferred_element_type=F32).astype(BF16)
        mark(rows)
        if r:
            rows = lax.ppermute(rows, "expert", [(i, i ^ r) for i in range(groups)])
        return rows

    def join(rows):
        rows = gate(*rows)
        return rows[0] if len(rows) == 1 else jnp.concatenate(rows, axis=0)

    halves = 2
    part_units = w_gate.shape[2] // halves

    def forward(rows, half):
        cols = slice(half * part_units, (half + 1) * part_units)
        rows_in, rows_grad = rows[:, :width], rows[:, width : 2 * width]
        part_gate = jnp.dot(rows_in, gate_mat[:, cols], preferred_element_type=F32)
        part_up = jnp.dot(rows_in, up_mat[:, cols], preferred_element_type=F32)
        part_back = lax.dot_general(
            rows_grad, down_mat[cols], over_units, preferred_element_type=F32
        )
        return jnp.concatenate(
            [part_gate.astype(BF16), part_up.astype(BF16), part_back.astype(BF16)], axis=1
        )

    count = len(chunks)
    pieces = halves * count
    kept = {}
    held = {}
    returned = {}

    def activate(c, sums):
        tail = held[c][:, 2 * width :]
        weight = jnp.where(tail[:, 2:3] == me.astype(BF16), tail[:, 0:1], tail[:, 1:2])
        sums = [
            jnp.concatenate([s[:, a * part_units : (a + 1) * part_units] for s in sums], axis=1)
            for a in range(3)
        ]
        scaled_hidden, gate_pre, up_pre, route_part = activation_grads(sums, weight)
        kept[c] = [
            held[c][:, :width],
            held[c][:, width : 2 * width],
            scaled_hidden,
            gate_pre,
            up_pre,
            route_part,
        ]
        mark(up_pre)

    def to_input(c):
        gate_pre, up_pre = gate(*kept[c][3:5])
        slot_grad = (
            lax.dot_general(gate_pre, gate_mat, over_units, preferred_element_type=F32)
            + lax.dot_general(up_pre, up_mat, over_units, preferred_element_type=F32)
        ).astype(BF16)
        kept[c].append(mark(slot_grad))

    def give_back(c):
        route_part, slot_grad = gate(*kept[c][5:])
        back = jnp.concatenate(
            [slot_grad, jnp.broadcast_to(route_part, (route_part.shape[0], lanes))], axis=1
        )
        for i, r in enumerate(chunks[c]):
            one = back[i * capacity : (i + 1) * capacity]
            mark(one)
            if r:
                one = lax.ppermute(one, "expert", [(i, i ^ r) for i in range(groups)])
            returned[r] = one

    combined = [None]
    route_cols = {}

    gradients = {}
    counted = {}

    def add_gradient(which):
        first = counted.get(which, 0)
        counted[which] = len(kept)
        left, right = ((2, 1), (0, 3), (0, 4))[which]
        these = [kept[c] for c in range(first, counted[which])]
        rows_left = jnp.concatenate([one[left] for one in these], axis=0)
        rows_right = jnp.concatenate([one[right] for one in these], axis=0)
        (rows_left,) = gate(rows_left)
        if first:
            gradients[which] = gradient_add(rows_left, rows_right, gradients[which])
            mark(gradients[which])
            return
        added = lax.dot_general(rows_left, rows_right, over_rows, preferred_element_type=F32)
        gradients[which] = added.astype(BF16)
        if counted[which] < count:
            gradients[which] = mark(gradients[which])

    def take_back(chunk):
        came = gate(*[returned[r] for r in chunk])
        for r, one in zip(chunk, came):
            route_cols[r] = one[:, width]
        stacked = jnp.concatenate([one[:, :width] for one in came], axis=0)
        spread = jnp.concatenate([pick[r] for r in chunk], axis=0)
        added = lax.dot_general(spread, stacked, over_rows, preferred_element_type=F32)
        if combined[0] is not None:
            added = combined[0] + added
        combined[0] = mark(added)

    if n_dp != 4:
        for c in range(count):
            held[c] = join([fetch(r) for r in chunks[c]])
            activate(c, [line_sum(forward(held[c], a), "dp", n_dp, place) for a in range(halves)])
            to_input(c)
            give_back(c)
    else:
        inward, across, outward = [(0, 1), (3, 2)], [(1, 2), (2, 1)], [(1, 0), (2, 3)]
        part, partly, total, spread_out = {}, {}, {}, {}
        arrived, crossed, joined = {}, {}, {}
        scalars = jnp.stack([middle.astype(jnp.int32), me.astype(jnp.int32)])
        pairs = {}

        ready_pairs = {}

        def pick_pair(c):
            r = chunks[c][0]
            (both,) = gate(pick[r : r + 2].reshape(2 * capacity, tokens))
            ready_pairs[c] = mark(jnp.dot(both, packed, preferred_element_type=F32).astype(BF16))

        def fetch_pair(c):
            r = chunks[c][0]
            if c not in ready_pairs:
                pick_pair(c)
            (sent,) = gate(ready_pairs[c])
            pairs[c] = lax.ppermute(sent, "expert", [(i, i ^ r) for i in range(groups)])

        others = {}

        def split(c):
            (pairs[c],) = gate(pairs[c])
            others[c] = mark(pairs[c][capacity:])

        def hand_on(c):
            (other,) = gate(others[c])
            rows[c] = [
                pairs[c],
                lax.ppermute(other, "expert", [(i, i ^ 1) for i in range(groups)]),
            ]

        rows = {}
        fetch_pair(1)
        fetch_pair(2)
        from_core = fetch(1)
        rows[0] = [fetch(0), from_core]

        def compute_part(k):
            c, half = divmod(k, halves)
            if half == 0:
                held[c] = gate(*rows[c])
            (ready,) = gate(scalars)
            part[k], *wide = forward_piece(
                ready, held[c], capacity, w_gate, w_up, w_down, half, part_units
            )
            mark(part[k])
            if half == 0:
                joined[c] = wide

        begun = {}

        def finish(k):
            c, half = divmod(k, halves)
            (came,) = gate(spread_out[k])
            results = backward_piece(
                scalars, total[k], came, held[c], capacity, w_gate, w_up, half, begun.get(c)
            )
            mark(results[3])
            if half == 0:
                begun[c] = results
                return
            kept[c] = [*joined[c], *results[:3]]
            for r, one in zip(chunks[c], results[3:]):
                if r:
                    one = lax.ppermute(one, "expert", [(i, i ^ r) for i in range(groups)])
                returned[r] = one

        work = {
            1: [(fetch_pair, 3)],
            4: [(finish, 0)],
            5: [(finish, 1)],
            6: [(finish, 2)],
            7: [(finish, 3), (take_back, chunks[0])],
            8: [(finish, 4)],
            9: [(finish, 5), (add_gradient, 0), (take_back, chunks[1])],
        }
        compute_part(0)
        arrived[0] = lax.ppermute(part[0], "dp", inward)
        compute_part(1)
        arrived[1] = lax.ppermute(part[1], "dp", inward)
        pick_pair(3)
        for t in range(1, pieces + 2):
            if t <= pieces:
                (came,) = gate(arrived[t - 1])
                partly[t - 1] = mark(add_pieces(part[t - 1], came))
                crossed[t - 1] = lax.ppermute(partly[t - 1], "dp", across)
            for c in {1: (1, 2), 4: (3,)}.get(t, ()):
                split(c)
            if t in (1, 2, 4):
                hand_on({1: 1, 2: 2, 4: 3}[t])
            if t + 1 < pieces:
                compute_part(t + 1)
            if t == 1:
                arrived[2] = lax.ppermute(part[2], "dp", inward)
            else:
                k = t - 2
                (came,) = gate(crossed[k])
                if t + 1 < pieces:
                    total[k], both = add_choose(scalars, partly[k], came, part[t + 1])
                    mark(both)
                    arrived[t + 1] = lax.ppermute(both, "dp", inward + outward)
                    spread_out[k] = arrived[t + 1]
                else:
                    total[k] = mark(add_pieces(partly[k], came))
                    spread_out[k] = lax.ppermute(total[k], "dp", outward)
            for step, c in work.get(t, ()):
                step(c)
        finish(6)
        add_gradient(1)
        add_gradient(2)
        finish(7)
        take_back(chunks[2])
    for which in range(3):
        add_gradient(which)
    grad_down, grad_gate, grad_up = (gradients[which] for which in range(3))
    mark(tie(grad_down, grad_gate, grad_up))
    if len(chunks[-1]) == 2:
        take_back(chunks[-1])
    else:
        take_back([r for r in offsets if r not in route_cols])
    input_grad = combined[0].astype(BF16)
    route_cols = jnp.stack([route_cols[r] for r in range(groups)], axis=0)
    per_offset = jnp.einsum("rst,rs->tr", pick, route_cols, preferred_element_type=F32)
    route_grad = jnp.sum(jnp.where(named, per_offset[:, None, :], 0.0), axis=2).astype(BF16)
    return (
        input_grad,
        route_grad,
        grad_gate[None],
        grad_up[None],
        grad_down[None],
    )


def solution(mesh):
    placed = (
        P("expert", "dp"),
        P("expert", "dp"),
        P("expert", None),
        P("expert", None),
        P("expert", "dp", None),
        P("expert", "dp", None),
        P("expert", None, "dp"),
    )
    return jax.shard_map(
        body,
        mesh=mesh,
        in_specs=placed,
        out_specs=(
            P("expert", "dp"),
            P("expert", None),
            P("expert", "dp", None),
            P("expert", "dp", None),
            P("expert", None, "dp"),
        ),
        check_vma=False,
    )
```

profile of v0, /device:TPU:0, one launch (start us, length us, event | category | flops | bytes accessed | tf_op | source)
XLA Modules:
  0.0 197.5 jit_solution(3168058856058530565)
XLA Ops:
  4.1 3.1 %convolution_convert_fusion.2 = bf16[192,3712]{1,0:T(8,128)(2,1)} fusion(pred[192,192]{1,0:T(32,128)(4,1)S(1)} %bitcast.60, bf16[192,3]{1,0:T(8,128)(2,1)S(1)} %copy.32, bf16[192,1792]{1,0:T(8,128)(2,1)} %param.8, bf16[192,1792]{1,0:T(8,128)(2,1)} %param.7), kind=kOutput, calls=%fused_computation.2 | convolution fusion | flops 280092672 | bytes 2839680 | tf_op jit(solution)/shard_map/dot_general | solution.py:408
  7.2 1.6 convolution_convert_fusion.1
  8.8 3.0 %collective-permute-start.2 = (bf16[192,3712]{1,0:T(8,128)(2,1)}, bf16[192,3712]{1,0:T(8,128)(2,1)S(1)}, u32[]{:S(2)}, u32[]{:S(2)}) collective-permute-start(bf16[192,3712]{1,0:T(8,128)(2,1)} %convolution_convert_fusion.1), channel_id=1, source_target_pairs={{0,4},{1,5},{2,6},{3,7},{4,0},{5,1},{6,2},{7,3},{8,12},{9,13},{10,... | collective-permute-start | bytes 4276232 | tf_op jit(solution)/shard_map/ppermute | solution.py:415
  11.8 1.5 collective-permute-start.3
  14.0 1.2 convolution_convert_fusion.4
  15.3 1.8 convolution_convert_fusion.3.refs_0_
  17.8 2.0 %copy-done.1 = bf16[1,1792,1024]{2,1,0:T(8,128)(2,1)S(1)} copy-done((bf16[1,1792,1024]{2,1,0:T(8,128)(2,1)S(1)}, bf16[1,1792,1024]{2,1,0:T(8,128)(2,1)}, u32[]{:S(2)}) %copy-start.1) | copy-done | bytes 3670040
  19.8 2.0 %copy-done.3 = bf16[1,1024,1792]{2,1,0:T(8,128)(2,1)S(1)} copy-done((bf16[1,1024,1792]{2,1,0:T(8,128)(2,1)S(1)}, bf16[1,1024,1792]{2,1,0:T(8,128)(2,1)}, u32[]{:S(2)}) %copy-start.3) | copy-done | bytes 3670040
  21.9 3.1 %shard_map.110 = (bf16[192,1536]{1,0:T(8,128)(2,1)S(1)}, bf16[192,1792]{1,0:T(8,128)(2,1)S(1)}, bf16[192,1792]{1,0:T(8,128)(2,1)S(1)}) custom-call(s32[2]{0:T(128)S(1)} %pad_add_fusion.scalars.middle_ref, bf16[96,3712]{1,0:T(8,128)(2,1)S(1)} %convolution_convert_fusion.3.refs_0_, bf16[96,3712]{1,0:T(8,128)(2,1)} %collective-permute-done.refs_1_, ...), custom_call_target="tpu_custom_call" | custom-call | flops 1 | bytes 1 | tf_op jit(solution)/shard_map/pallas_call | solution.py:84
  25.9 3.6 %collective-permute-start.4 = (bf16[192,1536]{1,0:T(8,128)(2,1)S(1)}, bf16[192,1536]{1,0:T(8,128)(2,1)S(1)}, u32[]{:S(2)}, u32[]{:S(2)}) collective-permute-start(bf16[192,1536]{1,0:T(8,128)(2,1)S(1)} %get-tuple-element.140.a_ref), channel_id=1, source_target_pairs={{0,8},{24,16},{1,9},{25,17},{2,10},{26,18},{3,11},{27,19},{4,12},{... | collective-permute-start | bytes 1769480 | tf_op jit(solution)/shard_map/ppermute | solution.py:476
  29.5 3.1 %shard_map.111.a_ref = bf16[192,1536]{1,0:T(8,128)(2,1)S(1)} custom-call(s32[2]{0:T(128)S(1)} %pad_add_fusion.scalars.middle_ref, bf16[96,3712]{1,0:T(8,128)(2,1)S(1)} %convolution_convert_fusion.3.refs_0_, bf16[96,3712]{1,0:T(8,128)(2,1)} %collective-permute-done.refs_1_, bf16[1,1792,1024]{2,1,0:T(8,128)(2,1)S(1)} %copy-done, ...), custom_call_target="tpu_custom_call" | custom-call | flops 1 | bytes 1 | tf_op jit(solution)/shard_map/pallas_call | solution.py:84
  33.2 9.5 %collective-permute-done.4.b_ref = bf16[192,1536]{1,0:T(8,128)(2,1)S(1)} collective-permute-done((bf16[192,1536]{1,0:T(8,128)(2,1)S(1)}, bf16[192,1536]{1,0:T(8,128)(2,1)S(1)}, u32[]{:S(2)}, u32[]{:S(2)}) %collective-permute-start.4) | collective-permute-done | bytes 589856 | tf_op jit(solution)/shard_map/ppermute | solution.py:476
  42.8 1.9 collective-permute-done.3.refs_0_
  44.9 3.5 %collective-permute-start.1 = (bf16[192,1536]{1,0:T(8,128)(2,1)S(1)}, bf16[192,1536]{1,0:T(8,128)(2,1)S(1)}, u32[]{:S(2)}, u32[]{:S(2)}) collective-permute-start(bf16[192,1536]{1,0:T(8,128)(2,1)S(1)} %shard_map.111.a_ref), channel_id=1, source_target_pairs={{0,8},{24,16},{1,9},{25,17},{2,10},{26,18},{3,11},{27,19},{4,12},{... | collective-permute-start | bytes 1769480 | tf_op jit(solution)/shard_map/ppermute | solution.py:478
  48.5 2.5 %shard_map.113 = (bf16[192,1536]{1,0:T(8,128)(2,1)S(1)}, bf16[192,1792]{1,0:T(8,128)(2,1)S(1)}, bf16[192,1792]{1,0:T(8,128)(2,1)S(1)}) custom-call(s32[2]{0:T(128)S(1)} %pad_add_fusion.scalars.middle_ref, bf16[192,3712]{1,0:T(8,128)(2,1)S(1)} %collective-permute-done.3.refs_0_, bf16[96,3712]{1,0:T(8,128)(2,1)S(1)} %collective-permute-done.5.refs_1_, ...), custom_call_target="tpu_custom_call" | custom-call | flops 1 | bytes 1 | tf_op jit(solution)/shard_map/pallas_call | solution.py:84
  51.8 1.4 collective-permute-start.14
  54.0 4.9 %collective-permute-start.7 = (bf16[192,1536]{1,0:T(8,128)(2,1)S(1)}, bf16[192,1536]{1,0:T(8,128)(2,1)S(1)}, u32[]{:S(2)}, u32[]{:S(2)}) collective-permute-start(bf16[192,1536]{1,0:T(8,128)(2,1)S(1)} %get-tuple-element.152.a_ref), channel_id=1, source_target_pairs={{0,8},{24,16},{1,9},{25,17},{2,10},{26,18},{3,11},{27,19},{4,12},{... | collective-permute-start | bytes 1769480 | tf_op jit(solution)/shard_map/ppermute | solution.py:492
  58.9 3.2 %collective-permute-done.1.b_ref = bf16[192,1536]{1,0:T(8,128)(2,1)S(1)} collective-permute-done((bf16[192,1536]{1,0:T(8,128)(2,1)S(1)}, bf16[192,1536]{1,0:T(8,128)(2,1)S(1)}, u32[]{:S(2)}, u32[]{:S(2)}) %collective-permute-start.1) | collective-permute-done | bytes 589856 | tf_op jit(solution)/shard_map/ppermute | solution.py:478
  63.0 2.5 %shard_map.115.other_ref.a_ref = bf16[192,1536]{1,0:T(8,128)(2,1)S(1)} custom-call(s32[2]{0:T(128)S(1)} %pad_add_fusion.scalars.middle_ref, bf16[192,3712]{1,0:T(8,128)(2,1)S(1)} %collective-permute-done.3.refs_0_, bf16[96,3712]{1,0:T(8,128)(2,1)S(1)} %collective-permute-done.5.refs_1_, bf16[1,1792,1024]{2,1,0:T(8,128)(2,1)S(1)} %copy-done, ...), custom_call_target="tpu_custom_call" | custom-call | flops 1 | bytes 1 | tf_op jit(solution)/shard_map/pallas_call | solution.py:84
  66.3 5.6 %collective-permute-start.11 = (bf16[192,1536]{1,0:T(8,128)(2,1)S(1)}, bf16[192,1536]{1,0:T(8,128)(2,1)S(1)}, u32[]{:S(2)}, u32[]{:S(2)}) collective-permute-start(bf16[192,1536]{1,0:T(8,128)(2,1)S(1)} %get-tuple-element.156), channel_id=1, source_target_pairs={{0,8},{24,16},{8,0},{16,24},{1,9},{25,17},{9,1},{17,25},{2,10},{26... | collective-permute-start | bytes 1769480 | tf_op jit(solution)/shard_map/ppermute | solution.py:499
  71.9 2.8 %collective-permute-done.7.b_ref = bf16[192,1536]{1,0:T(8,128)(2,1)S(1)} collective-permute-done((bf16[192,1536]{1,0:T(8,128)(2,1)S(1)}, bf16[192,1536]{1,0:T(8,128)(2,1)S(1)}, u32[]{:S(2)}, u32[]{:S(2)}) %collective-permute-start.7) | collective-permute-done | bytes 589856 | tf_op jit(solution)/shard_map/ppermute | solution.py:492
  75.5 2.5 %shard_map.118 = (bf16[192,1536]{1,0:T(8,128)(2,1)S(1)}, bf16[192,1792]{1,0:T(8,128)(2,1)S(1)}, bf16[192,1792]{1,0:T(8,128)(2,1)S(1)}) custom-call(s32[2]{0:T(128)S(1)} %pad_add_fusion.scalars.middle_ref, bf16[192,3712]{1,0:T(8,128)(2,1)S(1)} %collective-permute-done.2.refs_0_, bf16[96,3712]{1,0:T(8,128)(2,1)S(1)} %collective-permute-done.9.refs_1_, ...), custom_call_target="tpu_custom_call" | custom-call | flops 1 | bytes 1 | tf_op jit(solution)/shard_map/pallas_call | solution.py:84
  78.9 5.7 %collective-permute-start.10 = (bf16[192,1536]{1,0:T(8,128)(2,1)S(1)}, bf16[192,1536]{1,0:T(8,128)(2,1)S(1)}, u32[]{:S(2)}, u32[]{:S(2)}) collective-permute-start(bf16[192,1536]{1,0:T(8,128)(2,1)S(1)} %get-tuple-element.165), channel_id=1, source_target_pairs={{0,8},{24,16},{8,0},{16,24},{1,9},{25,17},{9,1},{17,25},{2,10},{26... | collective-permute-start | bytes 1769480 | tf_op jit(solution)/shard_map/ppermute | solution.py:499
  84.6 2.7 %collective-permute-done.11.b_ref.came_ref = bf16[192,1536]{1,0:T(8,128)(2,1)S(1)} collective-permute-done((bf16[192,1536]{1,0:T(8,128)(2,1)S(1)}, bf16[192,1536]{1,0:T(8,128)(2,1)S(1)}, u32[]{:S(2)}, u32[]{:S(2)}) %collective-permute-start.11) | collective-permute-done | bytes 589856 | tf_op jit(solution)/shard_map/ppermute | solution.py:499
  88.5 2.5 %shard_map.121.other_ref.a_ref = bf16[192,1536]{1,0:T(8,128)(2,1)S(1)} custom-call(s32[2]{0:T(128)S(1)} %pad_add_fusion.scalars.middle_ref, bf16[192,3712]{1,0:T(8,128)(2,1)S(1)} %collective-permute-done.2.refs_0_, bf16[96,3712]{1,0:T(8,128)(2,1)S(1)} %collective-permute-done.9.refs_1_, bf16[1,1792,1024]{2,1,0:T(8,128)(2,1)S(1)} %copy-done, ...), custom_call_target="tpu_custom_call" | custom-call | flops 1 | bytes 1 | tf_op jit(solution)/shard_map/pallas_call | solution.py:84
  91.0 1.6 shard_map.122
  92.6 5.3 %collective-permute-start.18 = (bf16[192,1536]{1,0:T(8,128)(2,1)}, bf16[192,1536]{1,0:T(8,128)(2,1)S(1)}, u32[]{:S(2)}, u32[]{:S(2)}) collective-permute-start(bf16[192,1536]{1,0:T(8,128)(2,1)} %get-tuple-element.172), channel_id=1, source_target_pairs={{0,8},{24,16},{8,0},{16,24},{1,9},{25,17},{9,1},{17,25},{2,10},{26... | collective-permute-start | bytes 1769480 | tf_op jit(solution)/shard_map/ppermute | solution.py:499
  97.9 2.5 %shard_map.123 = (bf16[192,1024]{1,0:T(8,128)(2,1)S(1)}, bf16[192,1024]{1,0:T(8,128)(2,1)S(1)}, bf16[192,1024]{1,0:T(8,128)(2,1)S(1)}, f32[192,1792]{1,0:T(8,128)S(1)}, f32[192,128]{1,0:T(8,128)S(1)}) custom-call(s32[2]{0:T(128)S(1)} %pad_add_fusion.scalars.middle_ref, bf16[192,1536]{1,0:T(8,128)(2,1)S(1)} %get-tuple-element.167.own_ref, ...), custom_call_target="tpu_custom_call" | custom-call | flops 1 | bytes 1 | tf_op jit(solution)/shard_map/pallas_call | solution.py:196
  101.2 2.5 %shard_map.125 = (bf16[192,1536]{1,0:T(8,128)(2,1)S(1)}, bf16[192,1792]{1,0:T(8,128)(2,1)S(1)}, bf16[192,1792]{1,0:T(8,128)(2,1)S(1)}) custom-call(s32[2]{0:T(128)S(1)} %pad_add_fusion.scalars.middle_ref, bf16[192,3712]{1,0:T(8,128)(2,1)S(1)} %collective-permute-done.14.refs_0_, bf16[96,3712]{1,0:T(8,128)(2,1)S(1)} %collective-permute-done.15.refs_1_, ...), custom_call_target="tpu_custom_call" | custom-call | flops 1 | bytes 1 | tf_op jit(solution)/shard_map/pallas_call | solution.py:84
  104.6 1.1 copy-done.6
  105.7 1.6 shard_map.126
  107.3 5.1 %collective-permute-start.17 = (bf16[192,1536]{1,0:T(8,128)(2,1)}, bf16[192,1536]{1,0:T(8,128)(2,1)S(1)}, u32[]{:S(2)}, u32[]{:S(2)}) collective-permute-start(bf16[192,1536]{1,0:T(8,128)(2,1)} %get-tuple-element.182), channel_id=1, source_target_pairs={{0,8},{24,16},{8,0},{16,24},{1,9},{25,17},{9,1},{17,25},{2,10},{26... | collective-permute-start | bytes 1769480 | tf_op jit(solution)/shard_map/ppermute | solution.py:499
  112.4 1.0 copy-done.8
  113.4 1.0 copy-done.12
  114.3 3.1 %shard_map.127 = (bf16[192,1024]{1,0:T(8,128)(2,1)S(1)}, bf16[192,1024]{1,0:T(8,128)(2,1)S(1)}, bf16[192,1024]{1,0:T(8,128)(2,1)S(1)}, bf16[96,1920]{1,0:T(8,128)(2,1)S(1)}, bf16[96,1920]{1,0:T(8,128)(2,1)}) custom-call(s32[2]{0:T(128)S(1)} %pad_add_fusion.scalars.middle_ref, ...), custom_call_target="tpu_custom_call", output_to_operand_aliasing={{0}: (9, {}), {1}: (10, {}), {2}: (11, {})} | custom-call | flops 1 | bytes 1 | tf_op jit(solution)/shard_map/pallas_call | solution.py:196
  119.0 2.5 %shard_map.129.other_ref.a_ref = bf16[192,1536]{1,0:T(8,128)(2,1)S(1)} custom-call(s32[2]{0:T(128)S(1)} %pad_add_fusion.scalars.middle_ref, bf16[192,3712]{1,0:T(8,128)(2,1)S(1)} %collective-permute-done.14.refs_0_, bf16[96,3712]{1,0:T(8,128)(2,1)S(1)} %collective-permute-done.15.refs_1_, bf16[1,1792,1024]{2,1,0:T(8,128)(2,1)S(1)} %copy-done, ...), custom_call_target="tpu_custom_call" | custom-call | flops 1 | bytes 1 | tf_op jit(solution)/shard_map/pallas_call | solution.py:84
  122.4 2.9 %collective-permute-start.24 = (bf16[192,1536]{1,0:T(8,128)(2,1)S(1)}, bf16[192,1536]{1,0:T(8,128)(2,1)S(1)}, u32[]{:S(2)}, u32[]{:S(2)}) collective-permute-start(bf16[192,1536]{1,0:T(8,128)(2,1)S(1)} %get-tuple-element.195), channel_id=1, source_target_pairs={{0,8},{24,16},{8,0},{16,24},{1,9},{25,17},{9,1},{17,25},{2,10},{26... | collective-permute-start | bytes 1769480 | tf_op jit(solution)/shard_map/ppermute | solution.py:499
  125.3 2.1 %shard_map.131 = (bf16[192,1024]{1,0:T(8,128)(2,1)S(1)}, bf16[192,1024]{1,0:T(8,128)(2,1)S(1)}, bf16[192,1024]{1,0:T(8,128)(2,1)S(1)}, f32[192,1792]{1,0:T(8,128)S(1)}, f32[192,128]{1,0:T(8,128)S(1)}) custom-call(s32[2]{0:T(128)S(1)} %pad_add_fusion.scalars.middle_ref, bf16[192,1536]{1,0:T(8,128)(2,1)S(1)} %get-tuple-element.192.own_ref, ...), custom_call_target="tpu_custom_call" | custom-call | flops 1 | bytes 1 | tf_op jit(solution)/shard_map/pallas_call | solution.py:196
  128.4 1.3 collective-permute-start.23
  129.7 2.1 %shard_map.134 = (bf16[192,1024]{1,0:T(8,128)(2,1)S(1)}, bf16[192,1024]{1,0:T(8,128)(2,1)S(1)}, bf16[192,1024]{1,0:T(8,128)(2,1)S(1)}, bf16[96,1920]{1,0:T(8,128)(2,1)S(1)}, bf16[96,1920]{1,0:T(8,128)(2,1)S(1)}) custom-call(s32[2]{0:T(128)S(1)} %pad_add_fusion.scalars.middle_ref, ...), custom_call_target="tpu_custom_call", output_to_operand_aliasing={{0}: (9, {}), {1}: (10, {}), {2}: (11, {})} | custom-call | flops 1 | bytes 1 | tf_op jit(solution)/shard_map/pallas_call | solution.py:196
  132.0 1.5 fusion.18
  133.4 6.0 %collective-permute-done.24.b_ref.came_ref = bf16[192,1536]{1,0:T(8,128)(2,1)S(1)} collective-permute-done((bf16[192,1536]{1,0:T(8,128)(2,1)S(1)}, bf16[192,1536]{1,0:T(8,128)(2,1)S(1)}, u32[]{:S(2)}, u32[]{:S(2)}) %collective-permute-start.24) | collective-permute-done | bytes 589856 | tf_op jit(solution)/shard_map/ppermute | solution.py:499
  141.5 1.5 collective-permute-start.30
  143.0 2.1 %shard_map.137 = (bf16[192,1024]{1,0:T(8,128)(2,1)S(1)}, bf16[192,1024]{1,0:T(8,128)(2,1)S(1)}, bf16[192,1024]{1,0:T(8,128)(2,1)S(1)}, f32[192,1792]{1,0:T(8,128)S(1)}, f32[192,128]{1,0:T(8,128)S(1)}) custom-call(s32[2]{0:T(128)S(1)} %pad_add_fusion.scalars.middle_ref, bf16[192,1536]{1,0:T(8,128)(2,1)S(1)} %get-tuple-element.212.own_ref, ...), custom_call_target="tpu_custom_call" | custom-call | flops 1 | bytes 1 | tf_op jit(solution)/shard_map/pallas_call | solution.py:196
  145.3 1.3 collective-permute-start.29
  146.6 3.9 %collective-permute-done.23.came_ref = bf16[192,1536]{1,0:T(8,128)(2,1)S(1)} collective-permute-done((bf16[192,1536]{1,0:T(8,128)(2,1)S(1)}, bf16[192,1536]{1,0:T(8,128)(2,1)S(1)}, u32[]{:S(2)}, u32[]{:S(2)}) %collective-permute-start.23) | collective-permute-done | bytes 589856 | tf_op jit(solution)/shard_map/ppermute | solution.py:503
  150.5 2.1 %shard_map.139 = (bf16[192,1024]{1,0:T(8,128)(2,1)S(1)}, bf16[192,1024]{1,0:T(8,128)(2,1)S(1)}, bf16[192,1024]{1,0:T(8,128)(2,1)S(1)}, bf16[96,1920]{1,0:T(8,128)(2,1)S(1)}, bf16[96,1920]{1,0:T(8,128)(2,1)S(1)}) custom-call(s32[2]{0:T(128)S(1)} %pad_add_fusion.scalars.middle_ref, ...), custom_call_target="tpu_custom_call", output_to_operand_aliasing={{0}: (9, {}), {1}: (10, {}), {2}: (11, {})} | custom-call | flops 1 | bytes 1 | tf_op jit(solution)/shard_map/pallas_call | solution.py:196
  152.7 1.6 collective-permute-start.27
  154.4 3.3 %convolution_convert_fusion.7.before_ref = bf16[1024,1792]{1,0:T(8,128)(2,1)S(1)} fusion(bf16[576,1024]{1,0:T(8,128)(2,1)S(1)} %pad_maximum_fusion, bf16[192,1792]{1,0:T(8,128)(2,1)S(1)} %copy-done.24, bf16[192,1792]{1,0:T(8,128)(2,1)S(1)} %copy-done.22, bf16[192,1792]{1,0:T(8,128)(2,1)S(1)} %copy-done.20), kind=kOutput, calls=%fused_computation.7 | convolution fusion | flops 2121957376 | bytes 6914048 | tf_op jit(solution)/shard_map/dot_general | solution.py:374
  158.0 1.0 copy-done.26
  159.5 5.0 %collective-permute-done.30.came_ref = bf16[192,1536]{1,0:T(8,128)(2,1)S(1)} collective-permute-done((bf16[192,1536]{1,0:T(8,128)(2,1)S(1)}, bf16[192,1536]{1,0:T(8,128)(2,1)S(1)}, u32[]{:S(2)}, u32[]{:S(2)}) %collective-permute-start.30) | collective-permute-done | bytes 589856 | tf_op jit(solution)/shard_map/ppermute | solution.py:503
  164.5 2.1 %shard_map.140 = (bf16[192,1024]{1,0:T(8,128)(2,1)S(1)}, bf16[192,1024]{1,0:T(8,128)(2,1)S(1)}, bf16[192,1024]{1,0:T(8,128)(2,1)S(1)}, f32[192,1792]{1,0:T(8,128)S(1)}, f32[192,128]{1,0:T(8,128)S(1)}) custom-call(s32[2]{0:T(128)S(1)} %pad_add_fusion.scalars.middle_ref, bf16[192,1536]{1,0:T(8,128)(2,1)S(1)} %shard_map.136.own_ref, ...), custom_call_target="tpu_custom_call" | custom-call | flops 1 | bytes 1 | tf_op jit(solution)/shard_map/pallas_call | solution.py:196
  166.6 3.3 %convolution_convert_fusion.6.before_ref = bf16[1792,1024]{1,0:T(8,128)(2,1)S(1)} fusion(bf16[576,1792]{1,0:T(8,128)(2,1)S(1)} %copy-done.28, bf16[192,1024]{1,0:T(8,128)(2,1)S(1)} %get-tuple-element.239, bf16[192,1024]{1,0:T(8,128)(2,1)S(1)} %copy-done.16, bf16[192,1024]{1,0:T(8,128)(2,1)S(1)} %copy-done.10), kind=kOutput, calls=%fused_computation.6 | convolution fusion | flops 2119303168 | bytes 6914048 | tf_op jit(solution)/shard_map/dot_general | solution.py:374
  170.0 3.3 %convolution_convert_fusion.5.before_ref = bf16[1792,1024]{1,0:T(8,128)(2,1)S(1)} fusion(bf16[576,1792]{1,0:T(8,128)(2,1)S(1)} %copy-done.29, bf16[192,1024]{1,0:T(8,128)(2,1)S(1)} %get-tuple-element.243, bf16[192,1024]{1,0:T(8,128)(2,1)S(1)} %copy-done.18, bf16[192,1024]{1,0:T(8,128)(2,1)S(1)} %copy-done.14), kind=kOutput, calls=%fused_computation.5 | convolution fusion | flops 2119303168 | bytes 6914048 | tf_op jit(solution)/shard_map/dot_general | solution.py:374
  173.3 2.3 %collective-permute-done.29.came_ref = bf16[192,1536]{1,0:T(8,128)(2,1)S(1)} collective-permute-done((bf16[192,1536]{1,0:T(8,128)(2,1)S(1)}, bf16[192,1536]{1,0:T(8,128)(2,1)S(1)}, u32[]{:S(2)}, u32[]{:S(2)}) %collective-permute-start.29) | collective-permute-done | bytes 589856 | tf_op jit(solution)/shard_map/ppermute | solution.py:503
  175.6 2.1 %shard_map.141 = (bf16[192,1024]{1,0:T(8,128)(2,1)S(1)}, bf16[192,1024]{1,0:T(8,128)(2,1)S(1)}, bf16[192,1024]{1,0:T(8,128)(2,1)S(1)}, bf16[96,1920]{1,0:T(8,128)(2,1)S(1)}, bf16[96,1920]{1,0:T(8,128)(2,1)S(1)}) custom-call(s32[2]{0:T(128)S(1)} %pad_add_fusion.scalars.middle_ref, ...), custom_call_target="tpu_custom_call", output_to_operand_aliasing={{0}: (9, {}), {1}: (10, {}), {2}: (11, {})} | custom-call | flops 1 | bytes 1 | tf_op jit(solution)/shard_map/pallas_call | solution.py:196
  177.7 1.5 collective-permute-start.31
  179.2 1.0 slice.125
  180.4 1.5 convolution_add_fusion.1
  181.9 3.3 %shard_map.142 = bf16[1024,1792]{1,0:T(8,128)(2,1)} custom-call(bf16[192,1024]{1,0:T(8,128)(2,1)S(1)} %get-tuple-element.257.left_ref, bf16[192,1792]{1,0:T(8,128)(2,1)S(1)} %get-tuple-element.258.right_ref, bf16[1024,1792]{1,0:T(8,128)(2,1)S(1)} %convolution_convert_fusion.7.before_ref), custom_call_target="tpu_custom_call" | custom-call | flops 1 | bytes 1 | tf_op jit(solution)/shard_map/pallas_call | solution.py:219
  185.1 4.5 %shard_map.143 = bf16[1792,1024]{1,0:T(8,128)(2,1)} custom-call(bf16[192,1792]{1,0:T(8,128)(2,1)S(1)} %get-tuple-element.261.left_ref, bf16[192,1024]{1,0:T(8,128)(2,1)S(1)} %get-tuple-element.260.right_ref, bf16[1792,1024]{1,0:T(8,128)(2,1)S(1)} %convolution_convert_fusion.6.before_ref), custom_call_target="tpu_custom_call" | custom-call | flops 1 | bytes 1 | tf_op jit(solution)/shard_map/pallas_call | solution.py:219
  189.7 4.5 %shard_map.144 = bf16[1792,1024]{1,0:T(8,128)(2,1)} custom-call(bf16[192,1792]{1,0:T(8,128)(2,1)S(1)} %get-tuple-element.261.left_ref, bf16[192,1024]{1,0:T(8,128)(2,1)S(1)} %get-tuple-element.262.right_ref, bf16[1792,1024]{1,0:T(8,128)(2,1)S(1)} %convolution_convert_fusion.5.before_ref), custom_call_target="tpu_custom_call" | custom-call | flops 1 | bytes 1 | tf_op jit(solution)/shard_map/pallas_call | solution.py:219
  194.2 1.0 slice_reduce_fusion.2
  196.3 1.2 fusion.1
  (179 shorter events, 21.9 us)
Async XLA Ops:
  4.1 3.1 %copy-start.41 = (bf16[192,1792]{1,0:T(8,128)(2,1)S(1)}, bf16[192,1792]{1,0:T(8,128)(2,1)}, u32[]{:S(2)}) copy-start(bf16[192,1792]{1,0:T(8,128)(2,1)} %param.8) | copy-start | bytes 2064388
  4.1 3.1 %copy-start.43 = (bf16[192,1792]{1,0:T(8,128)(2,1)S(1)}, bf16[192,1792]{1,0:T(8,128)(2,1)}, u32[]{:S(2)}) copy-start(bf16[192,1792]{1,0:T(8,128)(2,1)} %param.7) | copy-start | bytes 2064388
  8.8 35.9 %collective-permute-start.2 = (bf16[192,3712]{1,0:T(8,128)(2,1)}, bf16[192,3712]{1,0:T(8,128)(2,1)S(1)}, u32[]{:S(2)}, u32[]{:S(2)}) collective-permute-start(bf16[192,3712]{1,0:T(8,128)(2,1)} %convolution_convert_fusion.1), channel_id=1, source_target_pairs={{0,4},{1,5},{2,6},{3,7},{4,0},{5,1},{6,2},{7,3},{8,12},{9,13},{10,... | collective-permute-start | bytes 4276232 | tf_op jit(solution)/shard_map/ppermute | solution.py:415
  11.8 32.9 %collective-permute-start.3 = (bf16[192,3712]{1,0:T(8,128)(2,1)}, bf16[192,3712]{1,0:T(8,128)(2,1)S(1)}, u32[]{:S(2)}, u32[]{:S(2)}) collective-permute-start(bf16[192,3712]{1,0:T(8,128)(2,1)} %convolution_convert_fusion.2), channel_id=1, source_target_pairs={{0,2},{1,3},{2,0},{3,1},{4,6},{5,7},{6,4},{7,5},{8,10},{9,11},{10,... | collective-permute-start | bytes 4276232 | tf_op jit(solution)/shard_map/ppermute | solution.py:415
  15.3 2.5 %collective-permute-start = (bf16[96,3712]{1,0:T(8,128)(2,1)}, bf16[96,3712]{1,0:T(8,128)(2,1)}, u32[]{:S(2)}, u32[]{:S(2)}) collective-permute-start(bf16[96,3712]{1,0:T(8,128)(2,1)} %convolution_convert_fusion.4), channel_id=1, source_target_pairs={{0,1},{1,0},{2,3},{3,2},{4,5},{5,4},{6,7},{7,6},{8,9},{9,8},{10,11... | collective-permute-start | bytes 2138120 | tf_op jit(solution)/shard_map/ppermute | solution.py:290
  15.3 2.5 %copy-start = (bf16[1,1792,1024]{2,1,0:T(8,128)(2,1)S(1)}, bf16[1,1792,1024]{2,1,0:T(8,128)(2,1)}, u32[]{:S(2)}) copy-start(bf16[1,1792,1024]{2,1,0:T(8,128)(2,1)} %refs_2_.31) | copy-start | bytes 11010052
  17.8 2.0 %copy-start.1 = (bf16[1,1792,1024]{2,1,0:T(8,128)(2,1)S(1)}, bf16[1,1792,1024]{2,1,0:T(8,128)(2,1)}, u32[]{:S(2)}) copy-start(bf16[1,1792,1024]{2,1,0:T(8,128)(2,1)} %refs_3_.31) | copy-start | bytes 11010052
  25.9 6.8 %copy-start.42 = (bf16[192,1792]{1,0:T(8,128)(2,1)S(1)}, bf16[192,1792]{1,0:T(8,128)(2,1)}, u32[]{:S(2)}) copy-start(bf16[192,1792]{1,0:T(8,128)(2,1)} %param.8) | copy-start | bytes 2064388
  25.9 6.8 %copy-start.44 = (bf16[192,1792]{1,0:T(8,128)(2,1)S(1)}, bf16[192,1792]{1,0:T(8,128)(2,1)}, u32[]{:S(2)}) copy-start(bf16[192,1792]{1,0:T(8,128)(2,1)} %param.7) | copy-start | bytes 2064388
  25.9 16.8 %collective-permute-start.4 = (bf16[192,1536]{1,0:T(8,128)(2,1)S(1)}, bf16[192,1536]{1,0:T(8,128)(2,1)S(1)}, u32[]{:S(2)}, u32[]{:S(2)}) collective-permute-start(bf16[192,1536]{1,0:T(8,128)(2,1)S(1)} %get-tuple-element.140.a_ref), channel_id=1, source_target_pairs={{0,8},{24,16},{1,9},{25,17},{2,10},{26,18},{3,11},{27,19},{4,12},{... | collective-permute-start | bytes 1769480 | tf_op jit(solution)/shard_map/ppermute | solution.py:476
  33.2 15.3 %copy-start.2 = (bf16[1,1792,1024]{2,1,0:T(8,128)(2,1)S(1)}, bf16[1,1792,1024]{2,1,0:T(8,128)(2,1)}, u32[]{:S(2)}) copy-start(bf16[1,1792,1024]{2,1,0:T(8,128)(2,1)} %refs_3_.31) | copy-start | bytes 11010052
  44.8 3.6 %collective-permute-start.5 = (bf16[96,3712]{1,0:T(8,128)(2,1)S(1)}, bf16[96,3712]{1,0:T(8,128)(2,1)S(1)}, u32[]{:S(2)}, u32[]{:S(2)}) collective-permute-start(bf16[96,3712]{1,0:T(8,128)(2,1)S(1)} %slice.114), channel_id=1, source_target_pairs={{0,1},{1,0},{2,3},{3,2},{4,5},{5,4},{6,7},{7,6},{8,9},{9,8},{10,11... | collective-permute-start | bytes 2138120 | tf_op jit(solution)/shard_map/ppermute | solution.py:427
  44.9 17.1 %collective-permute-start.1 = (bf16[192,1536]{1,0:T(8,128)(2,1)S(1)}, bf16[192,1536]{1,0:T(8,128)(2,1)S(1)}, u32[]{:S(2)}, u32[]{:S(2)}) collective-permute-start(bf16[192,1536]{1,0:T(8,128)(2,1)S(1)} %shard_map.111.a_ref), channel_id=1, source_target_pairs={{0,8},{24,16},{1,9},{25,17},{2,10},{26,18},{3,11},{27,19},{4,12},{... | collective-permute-start | bytes 1769480 | tf_op jit(solution)/shard_map/ppermute | solution.py:478
  51.8 35.6 %collective-permute-start.14 = (bf16[192,3712]{1,0:T(8,128)(2,1)S(1)}, bf16[192,3712]{1,0:T(8,128)(2,1)S(1)}, u32[]{:S(2)}, u32[]{:S(2)}) collective-permute-start(bf16[192,3712]{1,0:T(8,128)(2,1)S(1)} %convolution_convert_fusion), channel_id=1, source_target_pairs={{0,6},{1,7},{2,4},{3,5},{4,2},{5,3},{6,0},{7,1},{8,14},{9,15},{10,... | collective-permute-start | bytes 4276232 | tf_op jit(solution)/shard_map/ppermute | solution.py:415
  53.3 12.2 %collective-permute-start.8 = (bf16[192,1536]{1,0:T(8,128)(2,1)S(1)}, bf16[192,1536]{1,0:T(8,128)(2,1)S(1)}, u32[]{:S(2)}, u32[]{:S(2)}) collective-permute-start(bf16[192,1536]{1,0:T(8,128)(2,1)S(1)} %shard_map.112.a_ref), channel_id=1, source_target_pairs={{8,16},{16,8},{9,17},{17,9},{10,18},{18,10},{11,19},{19,11},{12,20... | collective-permute-start | bytes 1769480 | tf_op jit(solution)/shard_map/ppermute | solution.py:484
  54.0 20.7 %collective-permute-start.7 = (bf16[192,1536]{1,0:T(8,128)(2,1)S(1)}, bf16[192,1536]{1,0:T(8,128)(2,1)S(1)}, u32[]{:S(2)}, u32[]{:S(2)}) collective-permute-start(bf16[192,1536]{1,0:T(8,128)(2,1)S(1)} %get-tuple-element.152.a_ref), channel_id=1, source_target_pairs={{0,8},{24,16},{1,9},{25,17},{2,10},{26,18},{3,11},{27,19},{4,12},{... | collective-permute-start | bytes 1769480 | tf_op jit(solution)/shard_map/ppermute | solution.py:492
  62.2 13.3 %collective-permute-start.9 = (bf16[96,3712]{1,0:T(8,128)(2,1)S(1)}, bf16[96,3712]{1,0:T(8,128)(2,1)S(1)}, u32[]{:S(2)}, u32[]{:S(2)}) collective-permute-start(bf16[96,3712]{1,0:T(8,128)(2,1)S(1)} %slice.115), channel_id=1, source_target_pairs={{0,1},{1,0},{2,3},{3,2},{4,5},{5,4},{6,7},{7,6},{8,9},{9,8},{10,11... | collective-permute-start | bytes 2138120 | tf_op jit(solution)/shard_map/ppermute | solution.py:427
  62.2 15.8 %collective-permute-start.6 = (bf16[192,1536]{1,0:T(8,128)(2,1)S(1)}, bf16[192,1536]{1,0:T(8,128)(2,1)S(1)}, u32[]{:S(2)}, u32[]{:S(2)}) collective-permute-start(bf16[192,1536]{1,0:T(8,128)(2,1)S(1)} %shard_map.114.a_ref), channel_id=1, source_target_pairs={{8,16},{16,8},{9,17},{17,9},{10,18},{18,10},{11,19},{19,11},{12,20... | collective-permute-start | bytes 1769480 | tf_op jit(solution)/shard_map/ppermute | solution.py:484
  66.3 21.0 %collective-permute-start.11 = (bf16[192,1536]{1,0:T(8,128)(2,1)S(1)}, bf16[192,1536]{1,0:T(8,128)(2,1)S(1)}, u32[]{:S(2)}, u32[]{:S(2)}) collective-permute-start(bf16[192,1536]{1,0:T(8,128)(2,1)S(1)} %get-tuple-element.156), channel_id=1, source_target_pairs={{0,8},{24,16},{8,0},{16,24},{1,9},{25,17},{9,1},{17,25},{2,10},{26... | collective-permute-start | bytes 1769480 | tf_op jit(solution)/shard_map/ppermute | solution.py:499
  74.8 16.2 %collective-permute-start.13 = (bf16[192,1536]{1,0:T(8,128)(2,1)S(1)}, bf16[192,1536]{1,0:T(8,128)(2,1)S(1)}, u32[]{:S(2)}, u32[]{:S(2)}) collective-permute-start(bf16[192,1536]{1,0:T(8,128)(2,1)S(1)} %shard_map.117.a_ref), channel_id=1, source_target_pairs={{8,16},{16,8},{9,17},{17,9},{10,18},{18,10},{11,19},{19,11},{12,20... | collective-permute-start | bytes 1769480 | tf_op jit(solution)/shard_map/ppermute | solution.py:484
  78.1 9.4 %copy-start.23 = (bf16[192,1792]{1,0:T(8,128)(2,1)}, bf16[192,1792]{1,0:T(8,128)(2,1)S(1)}, u32[]{:S(2)}) copy-start(bf16[192,1792]{1,0:T(8,128)(2,1)S(1)} %get-tuple-element.227) | copy-start | bytes 2064388
  78.9 21.5 %collective-permute-start.10 = (bf16[192,1536]{1,0:T(8,128)(2,1)S(1)}, bf16[192,1536]{1,0:T(8,128)(2,1)S(1)}, u32[]{:S(2)}, u32[]{:S(2)}) collective-permute-start(bf16[192,1536]{1,0:T(8,128)(2,1)S(1)} %get-tuple-element.165), channel_id=1, source_target_pairs={{0,8},{24,16},{8,0},{16,24},{1,9},{25,17},{9,1},{17,25},{2,10},{26... | collective-permute-start | bytes 1769480 | tf_op jit(solution)/shard_map/ppermute | solution.py:499
  87.5 13.7 %collective-permute-start.15 = (bf16[96,3712]{1,0:T(8,128)(2,1)S(1)}, bf16[96,3712]{1,0:T(8,128)(2,1)S(1)}, u32[]{:S(2)}, u32[]{:S(2)}) collective-permute-start(bf16[96,3712]{1,0:T(8,128)(2,1)S(1)} %slice.116), channel_id=1, source_target_pairs={{0,1},{1,0},{2,3},{3,2},{4,5},{5,4},{6,7},{7,6},{8,9},{9,8},{10,11... | collective-permute-start | bytes 2138120 | tf_op jit(solution)/shard_map/ppermute | solution.py:427
  87.6 16.2 %collective-permute-start.12 = (bf16[192,1536]{1,0:T(8,128)(2,1)S(1)}, bf16[192,1536]{1,0:T(8,128)(2,1)S(1)}, u32[]{:S(2)}, u32[]{:S(2)}) collective-permute-start(bf16[192,1536]{1,0:T(8,128)(2,1)S(1)} %shard_map.120.a_ref), channel_id=1, source_target_pairs={{8,16},{16,8},{9,17},{17,9},{10,18},{18,10},{11,19},{19,11},{12,20... | collective-permute-start | bytes 1769480 | tf_op jit(solution)/shard_map/ppermute | solution.py:484
  92.6 25.6 %collective-permute-start.18 = (bf16[192,1536]{1,0:T(8,128)(2,1)}, bf16[192,1536]{1,0:T(8,128)(2,1)S(1)}, u32[]{:S(2)}, u32[]{:S(2)}) collective-permute-start(bf16[192,1536]{1,0:T(8,128)(2,1)} %get-tuple-element.172), channel_id=1, source_target_pairs={{0,8},{24,16},{8,0},{16,24},{1,9},{25,17},{9,1},{17,25},{2,10},{26... | collective-permute-start | bytes 1769480 | tf_op jit(solution)/shard_map/ppermute | solution.py:499
  97.9 3.4 %copy-start.4 = (bf16[1,1024,1792]{2,1,0:T(8,128)(2,1)S(1)}, bf16[1,1024,1792]{2,1,0:T(8,128)(2,1)}, u32[]{:S(2)}) copy-start(bf16[1,1024,1792]{2,1,0:T(8,128)(2,1)} %refs_4_.15) | copy-start | bytes 11010052
  100.3 3.4 %copy-start.7 = (bf16[192,1024]{1,0:T(8,128)(2,1)}, bf16[192,1024]{1,0:T(8,128)(2,1)S(1)}, u32[]{:S(2)}) copy-start(bf16[192,1024]{1,0:T(8,128)(2,1)S(1)} %get-tuple-element.186.refs_7_) | copy-start | bytes 1179652
  100.4 3.4 %copy-start.11 = (bf16[192,1024]{1,0:T(8,128)(2,1)}, bf16[192,1024]{1,0:T(8,128)(2,1)S(1)}, u32[]{:S(2)}) copy-start(bf16[192,1024]{1,0:T(8,128)(2,1)S(1)} %get-tuple-element.187.refs_8_) | copy-start | bytes 1179652
  100.5 21.0 %collective-permute-start.20 = (bf16[192,1536]{1,0:T(8,128)(2,1)S(1)}, bf16[192,1536]{1,0:T(8,128)(2,1)S(1)}, u32[]{:S(2)}, u32[]{:S(2)}) collective-permute-start(bf16[192,1536]{1,0:T(8,128)(2,1)S(1)} %shard_map.124.a_ref), channel_id=1, source_target_pairs={{8,16},{16,8},{9,17},{17,9},{10,18},{18,10},{11,19},{19,11},{12,20... | collective-permute-start | bytes 1769480 | tf_op jit(solution)/shard_map/ppermute | solution.py:484
  107.3 20.1 %collective-permute-start.17 = (bf16[192,1536]{1,0:T(8,128)(2,1)}, bf16[192,1536]{1,0:T(8,128)(2,1)S(1)}, u32[]{:S(2)}, u32[]{:S(2)}) collective-permute-start(bf16[192,1536]{1,0:T(8,128)(2,1)} %get-tuple-element.182), channel_id=1, source_target_pairs={{0,8},{24,16},{8,0},{16,24},{1,9},{25,17},{9,1},{17,25},{2,10},{26... | collective-permute-start | bytes 1769480 | tf_op jit(solution)/shard_map/ppermute | solution.py:499
  118.2 3.4 %copy-start.13 = (bf16[192,1024]{1,0:T(8,128)(2,1)}, bf16[192,1024]{1,0:T(8,128)(2,1)S(1)}, u32[]{:S(2)}) copy-start(bf16[192,1024]{1,0:T(8,128)(2,1)S(1)} %get-tuple-element.241) | copy-start | bytes 1179652
  118.3 9.9 %collective-permute-start.19 = (bf16[192,1536]{1,0:T(8,128)(2,1)S(1)}, bf16[192,1536]{1,0:T(8,128)(2,1)S(1)}, u32[]{:S(2)}, u32[]{:S(2)}) collective-permute-start(bf16[192,1536]{1,0:T(8,128)(2,1)S(1)} %shard_map.128.a_ref), channel_id=1, source_target_pairs={{8,16},{16,8},{9,17},{17,9},{10,18},{18,10},{11,19},{19,11},{12,20... | collective-permute-start | bytes 1769480 | tf_op jit(solution)/shard_map/ppermute | solution.py:484
  122.4 17.1 %collective-permute-start.24 = (bf16[192,1536]{1,0:T(8,128)(2,1)S(1)}, bf16[192,1536]{1,0:T(8,128)(2,1)S(1)}, u32[]{:S(2)}, u32[]{:S(2)}) collective-permute-start(bf16[192,1536]{1,0:T(8,128)(2,1)S(1)} %get-tuple-element.195), channel_id=1, source_target_pairs={{0,8},{24,16},{8,0},{16,24},{1,9},{25,17},{9,1},{17,25},{2,10},{26... | collective-permute-start | bytes 1769480 | tf_op jit(solution)/shard_map/ppermute | solution.py:499
  125.2 6.7 %collective-permute-start.16 = (bf16[96,1920]{1,0:T(8,128)(2,1)}, bf16[96,1920]{1,0:T(8,128)(2,1)S(1)}, u32[]{:S(2)}, u32[]{:S(2)}) collective-permute-start(bf16[96,1920]{1,0:T(8,128)(2,1)} %get-tuple-element.189), channel_id=1, source_target_pairs={{0,1},{1,0},{2,3},{3,2},{4,5},{5,4},{6,7},{7,6},{8,9},{9,8},{10,11... | collective-permute-start | bytes 1105928 | tf_op jit(solution)/shard_map/ppermute | solution.py:463
  127.5 13.8 %collective-permute-start.26 = (bf16[192,1536]{1,0:T(8,128)(2,1)S(1)}, bf16[192,1536]{1,0:T(8,128)(2,1)S(1)}, u32[]{:S(2)}, u32[]{:S(2)}) collective-permute-start(bf16[192,1536]{1,0:T(8,128)(2,1)S(1)} %shard_map.132.a_ref), channel_id=1, source_target_pairs={{8,16},{16,8},{9,17},{17,9},{10,18},{18,10},{11,19},{19,11},{12,20... | collective-permute-start | bytes 1769480 | tf_op jit(solution)/shard_map/ppermute | solution.py:484
  128.4 22.1 %collective-permute-start.23 = (bf16[192,1536]{1,0:T(8,128)(2,1)S(1)}, bf16[192,1536]{1,0:T(8,128)(2,1)S(1)}, u32[]{:S(2)}, u32[]{:S(2)}) collective-permute-start(bf16[192,1536]{1,0:T(8,128)(2,1)S(1)} %shard_map.133.own_ref), channel_id=1, source_target_pairs={{8,0},{16,24},{9,1},{17,25},{10,2},{18,26},{11,3},{19,27},{12,4},{... | collective-permute-start | bytes 1769480 | tf_op jit(solution)/shard_map/ppermute | solution.py:503
  129.7 2.2 %copy-start.37 = (bf16[96,192]{1,0:T(8,128)(2,1)S(1)}, bf16[96,192]{1,0:T(8,128)(2,1)}, u32[]{:S(2)}) copy-start(bf16[96,192]{1,0:T(8,128)(2,1)} %copy-done.36) | copy-start | bytes 110596
  129.7 2.2 %copy-start.39 = (bf16[96,192]{1,0:T(8,128)(2,1)S(1)}, bf16[96,192]{1,0:T(8,128)(2,1)}, u32[]{:S(2)}) copy-start(bf16[96,192]{1,0:T(8,128)(2,1)} %copy-done.38) | copy-start | bytes 110596
  131.8 7.7 %copy-start.15 = (bf16[192,1024]{1,0:T(8,128)(2,1)}, bf16[192,1024]{1,0:T(8,128)(2,1)S(1)}, u32[]{:S(2)}) copy-start(bf16[192,1024]{1,0:T(8,128)(2,1)S(1)} %get-tuple-element.238) | copy-start | bytes 1179652
  131.9 7.7 %copy-start.17 = (bf16[192,1024]{1,0:T(8,128)(2,1)}, bf16[192,1024]{1,0:T(8,128)(2,1)S(1)}, u32[]{:S(2)}) copy-start(bf16[192,1024]{1,0:T(8,128)(2,1)S(1)} %get-tuple-element.242) | copy-start | bytes 1179652
  139.6 5.5 %collective-permute-start.25 = (bf16[192,1536]{1,0:T(8,128)(2,1)S(1)}, bf16[192,1536]{1,0:T(8,128)(2,1)S(1)}, u32[]{:S(2)}, u32[]{:S(2)}) collective-permute-start(bf16[192,1536]{1,0:T(8,128)(2,1)S(1)} %shard_map.135.a_ref), channel_id=1, source_target_pairs={{8,16},{16,8},{9,17},{17,9},{10,18},{18,10},{11,19},{19,11},{12,20... | collective-permute-start | bytes 1769480 | tf_op jit(solution)/shard_map/ppermute | solution.py:484
  140.4 4.7 %copy-start.27 = (bf16[576,1792]{1,0:T(8,128)(2,1)}, bf16[576,1792]{1,0:T(8,128)(2,1)S(1)}, u32[]{:S(2)}) copy-start(bf16[576,1792]{1,0:T(8,128)(2,1)S(1)} %constant_dynamic-update-slice_fusion) | copy-start | bytes 6193156
  140.4 17.4 %collective-permute-start.21 = (bf16[96,1920]{1,0:T(8,128)(2,1)S(1)}, bf16[96,1920]{1,0:T(8,128)(2,1)S(1)}, u32[]{:S(2)}, u32[]{:S(2)}) collective-permute-start(bf16[96,1920]{1,0:T(8,128)(2,1)S(1)} %get-tuple-element.205), channel_id=1, source_target_pairs={{0,2},{1,3},{2,0},{3,1},{4,6},{5,7},{6,4},{7,5},{8,10},{9,11},{10,... | collective-permute-start | bytes 1105928 | tf_op jit(solution)/shard_map/ppermute | solution.py:463
  141.2 16.5 %collective-permute-start.22 = (bf16[96,1920]{1,0:T(8,128)(2,1)S(1)}, bf16[96,1920]{1,0:T(8,128)(2,1)S(1)}, u32[]{:S(2)}, u32[]{:S(2)}) collective-permute-start(bf16[96,1920]{1,0:T(8,128)(2,1)S(1)} %get-tuple-element.208), channel_id=1, source_target_pairs={{0,3},{1,2},{2,1},{3,0},{4,7},{5,6},{6,5},{7,4},{8,11},{9,10},{10,... | collective-permute-start | bytes 1105928 | tf_op jit(solution)/shard_map/ppermute | solution.py:463
  141.5 23.0 %collective-permute-start.30 = (bf16[192,1536]{1,0:T(8,128)(2,1)S(1)}, bf16[192,1536]{1,0:T(8,128)(2,1)S(1)}, u32[]{:S(2)}, u32[]{:S(2)}) collective-permute-start(bf16[192,1536]{1,0:T(8,128)(2,1)S(1)} %shard_map.136.own_ref), channel_id=1, source_target_pairs={{8,0},{16,24},{9,1},{17,25},{10,2},{18,26},{11,3},{19,27},{12,4},{... | collective-permute-start | bytes 1769480 | tf_op jit(solution)/shard_map/ppermute | solution.py:503
  145.3 30.3 %collective-permute-start.29 = (bf16[192,1536]{1,0:T(8,128)(2,1)S(1)}, bf16[192,1536]{1,0:T(8,128)(2,1)S(1)}, u32[]{:S(2)}, u32[]{:S(2)}) collective-permute-start(bf16[192,1536]{1,0:T(8,128)(2,1)S(1)} %shard_map.138.own_ref), channel_id=1, source_target_pairs={{8,0},{16,24},{9,1},{17,25},{10,2},{18,26},{11,3},{19,27},{12,4},{... | collective-permute-start | bytes 1769480 | tf_op jit(solution)/shard_map/ppermute | solution.py:503
  152.7 26.6 %collective-permute-start.27 = (bf16[96,1920]{1,0:T(8,128)(2,1)S(1)}, bf16[96,1920]{1,0:T(8,128)(2,1)}, u32[]{:S(2)}, u32[]{:S(2)}) collective-permute-start(bf16[96,1920]{1,0:T(8,128)(2,1)S(1)} %get-tuple-element.223), channel_id=1, source_target_pairs={{0,4},{1,5},{2,6},{3,7},{4,0},{5,1},{6,2},{7,3},{8,12},{9,13},{10,... | collective-permute-start | bytes 1105928 | tf_op jit(solution)/shard_map/ppermute | solution.py:463
  154.4 3.6 %copy-start.32 = (bf16[96,192]{1,0:T(8,128)(2,1)S(1)}, bf16[96,192]{1,0:T(8,128)(2,1)}, u32[]{:S(2)}) copy-start(bf16[96,192]{1,0:T(8,128)(2,1)} %get-tuple-element.267) | copy-start | bytes 110596
  154.4 3.6 %copy-start.33 = (bf16[96,192]{1,0:T(8,128)(2,1)S(1)}, bf16[96,192]{1,0:T(8,128)(2,1)}, u32[]{:S(2)}) copy-start(bf16[96,192]{1,0:T(8,128)(2,1)} %get-tuple-element.268) | copy-start | bytes 110596
  157.7 21.5 %collective-permute-start.28 = (bf16[96,1920]{1,0:T(8,128)(2,1)S(1)}, bf16[96,1920]{1,0:T(8,128)(2,1)S(1)}, u32[]{:S(2)}, u32[]{:S(2)}) collective-permute-start(bf16[96,1920]{1,0:T(8,128)(2,1)S(1)} %get-tuple-element.230), channel_id=1, source_target_pairs={{0,5},{1,4},{2,7},{3,6},{4,1},{5,0},{6,3},{7,2},{8,13},{9,12},{10,... | collective-permute-start | bytes 1105928 | tf_op jit(solution)/shard_map/ppermute | solution.py:463
  159.4 7.1 %copy-start.10 = (bf16[192,1024]{1,0:T(8,128)(2,1)S(1)}, bf16[192,1024]{1,0:T(8,128)(2,1)}, u32[]{:S(2)}) copy-start(bf16[192,1024]{1,0:T(8,128)(2,1)} %copy-done.9) | copy-start | bytes 1179652
  159.5 7.1 %copy-start.16 = (bf16[192,1024]{1,0:T(8,128)(2,1)S(1)}, bf16[192,1024]{1,0:T(8,128)(2,1)}, u32[]{:S(2)}) copy-start(bf16[192,1024]{1,0:T(8,128)(2,1)} %copy-done.15) | copy-start | bytes 1179652
  159.5 7.1 %copy-start.28 = (bf16[576,1792]{1,0:T(8,128)(2,1)S(1)}, bf16[576,1792]{1,0:T(8,128)(2,1)}, u32[]{:S(2)}) copy-start(bf16[576,1792]{1,0:T(8,128)(2,1)} %copy-done.27) | copy-start | bytes 6193156
  166.6 3.3 %copy-start.14 = (bf16[192,1024]{1,0:T(8,128)(2,1)S(1)}, bf16[192,1024]{1,0:T(8,128)(2,1)}, u32[]{:S(2)}) copy-start(bf16[192,1024]{1,0:T(8,128)(2,1)} %copy-done.13) | copy-start | bytes 1179652
  166.6 3.3 %copy-start.18 = (bf16[192,1024]{1,0:T(8,128)(2,1)S(1)}, bf16[192,1024]{1,0:T(8,128)(2,1)}, u32[]{:S(2)}) copy-start(bf16[192,1024]{1,0:T(8,128)(2,1)} %copy-done.17) | copy-start | bytes 1179652
  166.6 3.3 %copy-start.29 = (bf16[576,1792]{1,0:T(8,128)(2,1)S(1)}, bf16[576,1792]{1,0:T(8,128)(2,1)}, u32[]{:S(2)}) copy-start(bf16[576,1792]{1,0:T(8,128)(2,1)} %copy-done.27) | copy-start | bytes 6193156
  175.6 4.8 %copy-start.30 = (bf16[96,192]{1,0:T(8,128)(2,1)S(1)}, bf16[96,192]{1,0:T(8,128)(2,1)}, u32[]{:S(2)}) copy-start(bf16[96,192]{1,0:T(8,128)(2,1)} %get-tuple-element.265) | copy-start | bytes 110596
  175.6 4.8 %copy-start.31 = (bf16[96,192]{1,0:T(8,128)(2,1)S(1)}, bf16[96,192]{1,0:T(8,128)(2,1)}, u32[]{:S(2)}) copy-start(bf16[96,192]{1,0:T(8,128)(2,1)} %get-tuple-element.266) | copy-start | bytes 110596
  177.7 17.4 %collective-permute-start.31 = (bf16[96,1920]{1,0:T(8,128)(2,1)S(1)}, bf16[96,1920]{1,0:T(8,128)(2,1)S(1)}, u32[]{:S(2)}, u32[]{:S(2)}) collective-permute-start(bf16[96,1920]{1,0:T(8,128)(2,1)S(1)} %get-tuple-element.249), channel_id=1, source_target_pairs={{0,6},{1,7},{2,4},{3,5},{4,2},{5,3},{6,0},{7,1},{8,14},{9,15},{10,... | collective-permute-start | bytes 1105928 | tf_op jit(solution)/shard_map/ppermute | solution.py:463
  180.3 14.9 %collective-permute-start.32 = (bf16[96,1920]{1,0:T(8,128)(2,1)S(1)}, bf16[96,1920]{1,0:T(8,128)(2,1)S(1)}, u32[]{:S(2)}, u32[]{:S(2)}) collective-permute-start(bf16[96,1920]{1,0:T(8,128)(2,1)S(1)} %get-tuple-element.252), channel_id=1, source_target_pairs={{0,7},{1,6},{2,5},{3,4},{4,3},{5,2},{6,1},{7,0},{8,15},{9,14},{10,... | collective-permute-start | bytes 1105928 | tf_op jit(solution)/shard_map/ppermute | solution.py:463
  189.7 6.0 %copy-start.40 = (s32[192,2]{0,1:T(2,128)S(1)}, s32[192,2]{0,1:T(2,128)}, u32[]{:S(2)}) copy-start(s32[192,2]{0,1:T(2,128)} %param.9) | copy-start | bytes 4612
  189.7 6.6 %copy-start.34 = (bf16[96,192]{1,0:T(8,128)(2,1)S(1)}, bf16[96,192]{1,0:T(8,128)(2,1)}, u32[]{:S(2)}) copy-start(bf16[96,192]{1,0:T(8,128)(2,1)} %get-tuple-element.263) | copy-start | bytes 110596
  189.7 6.6 %copy-start.35 = (bf16[96,192]{1,0:T(8,128)(2,1)S(1)}, bf16[96,192]{1,0:T(8,128)(2,1)}, u32[]{:S(2)}) copy-start(bf16[96,192]{1,0:T(8,128)(2,1)} %get-tuple-element.264) | copy-start | bytes 110596
  194.2 2.1 %copy-start.25 = (f32[192,1792]{1,0:T(8,128)S(1)}, f32[192,1792]{1,0:T(8,128)}, u32[]{:S(2)}) copy-start(f32[192,1792]{1,0:T(8,128)} %convolution_add_fusion.1) | copy-start | bytes 4128772
  (14 other events, 17.4 us)
where the time goes:
time: 201 us; the launch traced here: 198 us
  Pallas kernels  58.9 us (29%)
  starting transfers between devices  56.6 us (28%)
  waiting for transfers between devices  37.9 us (19%)
  matrix products  23 us (11%)
  local copies, waits for them, and re-layouts  15.6 us (8%)
  other arithmetic  3.83 us (2%)
    ppermute x5, starting transfers between devices, body(): arrived[t + 1] = lax.ppermute(both, 'dp', inward + outward)  24.5 us
    pallas_call x8, Pallas kernels, forward_piece(): pl.pallas_call(functools.partial(forward_kernel, len(rows), width, per_ar...  21.3 us
    pallas_call x8, Pallas kernels, backward_piece(): pl.pallas_call(functools.partial(backward_kernel, len(rows), width, half...  18.3 us
    pallas_call x3, Pallas kernels, gradient_add(): pl.pallas_call(gradient_kernel, grid=(height // BLOCK,), in_specs=[pl.Blo...  12.3 us
    unnamed x93, local copies, waits for them, and re-layouts  11.9 us
    ppermute x3, waiting for transfers between devices, body(): spread_out[k] = lax.ppermute(total[k], 'dp', outward)  11.2 us
    dot_general x3, matrix products, add_gradient(): lax.dot_general(rows_left, rows_right, over_rows, preferred_element_type=...  9.92 us
    ppermute x1, waiting for transfers between devices, body(): arrived[0] = lax.ppermute(part[0], 'dp', inward)  9.5 us
  transfers between devices with their start and end apart: 33, of which 10 were waited for; matrix products, arithmetic and copies ran while one was open for 10% of the time, Pallas kernels for 30%

commit v1 on v0

--- a/solution.py
+++ b/solution.py
@@ -469,8 +469,8 @@
             5: [(finish, 1)],
             6: [(finish, 2)],
             7: [(finish, 3), (take_back, chunks[0])],
-            8: [(finish, 4)],
-            9: [(finish, 5), (add_gradient, 0), (take_back, chunks[1])],
+            8: [(finish, 4), (finish, 5), (add_gradient, 0)],
+            9: [(take_back, chunks[1]), (add_gradient, 1), (add_gradient, 2)],
         }
         compute_part(0)
         arrived[0] = lax.ppermute(part[0], "dp", inward)
@@ -504,8 +504,6 @@
             for step, c in work.get(t, ()):
                 step(c)
         finish(6)
-        add_gradient(1)
-        add_gradient(2)
         finish(7)
         take_back(chunks[2])
     for which in range(3):

time: 201 us -> 209 us (1.040)
  waiting for transfers between devices: 37.9 us -> 58.6 us
  starting transfers between devices: 56.6 us -> 49.4 us
  local copies, waits for them, and re-layouts: 15.6 us -> 13.4 us
    ppermute x5, waiting for transfers between devices: 8.76 us -> 17.5 us  [body(): arrived[t + 1] = lax.ppermute(both, 'dp', inward + outward)]
    ppermute x5, starting transfers between devices: 24.5 us -> 17.3 us  [body(): arrived[t + 1] = lax.ppermute(both, 'dp', inward + outward)]
    ppermute x1, waiting for transfers between devices: 3.16 us -> 8.88 us  [body(): arrived[1] = lax.ppermute(part[1], 'dp', inward)]
    ppermute x7, waiting for transfers between devices: 0.02 us -> 2.44 us  [finish(): one = lax.ppermute(one, 'expert', [(i, i ^ r) for i in range(groups)])]
    dot_general x4, matrix products: 4.55 us -> 2.35 us  [take_back(): lax.dot_general(spread, stacked, over_rows, preferred_element_type=F32)]
    ppermute x3, waiting for transfers between devices: 11.2 us -> 13.4 us  [body(): spread_out[k] = lax.ppermute(total[k], 'dp', outward)]
    ppermute x3, waiting for transfers between devices: 0.01 us -> 2.17 us  [hand_on(): lax.ppermute(other, 'expert', [(i, i ^ 1) for i in range(groups)])]
    unnamed x93 -> x77, local copies, waits for them, and re-layouts: 11.9 us -> 11.6 us
  transfers between devices with their start and end apart: 33 -> 33, of which waited for: 10 -> 13; matrix products, arithmetic and copies ran while one was open for 10% -> 9% of each run, Pallas kernels for 30% -> 27%
where the time goes in v1:
time: 209 us; the launch traced here: 207 us
  Pallas kernels  58.9 us (28%)
  waiting for transfers between devices  58.6 us (28%)
  starting transfers between devices  49.4 us (24%)
  matrix products  21.6 us (10%)
  local copies, waits for them, and re-layouts  13.4 us (6%)
  other arithmetic  3.83 us (2%)
    pallas_call x8, Pallas kernels, forward_piece(): pl.pallas_call(functools.partial(forward_kernel, len(rows), width, per_ar...  21.3 us
    pallas_call x8, Pallas kernels, backward_piece(): pl.pallas_call(functools.partial(backward_kernel, len(rows), width, half...  18.3 us
    ppermute x5, waiting for transfers between devices, body(): arrived[t + 1] = lax.ppermute(both, 'dp', inward + outward)  17.5 us
    ppermute x5, starting transfers between devices, body(): arrived[t + 1] = lax.ppermute(both, 'dp', inward + outward)  17.3 us
    ppermute x3, waiting for transfers between devices, body(): spread_out[k] = lax.ppermute(total[k], 'dp', outward)  13.4 us
    pallas_call x3, Pallas kernels, gradient_add(): pl.pallas_call(gradient_kernel, grid=(height // BLOCK,), in_specs=[pl.Blo...  12.3 us
    unnamed x77, local copies, waits for them, and re-layouts  11.6 us
    dot_general x3, matrix products, add_gradient(): lax.dot_general(rows_left, rows_right, over_rows, preferred_element_type=...  9.89 us
  transfers between devices with their start and end apart: 33, of which 13 were waited for; matrix products, arithmetic and copies ran while one was open for 9% of the time, Pallas kernels for 27%

profile of v1, /device:TPU:0, one launch (start us, length us, event | category | flops | bytes accessed | tf_op | source)
XLA Modules:
  0.0 207.4 jit_solution(17822859210421220685)
XLA Ops:
  4.2 3.1 %convolution_convert_fusion.2 = bf16[192,3712]{1,0:T(8,128)(2,1)} fusion(pred[192,192]{1,0:T(32,128)(4,1)S(1)} %bitcast.60, bf16[192,3]{1,0:T(8,128)(2,1)S(1)} %copy.32, bf16[192,1792]{1,0:T(8,128)(2,1)} %param.8, bf16[192,1792]{1,0:T(8,128)(2,1)} %param.7), kind=kOutput, calls=%fused_computation.2 | convolution fusion | flops 280092672 | bytes 2839680 | tf_op jit(solution)/shard_map/dot_general | solution.py:408
  7.2 1.6 convolution_convert_fusion.1
  8.9 3.0 %collective-permute-start.2 = (bf16[192,3712]{1,0:T(8,128)(2,1)}, bf16[192,3712]{1,0:T(8,128)(2,1)S(1)}, u32[]{:S(2)}, u32[]{:S(2)}) collective-permute-start(bf16[192,3712]{1,0:T(8,128)(2,1)} %convolution_convert_fusion.1), channel_id=1, source_target_pairs={{0,4},{1,5},{2,6},{3,7},{4,0},{5,1},{6,2},{7,3},{8,12},{9,13},{10,... | collective-permute-start | bytes 4276232 | tf_op jit(solution)/shard_map/ppermute | solution.py:415
  11.8 1.5 collective-permute-start.3
  14.0 2.1 %convolution_convert_fusion.4 = bf16[96,3712]{1,0:T(8,128)(2,1)} fusion(bf16[96,192]{1,0:T(8,128)(2,1)S(1)} %get-tuple-element.135, bf16[192,3]{1,0:T(8,128)(2,1)} %copy-done.30, bf16[192,1792]{1,0:T(8,128)(2,1)S(1)} %copy-done.33, bf16[192,1792]{1,0:T(8,128)(2,1)S(1)} %copy-done.35), kind=kOutput, calls=%fused_computation.4 | convolution fusion | flops 142897152 | bytes 2126976 | tf_op jit(solution)/shard_map/dot_general | solution.py:287
  16.2 1.8 convolution_convert_fusion.3.refs_0_
  18.6 2.0 copy-done.1
  20.7 2.0 copy-done.3
  22.7 3.1 %shard_map.110 = (bf16[192,1536]{1,0:T(8,128)(2,1)S(1)}, bf16[192,1792]{1,0:T(8,128)(2,1)S(1)}, bf16[192,1792]{1,0:T(8,128)(2,1)S(1)}) custom-call(s32[2]{0:T(128)S(1)} %pad_add_fusion.scalars.middle_ref, bf16[96,3712]{1,0:T(8,128)(2,1)S(1)} %convolution_convert_fusion.3.refs_0_, bf16[96,3712]{1,0:T(8,128)(2,1)} %collective-permute-done.refs_1_, ...), custom_call_target="tpu_custom_call" | custom-call | flops 1 | bytes 1 | tf_op jit(solution)/shard_map/pallas_call | solution.py:84
  25.8 0.8 copy-done.13
  26.7 3.6 %collective-permute-start.4 = (bf16[192,1536]{1,0:T(8,128)(2,1)S(1)}, bf16[192,1536]{1,0:T(8,128)(2,1)S(1)}, u32[]{:S(2)}, u32[]{:S(2)}) collective-permute-start(bf16[192,1536]{1,0:T(8,128)(2,1)S(1)} %get-tuple-element.140.a_ref), channel_id=1, source_target_pairs={{0,8},{24,16},{1,9},{25,17},{2,10},{26,18},{3,11},{27,19},{4,12},{... | collective-permute-start | bytes 1769480 | tf_op jit(solution)/shard_map/ppermute | solution.py:476
  30.3 3.1 %shard_map.111.a_ref = bf16[192,1536]{1,0:T(8,128)(2,1)S(1)} custom-call(s32[2]{0:T(128)S(1)} %pad_add_fusion.scalars.middle_ref, bf16[96,3712]{1,0:T(8,128)(2,1)S(1)} %convolution_convert_fusion.3.refs_0_, bf16[96,3712]{1,0:T(8,128)(2,1)} %collective-permute-done.refs_1_, bf16[1,1792,1024]{2,1,0:T(8,128)(2,1)S(1)} %copy-done, ...), custom_call_target="tpu_custom_call" | custom-call | flops 1 | bytes 1 | tf_op jit(solution)/shard_map/pallas_call | solution.py:84
  34.0 9.5 %collective-permute-done.4.b_ref = bf16[192,1536]{1,0:T(8,128)(2,1)S(1)} collective-permute-done((bf16[192,1536]{1,0:T(8,128)(2,1)S(1)}, bf16[192,1536]{1,0:T(8,128)(2,1)S(1)}, u32[]{:S(2)}, u32[]{:S(2)}) %collective-permute-start.4) | collective-permute-done | bytes 589856 | tf_op jit(solution)/shard_map/ppermute | solution.py:476
  43.6 1.1 collective-permute-done.3.refs_0_
  44.9 2.2 %collective-permute-done.5.refs_1_ = bf16[96,3712]{1,0:T(8,128)(2,1)S(1)} collective-permute-done((bf16[96,3712]{1,0:T(8,128)(2,1)S(1)}, bf16[96,3712]{1,0:T(8,128)(2,1)S(1)}, u32[]{:S(2)}, u32[]{:S(2)}) %collective-permute-start.5) | collective-permute-done | bytes 712736 | tf_op jit(solution)/shard_map/ppermute | solution.py:427
  47.1 2.5 %shard_map.113 = (bf16[192,1536]{1,0:T(8,128)(2,1)S(1)}, bf16[192,1792]{1,0:T(8,128)(2,1)S(1)}, bf16[192,1792]{1,0:T(8,128)(2,1)S(1)}) custom-call(s32[2]{0:T(128)S(1)} %pad_add_fusion.scalars.middle_ref, bf16[192,3712]{1,0:T(8,128)(2,1)S(1)} %collective-permute-done.3.refs_0_, bf16[96,3712]{1,0:T(8,128)(2,1)S(1)} %collective-permute-done.5.refs_1_, ...), custom_call_target="tpu_custom_call" | custom-call | flops 1 | bytes 1 | tf_op jit(solution)/shard_map/pallas_call | solution.py:84
  49.6 0.8 copy-done.15
  50.5 1.4 collective-permute-start.14
  51.9 3.5 %collective-permute-start.1 = (bf16[192,1536]{1,0:T(8,128)(2,1)S(1)}, bf16[192,1536]{1,0:T(8,128)(2,1)S(1)}, u32[]{:S(2)}, u32[]{:S(2)}) collective-permute-start(bf16[192,1536]{1,0:T(8,128)(2,1)S(1)} %shard_map.111.a_ref), channel_id=1, source_target_pairs={{0,8},{24,16},{1,9},{25,17},{2,10},{26,18},{3,11},{27,19},{4,12},{... | collective-permute-start | bytes 1769480 | tf_op jit(solution)/shard_map/ppermute | solution.py:478
  56.1 4.1 %collective-permute-start.7 = (bf16[192,1536]{1,0:T(8,128)(2,1)S(1)}, bf16[192,1536]{1,0:T(8,128)(2,1)S(1)}, u32[]{:S(2)}, u32[]{:S(2)}) collective-permute-start(bf16[192,1536]{1,0:T(8,128)(2,1)S(1)} %get-tuple-element.152.a_ref), channel_id=1, source_target_pairs={{0,8},{24,16},{1,9},{25,17},{2,10},{26,18},{3,11},{27,19},{4,12},{... | collective-permute-start | bytes 1769480 | tf_op jit(solution)/shard_map/ppermute | solution.py:492
  60.2 8.9 %collective-permute-done.1.b_ref = bf16[192,1536]{1,0:T(8,128)(2,1)S(1)} collective-permute-done((bf16[192,1536]{1,0:T(8,128)(2,1)S(1)}, bf16[192,1536]{1,0:T(8,128)(2,1)S(1)}, u32[]{:S(2)}, u32[]{:S(2)}) %collective-permute-start.1) | collective-permute-done | bytes 589856 | tf_op jit(solution)/shard_map/ppermute | solution.py:478
  70.0 2.5 %shard_map.115.other_ref.a_ref = bf16[192,1536]{1,0:T(8,128)(2,1)S(1)} custom-call(s32[2]{0:T(128)S(1)} %pad_add_fusion.scalars.middle_ref, bf16[192,3712]{1,0:T(8,128)(2,1)S(1)} %collective-permute-done.3.refs_0_, bf16[96,3712]{1,0:T(8,128)(2,1)S(1)} %collective-permute-done.5.refs_1_, bf16[1,1792,1024]{2,1,0:T(8,128)(2,1)S(1)} %copy-done, ...), custom_call_target="tpu_custom_call" | custom-call | flops 1 | bytes 1 | tf_op jit(solution)/shard_map/pallas_call | solution.py:84
  73.4 5.3 %collective-permute-start.11 = (bf16[192,1536]{1,0:T(8,128)(2,1)S(1)}, bf16[192,1536]{1,0:T(8,128)(2,1)S(1)}, u32[]{:S(2)}, u32[]{:S(2)}) collective-permute-start(bf16[192,1536]{1,0:T(8,128)(2,1)S(1)} %get-tuple-element.156), channel_id=1, source_target_pairs={{0,8},{24,16},{8,0},{16,24},{1,9},{25,17},{9,1},{17,25},{2,10},{26... | collective-permute-start | bytes 1769480 | tf_op jit(solution)/shard_map/ppermute | solution.py:499
  78.7 3.0 %collective-permute-done.7.b_ref = bf16[192,1536]{1,0:T(8,128)(2,1)S(1)} collective-permute-done((bf16[192,1536]{1,0:T(8,128)(2,1)S(1)}, bf16[192,1536]{1,0:T(8,128)(2,1)S(1)}, u32[]{:S(2)}, u32[]{:S(2)}) %collective-permute-start.7) | collective-permute-done | bytes 589856 | tf_op jit(solution)/shard_map/ppermute | solution.py:492
  82.6 2.5 %shard_map.118 = (bf16[192,1536]{1,0:T(8,128)(2,1)S(1)}, bf16[192,1792]{1,0:T(8,128)(2,1)S(1)}, bf16[192,1792]{1,0:T(8,128)(2,1)S(1)}) custom-call(s32[2]{0:T(128)S(1)} %pad_add_fusion.scalars.middle_ref, bf16[192,3712]{1,0:T(8,128)(2,1)S(1)} %collective-permute-done.2.refs_0_, bf16[96,3712]{1,0:T(8,128)(2,1)S(1)} %collective-permute-done.9.refs_1_, ...), custom_call_target="tpu_custom_call" | custom-call | flops 1 | bytes 1 | tf_op jit(solution)/shard_map/pallas_call | solution.py:84
  85.9 7.3 %collective-permute-done.11.b_ref.came_ref = bf16[192,1536]{1,0:T(8,128)(2,1)S(1)} collective-permute-done((bf16[192,1536]{1,0:T(8,128)(2,1)S(1)}, bf16[192,1536]{1,0:T(8,128)(2,1)S(1)}, u32[]{:S(2)}, u32[]{:S(2)}) %collective-permute-start.11) | collective-permute-done | bytes 589856 | tf_op jit(solution)/shard_map/ppermute | solution.py:499
  93.5 2.5 %collective-permute-start.10 = (bf16[192,1536]{1,0:T(8,128)(2,1)S(1)}, bf16[192,1536]{1,0:T(8,128)(2,1)S(1)}, u32[]{:S(2)}, u32[]{:S(2)}) collective-permute-start(bf16[192,1536]{1,0:T(8,128)(2,1)S(1)} %get-tuple-element.165), channel_id=1, source_target_pairs={{0,8},{24,16},{8,0},{16,24},{1,9},{25,17},{9,1},{17,25},{2,10},{26... | collective-permute-start | bytes 1769480 | tf_op jit(solution)/shard_map/ppermute | solution.py:499
  96.1 0.9 collective-permute-start.12
  97.0 2.5 %shard_map.121.other_ref.a_ref = bf16[192,1536]{1,0:T(8,128)(2,1)S(1)} custom-call(s32[2]{0:T(128)S(1)} %pad_add_fusion.scalars.middle_ref, bf16[192,3712]{1,0:T(8,128)(2,1)S(1)} %collective-permute-done.2.refs_0_, bf16[96,3712]{1,0:T(8,128)(2,1)S(1)} %collective-permute-done.9.refs_1_, bf16[1,1792,1024]{2,1,0:T(8,128)(2,1)S(1)} %copy-done, ...), custom_call_target="tpu_custom_call" | custom-call | flops 1 | bytes 1 | tf_op jit(solution)/shard_map/pallas_call | solution.py:84
  99.5 1.6 shard_map.122
  101.1 3.0 %collective-permute-start.18 = (bf16[192,1536]{1,0:T(8,128)(2,1)}, bf16[192,1536]{1,0:T(8,128)(2,1)S(1)}, u32[]{:S(2)}, u32[]{:S(2)}) collective-permute-start(bf16[192,1536]{1,0:T(8,128)(2,1)} %get-tuple-element.172), channel_id=1, source_target_pairs={{0,8},{24,16},{8,0},{16,24},{1,9},{25,17},{9,1},{17,25},{2,10},{26... | collective-permute-start | bytes 1769480 | tf_op jit(solution)/shard_map/ppermute | solution.py:499
  104.1 2.5 %shard_map.123 = (bf16[192,1024]{1,0:T(8,128)(2,1)S(1)}, bf16[192,1024]{1,0:T(8,128)(2,1)S(1)}, bf16[192,1024]{1,0:T(8,128)(2,1)S(1)}, f32[192,1792]{1,0:T(8,128)S(1)}, f32[192,128]{1,0:T(8,128)S(1)}) custom-call(s32[2]{0:T(128)S(1)} %pad_add_fusion.scalars.middle_ref, bf16[192,1536]{1,0:T(8,128)(2,1)S(1)} %get-tuple-element.167.own_ref, ...), custom_call_target="tpu_custom_call" | custom-call | flops 1 | bytes 1 | tf_op jit(solution)/shard_map/pallas_call | solution.py:196
  106.6 3.7 %collective-permute-done.10.b_ref.came_ref = bf16[192,1536]{1,0:T(8,128)(2,1)S(1)} collective-permute-done((bf16[192,1536]{1,0:T(8,128)(2,1)S(1)}, bf16[192,1536]{1,0:T(8,128)(2,1)S(1)}, u32[]{:S(2)}, u32[]{:S(2)}) %collective-permute-start.10) | collective-permute-done | bytes 589856 | tf_op jit(solution)/shard_map/ppermute | solution.py:499
  111.1 2.5 %shard_map.125 = (bf16[192,1536]{1,0:T(8,128)(2,1)S(1)}, bf16[192,1792]{1,0:T(8,128)(2,1)S(1)}, bf16[192,1792]{1,0:T(8,128)(2,1)S(1)}) custom-call(s32[2]{0:T(128)S(1)} %pad_add_fusion.scalars.middle_ref, bf16[192,3712]{1,0:T(8,128)(2,1)S(1)} %collective-permute-done.14.refs_0_, bf16[96,3712]{1,0:T(8,128)(2,1)S(1)} %collective-permute-done.15.refs_1_, ...), custom_call_target="tpu_custom_call" | custom-call | flops 1 | bytes 1 | tf_op jit(solution)/shard_map/pallas_call | solution.py:84
  114.5 1.1 copy-done.6
  115.6 1.6 shard_map.126
  117.2 4.7 %collective-permute-start.17 = (bf16[192,1536]{1,0:T(8,128)(2,1)}, bf16[192,1536]{1,0:T(8,128)(2,1)S(1)}, u32[]{:S(2)}, u32[]{:S(2)}) collective-permute-start(bf16[192,1536]{1,0:T(8,128)(2,1)} %get-tuple-element.182), channel_id=1, source_target_pairs={{0,8},{24,16},{8,0},{16,24},{1,9},{25,17},{9,1},{17,25},{2,10},{26... | collective-permute-start | bytes 1769480 | tf_op jit(solution)/shard_map/ppermute | solution.py:499
  121.9 3.1 %shard_map.127 = (bf16[192,1024]{1,0:T(8,128)(2,1)S(1)}, bf16[192,1024]{1,0:T(8,128)(2,1)S(1)}, bf16[192,1024]{1,0:T(8,128)(2,1)S(1)}, bf16[96,1920]{1,0:T(8,128)(2,1)S(1)}, bf16[96,1920]{1,0:T(8,128)(2,1)}) custom-call(s32[2]{0:T(128)S(1)} %pad_add_fusion.scalars.middle_ref, ...), custom_call_target="tpu_custom_call", output_to_operand_aliasing={{0}: (9, {}), {1}: (10, {}), {2}: (11, {})} | custom-call | flops 1 | bytes 1 | tf_op jit(solution)/shard_map/pallas_call | solution.py:196
  127.4 0.9 constant_dynamic-update-slice_fusion.2
  128.2 2.5 %shard_map.129.other_ref.a_ref = bf16[192,1536]{1,0:T(8,128)(2,1)S(1)} custom-call(s32[2]{0:T(128)S(1)} %pad_add_fusion.scalars.middle_ref, bf16[192,3712]{1,0:T(8,128)(2,1)S(1)} %collective-permute-done.14.refs_0_, bf16[96,3712]{1,0:T(8,128)(2,1)S(1)} %collective-permute-done.15.refs_1_, bf16[1,1792,1024]{2,1,0:T(8,128)(2,1)S(1)} %copy-done, ...), custom_call_target="tpu_custom_call" | custom-call | flops 1 | bytes 1 | tf_op jit(solution)/shard_map/pallas_call | solution.py:84
  131.6 1.7 collective-permute-start.23
  133.3 2.1 %shard_map.131 = (bf16[192,1024]{1,0:T(8,128)(2,1)S(1)}, bf16[192,1024]{1,0:T(8,128)(2,1)S(1)}, bf16[192,1024]{1,0:T(8,128)(2,1)S(1)}, f32[192,1792]{1,0:T(8,128)S(1)}, f32[192,128]{1,0:T(8,128)S(1)}) custom-call(s32[2]{0:T(128)S(1)} %pad_add_fusion.scalars.middle_ref, bf16[192,1536]{1,0:T(8,128)(2,1)S(1)} %get-tuple-element.192.own_ref, ...), custom_call_target="tpu_custom_call" | custom-call | flops 1 | bytes 1 | tf_op jit(solution)/shard_map/pallas_call | solution.py:196
  135.9 0.8 collective-permute-start.26
  136.9 1.3 collective-permute-start.25
  138.4 2.1 %shard_map.134 = (bf16[192,1024]{1,0:T(8,128)(2,1)S(1)}, bf16[192,1024]{1,0:T(8,128)(2,1)S(1)}, bf16[192,1024]{1,0:T(8,128)(2,1)S(1)}, bf16[96,1920]{1,0:T(8,128)(2,1)S(1)}, bf16[96,1920]{1,0:T(8,128)(2,1)S(1)}) custom-call(s32[2]{0:T(128)S(1)} %pad_add_fusion.scalars.middle_ref, ...), custom_call_target="tpu_custom_call", output_to_operand_aliasing={{0}: (9, {}), {1}: (10, {}), {2}: (11, {})} | custom-call | flops 1 | bytes 1 | tf_op jit(solution)/shard_map/pallas_call | solution.py:196
  142.3 6.1 %collective-permute-done.23.b_ref.came_ref = bf16[192,1536]{1,0:T(8,128)(2,1)S(1)} collective-permute-done((bf16[192,1536]{1,0:T(8,128)(2,1)S(1)}, bf16[192,1536]{1,0:T(8,128)(2,1)S(1)}, u32[]{:S(2)}, u32[]{:S(2)}) %collective-permute-start.23) | collective-permute-done | bytes 589856 | tf_op jit(solution)/shard_map/ppermute | solution.py:499
  149.5 1.5 collective-permute-start.30
  151.0 2.1 %shard_map.137 = (bf16[192,1024]{1,0:T(8,128)(2,1)S(1)}, bf16[192,1024]{1,0:T(8,128)(2,1)S(1)}, bf16[192,1024]{1,0:T(8,128)(2,1)S(1)}, f32[192,1792]{1,0:T(8,128)S(1)}, f32[192,128]{1,0:T(8,128)S(1)}) custom-call(s32[2]{0:T(128)S(1)} %pad_add_fusion.scalars.middle_ref, bf16[192,1536]{1,0:T(8,128)(2,1)S(1)} %get-tuple-element.212.own_ref, ...), custom_call_target="tpu_custom_call" | custom-call | flops 1 | bytes 1 | tf_op jit(solution)/shard_map/pallas_call | solution.py:196
  153.1 7.9 %collective-permute-done.25.came_ref = bf16[192,1536]{1,0:T(8,128)(2,1)S(1)} collective-permute-done((bf16[192,1536]{1,0:T(8,128)(2,1)S(1)}, bf16[192,1536]{1,0:T(8,128)(2,1)S(1)}, u32[]{:S(2)}, u32[]{:S(2)}) %collective-permute-start.25) | collective-permute-done | bytes 589856 | tf_op jit(solution)/shard_map/ppermute | solution.py:503
  161.0 2.1 %shard_map.138 = (bf16[192,1024]{1,0:T(8,128)(2,1)S(1)}, bf16[192,1024]{1,0:T(8,128)(2,1)S(1)}, bf16[192,1024]{1,0:T(8,128)(2,1)S(1)}, bf16[96,1920]{1,0:T(8,128)(2,1)S(1)}, bf16[96,1920]{1,0:T(8,128)(2,1)S(1)}) custom-call(s32[2]{0:T(128)S(1)} %pad_add_fusion.scalars.middle_ref, ...), custom_call_target="tpu_custom_call", output_to_operand_aliasing={{0}: (9, {}), {1}: (10, {}), {2}: (11, {})} | custom-call | flops 1 | bytes 1 | tf_op jit(solution)/shard_map/pallas_call | solution.py:196
  163.2 1.6 collective-permute-start.27
  164.9 3.3 %convolution_convert_fusion.7.before_ref = bf16[1024,1792]{1,0:T(8,128)(2,1)S(1)} fusion(bf16[576,1024]{1,0:T(8,128)(2,1)S(1)} %pad_maximum_fusion, bf16[192,1792]{1,0:T(8,128)(2,1)S(1)} %copy-done.18, bf16[192,1792]{1,0:T(8,128)(2,1)S(1)} %copy-done.16, bf16[192,1792]{1,0:T(8,128)(2,1)S(1)} %copy-done.14), kind=kOutput, calls=%fused_computation.7 | convolution fusion | flops 2121957376 | bytes 6914048 | tf_op jit(solution)/shard_map/dot_general | solution.py:374
  168.4 1.3 collective-permute-start.29
  171.5 3.3 %convolution_convert_fusion.6.before_ref = bf16[1792,1024]{1,0:T(8,128)(2,1)S(1)} fusion(bf16[576,1792]{1,0:T(8,128)(2,1)S(1)} %copy-done.21, bf16[192,1024]{1,0:T(8,128)(2,1)S(1)} %get-tuple-element.237, bf16[192,1024]{1,0:T(8,128)(2,1)S(1)} %get-tuple-element.236, bf16[192,1024]{1,0:T(8,128)(2,1)S(1)} %copy-done.10), kind=kOutput, calls=%fused_computation.6 | convolution fusion | flops 2119303168 | bytes 6914048 | tf_op jit(solution)/shard_map/dot_general | solution.py:374
  174.9 3.3 %convolution_convert_fusion.5.before_ref = bf16[1792,1024]{1,0:T(8,128)(2,1)S(1)} fusion(bf16[576,1792]{1,0:T(8,128)(2,1)S(1)} %copy-done.21, bf16[192,1024]{1,0:T(8,128)(2,1)S(1)} %get-tuple-element.241, bf16[192,1024]{1,0:T(8,128)(2,1)S(1)} %get-tuple-element.240, bf16[192,1024]{1,0:T(8,128)(2,1)S(1)} %copy-done.12), kind=kOutput, calls=%fused_computation.5 | convolution fusion | flops 2119303168 | bytes 6914048 | tf_op jit(solution)/shard_map/dot_general | solution.py:374
  178.2 2.1 %shard_map.140 = (bf16[192,1024]{1,0:T(8,128)(2,1)S(1)}, bf16[192,1024]{1,0:T(8,128)(2,1)S(1)}, bf16[192,1024]{1,0:T(8,128)(2,1)S(1)}, f32[192,1792]{1,0:T(8,128)S(1)}, f32[192,128]{1,0:T(8,128)S(1)}) custom-call(s32[2]{0:T(128)S(1)} %pad_add_fusion.scalars.middle_ref, bf16[192,1536]{1,0:T(8,128)(2,1)S(1)} %shard_map.136.own_ref, ...), custom_call_target="tpu_custom_call" | custom-call | flops 1 | bytes 1 | tf_op jit(solution)/shard_map/pallas_call | solution.py:196
  180.3 5.5 %collective-permute-done.29.came_ref = bf16[192,1536]{1,0:T(8,128)(2,1)S(1)} collective-permute-done((bf16[192,1536]{1,0:T(8,128)(2,1)S(1)}, bf16[192,1536]{1,0:T(8,128)(2,1)S(1)}, u32[]{:S(2)}, u32[]{:S(2)}) %collective-permute-start.29) | collective-permute-done | bytes 589856 | tf_op jit(solution)/shard_map/ppermute | solution.py:503
  185.8 2.1 %shard_map.141 = (bf16[192,1024]{1,0:T(8,128)(2,1)S(1)}, bf16[192,1024]{1,0:T(8,128)(2,1)S(1)}, bf16[192,1024]{1,0:T(8,128)(2,1)S(1)}, bf16[96,1920]{1,0:T(8,128)(2,1)S(1)}, bf16[96,1920]{1,0:T(8,128)(2,1)S(1)}) custom-call(s32[2]{0:T(128)S(1)} %pad_add_fusion.scalars.middle_ref, ...), custom_call_target="tpu_custom_call", output_to_operand_aliasing={{0}: (9, {}), {1}: (10, {}), {2}: (11, {})} | custom-call | flops 1 | bytes 1 | tf_op jit(solution)/shard_map/pallas_call | solution.py:196
  188.0 1.6 collective-permute-start.31
  190.2 3.3 %shard_map.142 = bf16[1024,1792]{1,0:T(8,128)(2,1)} custom-call(bf16[192,1024]{1,0:T(8,128)(2,1)S(1)} %get-tuple-element.257.left_ref, bf16[192,1792]{1,0:T(8,128)(2,1)S(1)} %get-tuple-element.258.right_ref, bf16[1024,1792]{1,0:T(8,128)(2,1)S(1)} %convolution_convert_fusion.7.before_ref), custom_call_target="tpu_custom_call" | custom-call | flops 1 | bytes 1 | tf_op jit(solution)/shard_map/pallas_call | solution.py:219
  193.4 4.5 %shard_map.143 = bf16[1792,1024]{1,0:T(8,128)(2,1)} custom-call(bf16[192,1792]{1,0:T(8,128)(2,1)S(1)} %get-tuple-element.261.left_ref, bf16[192,1024]{1,0:T(8,128)(2,1)S(1)} %get-tuple-element.260.right_ref, bf16[1792,1024]{1,0:T(8,128)(2,1)S(1)} %convolution_convert_fusion.6.before_ref), custom_call_target="tpu_custom_call" | custom-call | flops 1 | bytes 1 | tf_op jit(solution)/shard_map/pallas_call | solution.py:219
  198.0 4.5 %shard_map.144 = bf16[1792,1024]{1,0:T(8,128)(2,1)} custom-call(bf16[192,1792]{1,0:T(8,128)(2,1)S(1)} %get-tuple-element.261.left_ref, bf16[192,1024]{1,0:T(8,128)(2,1)S(1)} %get-tuple-element.262.right_ref, bf16[1792,1024]{1,0:T(8,128)(2,1)S(1)} %convolution_convert_fusion.5.before_ref), custom_call_target="tpu_custom_call" | custom-call | flops 1 | bytes 1 | tf_op jit(solution)/shard_map/pallas_call | solution.py:219
  202.6 2.4 %collective-permute-done.32 = bf16[96,1920]{1,0:T(8,128)(2,1)S(1)} collective-permute-done((bf16[96,1920]{1,0:T(8,128)(2,1)S(1)}, bf16[96,1920]{1,0:T(8,128)(2,1)S(1)}, u32[]{:S(2)}, u32[]{:S(2)}) %collective-permute-start.32) | collective-permute-done | bytes 368672 | tf_op jit(solution)/shard_map/ppermute | solution.py:463
  206.2 1.2 fusion.1
  (163 shorter events, 22.3 us)
Async XLA Ops:
  4.1 3.1 %copy-start.30 = (bf16[192,3]{1,0:T(8,128)(2,1)}, bf16[192,3]{1,0:T(8,128)(2,1)S(1)}, u32[]{:S(2)}) copy-start(bf16[192,3]{1,0:T(8,128)(2,1)S(1)} %copy.32) | copy-start | bytes 3460
  4.1 3.1 %copy-start.33 = (bf16[192,1792]{1,0:T(8,128)(2,1)S(1)}, bf16[192,1792]{1,0:T(8,128)(2,1)}, u32[]{:S(2)}) copy-start(bf16[192,1792]{1,0:T(8,128)(2,1)} %param.8) | copy-start | bytes 2064388
  4.1 3.1 %copy-start.35 = (bf16[192,1792]{1,0:T(8,128)(2,1)S(1)}, bf16[192,1792]{1,0:T(8,128)(2,1)}, u32[]{:S(2)}) copy-start(bf16[192,1792]{1,0:T(8,128)(2,1)} %param.7) | copy-start | bytes 2064388
  8.9 35.9 %collective-permute-start.2 = (bf16[192,3712]{1,0:T(8,128)(2,1)}, bf16[192,3712]{1,0:T(8,128)(2,1)S(1)}, u32[]{:S(2)}, u32[]{:S(2)}) collective-permute-start(bf16[192,3712]{1,0:T(8,128)(2,1)} %convolution_convert_fusion.1), channel_id=1, source_target_pairs={{0,4},{1,5},{2,6},{3,7},{4,0},{5,1},{6,2},{7,3},{8,12},{9,13},{10,... | collective-permute-start | bytes 4276232 | tf_op jit(solution)/shard_map/ppermute | solution.py:415
  11.8 32.9 %collective-permute-start.3 = (bf16[192,3712]{1,0:T(8,128)(2,1)}, bf16[192,3712]{1,0:T(8,128)(2,1)S(1)}, u32[]{:S(2)}, u32[]{:S(2)}) collective-permute-start(bf16[192,3712]{1,0:T(8,128)(2,1)} %convolution_convert_fusion.2), channel_id=1, source_target_pairs={{0,2},{1,3},{2,0},{3,1},{4,6},{5,7},{6,4},{7,5},{8,10},{9,11},{10,... | collective-permute-start | bytes 4276232 | tf_op jit(solution)/shard_map/ppermute | solution.py:415
  14.0 2.1 %copy-start.26 = (bf16[96,192]{1,0:T(8,128)(2,1)}, bf16[96,192]{1,0:T(8,128)(2,1)S(1)}, u32[]{:S(2)}) copy-start(bf16[96,192]{1,0:T(8,128)(2,1)S(1)} %get-tuple-element.135) | copy-start | bytes 110596
  14.0 2.2 %copy-start.28 = (bf16[96,192]{1,0:T(8,128)(2,1)}, bf16[96,192]{1,0:T(8,128)(2,1)S(1)}, u32[]{:S(2)}) copy-start(bf16[96,192]{1,0:T(8,128)(2,1)S(1)} %get-tuple-element.136) | copy-start | bytes 110596
  14.0 2.2 %copy-start.31 = (bf16[192,3]{1,0:T(8,128)(2,1)S(1)}, bf16[192,3]{1,0:T(8,128)(2,1)}, u32[]{:S(2)}) copy-start(bf16[192,3]{1,0:T(8,128)(2,1)} %copy-done.30) | copy-start | bytes 3460
  16.1 2.5 %collective-permute-start = (bf16[96,3712]{1,0:T(8,128)(2,1)}, bf16[96,3712]{1,0:T(8,128)(2,1)}, u32[]{:S(2)}, u32[]{:S(2)}) collective-permute-start(bf16[96,3712]{1,0:T(8,128)(2,1)} %convolution_convert_fusion.4), channel_id=1, source_target_pairs={{0,1},{1,0},{2,3},{3,2},{4,5},{5,4},{6,7},{7,6},{8,9},{9,8},{10,11... | collective-permute-start | bytes 2138120 | tf_op jit(solution)/shard_map/ppermute | solution.py:290
  16.2 2.5 %copy-start = (bf16[1,1792,1024]{2,1,0:T(8,128)(2,1)S(1)}, bf16[1,1792,1024]{2,1,0:T(8,128)(2,1)}, u32[]{:S(2)}) copy-start(bf16[1,1792,1024]{2,1,0:T(8,128)(2,1)} %refs_2_.31) | copy-start | bytes 11010052
  18.6 2.0 copy-start.1
  20.7 2.0 copy-start.3
  26.7 6.8 %copy-start.34 = (bf16[192,1792]{1,0:T(8,128)(2,1)S(1)}, bf16[192,1792]{1,0:T(8,128)(2,1)}, u32[]{:S(2)}) copy-start(bf16[192,1792]{1,0:T(8,128)(2,1)} %param.8) | copy-start | bytes 2064388
  26.7 6.8 %copy-start.36 = (bf16[192,1792]{1,0:T(8,128)(2,1)S(1)}, bf16[192,1792]{1,0:T(8,128)(2,1)}, u32[]{:S(2)}) copy-start(bf16[192,1792]{1,0:T(8,128)(2,1)} %param.7) | copy-start | bytes 2064388
  26.7 16.9 %collective-permute-start.4 = (bf16[192,1536]{1,0:T(8,128)(2,1)S(1)}, bf16[192,1536]{1,0:T(8,128)(2,1)S(1)}, u32[]{:S(2)}, u32[]{:S(2)}) collective-permute-start(bf16[192,1536]{1,0:T(8,128)(2,1)S(1)} %get-tuple-element.140.a_ref), channel_id=1, source_target_pairs={{0,8},{24,16},{1,9},{25,17},{2,10},{26,18},{3,11},{27,19},{4,12},{... | collective-permute-start | bytes 1769480 | tf_op jit(solution)/shard_map/ppermute | solution.py:476
  34.0 13.1 %copy-start.2 = (bf16[1,1792,1024]{2,1,0:T(8,128)(2,1)S(1)}, bf16[1,1792,1024]{2,1,0:T(8,128)(2,1)}, u32[]{:S(2)}) copy-start(bf16[1,1792,1024]{2,1,0:T(8,128)(2,1)} %refs_3_.31) | copy-start | bytes 11010052
  44.9 2.2 %collective-permute-start.5 = (bf16[96,3712]{1,0:T(8,128)(2,1)S(1)}, bf16[96,3712]{1,0:T(8,128)(2,1)S(1)}, u32[]{:S(2)}, u32[]{:S(2)}) collective-permute-start(bf16[96,3712]{1,0:T(8,128)(2,1)S(1)} %slice.114), channel_id=1, source_target_pairs={{0,1},{1,0},{2,3},{3,2},{4,5},{5,4},{6,7},{7,6},{8,9},{9,8},{10,11... | collective-permute-start | bytes 2138120 | tf_op jit(solution)/shard_map/ppermute | solution.py:427
  50.5 42.9 %collective-permute-start.14 = (bf16[192,3712]{1,0:T(8,128)(2,1)S(1)}, bf16[192,3712]{1,0:T(8,128)(2,1)S(1)}, u32[]{:S(2)}, u32[]{:S(2)}) collective-permute-start(bf16[192,3712]{1,0:T(8,128)(2,1)S(1)} %convolution_convert_fusion), channel_id=1, source_target_pairs={{0,6},{1,7},{2,4},{3,5},{4,2},{5,3},{6,0},{7,1},{8,14},{9,15},{10,... | collective-permute-start | bytes 4276232 | tf_op jit(solution)/shard_map/ppermute | solution.py:415
  51.9 17.2 %collective-permute-start.1 = (bf16[192,1536]{1,0:T(8,128)(2,1)S(1)}, bf16[192,1536]{1,0:T(8,128)(2,1)S(1)}, u32[]{:S(2)}, u32[]{:S(2)}) collective-permute-start(bf16[192,1536]{1,0:T(8,128)(2,1)S(1)} %shard_map.111.a_ref), channel_id=1, source_target_pairs={{0,8},{24,16},{1,9},{25,17},{2,10},{26,18},{3,11},{27,19},{4,12},{... | collective-permute-start | bytes 1769480 | tf_op jit(solution)/shard_map/ppermute | solution.py:478
  55.4 17.1 %collective-permute-start.8 = (bf16[192,1536]{1,0:T(8,128)(2,1)S(1)}, bf16[192,1536]{1,0:T(8,128)(2,1)S(1)}, u32[]{:S(2)}, u32[]{:S(2)}) collective-permute-start(bf16[192,1536]{1,0:T(8,128)(2,1)S(1)} %shard_map.112.a_ref), channel_id=1, source_target_pairs={{8,16},{16,8},{9,17},{17,9},{10,18},{18,10},{11,19},{19,11},{12,20... | collective-permute-start | bytes 1769480 | tf_op jit(solution)/shard_map/ppermute | solution.py:484
  56.1 25.6 %collective-permute-start.7 = (bf16[192,1536]{1,0:T(8,128)(2,1)S(1)}, bf16[192,1536]{1,0:T(8,128)(2,1)S(1)}, u32[]{:S(2)}, u32[]{:S(2)}) collective-permute-start(bf16[192,1536]{1,0:T(8,128)(2,1)S(1)} %get-tuple-element.152.a_ref), channel_id=1, source_target_pairs={{0,8},{24,16},{1,9},{25,17},{2,10},{26,18},{3,11},{27,19},{4,12},{... | collective-permute-start | bytes 1769480 | tf_op jit(solution)/shard_map/ppermute | solution.py:492
  69.2 13.3 %collective-permute-start.9 = (bf16[96,3712]{1,0:T(8,128)(2,1)S(1)}, bf16[96,3712]{1,0:T(8,128)(2,1)S(1)}, u32[]{:S(2)}, u32[]{:S(2)}) collective-permute-start(bf16[96,3712]{1,0:T(8,128)(2,1)S(1)} %slice.115), channel_id=1, source_target_pairs={{0,1},{1,0},{2,3},{3,2},{4,5},{5,4},{6,7},{7,6},{8,9},{9,8},{10,11... | collective-permute-start | bytes 2138120 | tf_op jit(solution)/shard_map/ppermute | solution.py:427
  69.3 15.8 %collective-permute-start.6 = (bf16[192,1536]{1,0:T(8,128)(2,1)S(1)}, bf16[192,1536]{1,0:T(8,128)(2,1)S(1)}, u32[]{:S(2)}, u32[]{:S(2)}) collective-permute-start(bf16[192,1536]{1,0:T(8,128)(2,1)S(1)} %shard_map.114.a_ref), channel_id=1, source_target_pairs={{8,16},{16,8},{9,17},{17,9},{10,18},{18,10},{11,19},{19,11},{12,20... | collective-permute-start | bytes 1769480 | tf_op jit(solution)/shard_map/ppermute | solution.py:484
  73.4 19.9 %collective-permute-start.11 = (bf16[192,1536]{1,0:T(8,128)(2,1)S(1)}, bf16[192,1536]{1,0:T(8,128)(2,1)S(1)}, u32[]{:S(2)}, u32[]{:S(2)}) collective-permute-start(bf16[192,1536]{1,0:T(8,128)(2,1)S(1)} %get-tuple-element.156), channel_id=1, source_target_pairs={{0,8},{24,16},{8,0},{16,24},{1,9},{25,17},{9,1},{17,25},{2,10},{26... | collective-permute-start | bytes 1769480 | tf_op jit(solution)/shard_map/ppermute | solution.py:499
  81.9 17.6 %collective-permute-start.13 = (bf16[192,1536]{1,0:T(8,128)(2,1)S(1)}, bf16[192,1536]{1,0:T(8,128)(2,1)S(1)}, u32[]{:S(2)}, u32[]{:S(2)}) collective-permute-start(bf16[192,1536]{1,0:T(8,128)(2,1)S(1)} %shard_map.117.a_ref), channel_id=1, source_target_pairs={{8,16},{16,8},{9,17},{17,9},{10,18},{18,10},{11,19},{19,11},{12,20... | collective-permute-start | bytes 1769480 | tf_op jit(solution)/shard_map/ppermute | solution.py:484
  85.1 8.3 %copy-start.17 = (bf16[192,1792]{1,0:T(8,128)(2,1)}, bf16[192,1792]{1,0:T(8,128)(2,1)S(1)}, u32[]{:S(2)}) copy-start(bf16[192,1792]{1,0:T(8,128)(2,1)S(1)} %get-tuple-element.226) | copy-start | bytes 2064388
  93.5 17.7 %collective-permute-start.15 = (bf16[96,3712]{1,0:T(8,128)(2,1)S(1)}, bf16[96,3712]{1,0:T(8,128)(2,1)S(1)}, u32[]{:S(2)}, u32[]{:S(2)}) collective-permute-start(bf16[96,3712]{1,0:T(8,128)(2,1)S(1)} %slice.116), channel_id=1, source_target_pairs={{0,1},{1,0},{2,3},{3,2},{4,5},{5,4},{6,7},{7,6},{8,9},{9,8},{10,11... | collective-permute-start | bytes 2138120 | tf_op jit(solution)/shard_map/ppermute | solution.py:427
  93.5 16.7 %collective-permute-start.10 = (bf16[192,1536]{1,0:T(8,128)(2,1)S(1)}, bf16[192,1536]{1,0:T(8,128)(2,1)S(1)}, u32[]{:S(2)}, u32[]{:S(2)}) collective-permute-start(bf16[192,1536]{1,0:T(8,128)(2,1)S(1)} %get-tuple-element.165), channel_id=1, source_target_pairs={{0,8},{24,16},{8,0},{16,24},{1,9},{25,17},{9,1},{17,25},{2,10},{26... | collective-permute-start | bytes 1769480 | tf_op jit(solution)/shard_map/ppermute | solution.py:499
  96.1 17.6 %collective-permute-start.12 = (bf16[192,1536]{1,0:T(8,128)(2,1)S(1)}, bf16[192,1536]{1,0:T(8,128)(2,1)S(1)}, u32[]{:S(2)}, u32[]{:S(2)}) collective-permute-start(bf16[192,1536]{1,0:T(8,128)(2,1)S(1)} %shard_map.120.a_ref), channel_id=1, source_target_pairs={{8,16},{16,8},{9,17},{17,9},{10,18},{18,10},{11,19},{19,11},{12,20... | collective-permute-start | bytes 1769480 | tf_op jit(solution)/shard_map/ppermute | solution.py:484
  101.1 25.4 %collective-permute-start.18 = (bf16[192,1536]{1,0:T(8,128)(2,1)}, bf16[192,1536]{1,0:T(8,128)(2,1)S(1)}, u32[]{:S(2)}, u32[]{:S(2)}) collective-permute-start(bf16[192,1536]{1,0:T(8,128)(2,1)} %get-tuple-element.172), channel_id=1, source_target_pairs={{0,8},{24,16},{8,0},{16,24},{1,9},{25,17},{9,1},{17,25},{2,10},{26... | collective-permute-start | bytes 1769480 | tf_op jit(solution)/shard_map/ppermute | solution.py:499
  104.1 7.1 %copy-start.4 = (bf16[1,1024,1792]{2,1,0:T(8,128)(2,1)S(1)}, bf16[1,1024,1792]{2,1,0:T(8,128)(2,1)}, u32[]{:S(2)}) copy-start(bf16[1,1024,1792]{2,1,0:T(8,128)(2,1)} %refs_4_.15) | copy-start | bytes 11010052
  106.5 4.6 %copy-start.7 = (bf16[192,1024]{1,0:T(8,128)(2,1)}, bf16[192,1024]{1,0:T(8,128)(2,1)S(1)}, u32[]{:S(2)}) copy-start(bf16[192,1024]{1,0:T(8,128)(2,1)S(1)} %get-tuple-element.186.refs_7_) | copy-start | bytes 1179652
  110.4 20.4 %collective-permute-start.20 = (bf16[192,1536]{1,0:T(8,128)(2,1)S(1)}, bf16[192,1536]{1,0:T(8,128)(2,1)S(1)}, u32[]{:S(2)}, u32[]{:S(2)}) collective-permute-start(bf16[192,1536]{1,0:T(8,128)(2,1)S(1)} %shard_map.124.a_ref), channel_id=1, source_target_pairs={{8,16},{16,8},{9,17},{17,9},{10,18},{18,10},{11,19},{19,11},{12,20... | collective-permute-start | bytes 1769480 | tf_op jit(solution)/shard_map/ppermute | solution.py:484
  111.1 10.8 %copy-start.8 = (bf16[192,1024]{1,0:T(8,128)(2,1)S(1)}, bf16[192,1024]{1,0:T(8,128)(2,1)}, u32[]{:S(2)}) copy-start(bf16[192,1024]{1,0:T(8,128)(2,1)} %copy-done.7) | copy-start | bytes 1179652
  114.5 1.1 copy-start.6
  117.2 18.6 %collective-permute-start.17 = (bf16[192,1536]{1,0:T(8,128)(2,1)}, bf16[192,1536]{1,0:T(8,128)(2,1)S(1)}, u32[]{:S(2)}, u32[]{:S(2)}) collective-permute-start(bf16[192,1536]{1,0:T(8,128)(2,1)} %get-tuple-element.182), channel_id=1, source_target_pairs={{0,8},{24,16},{8,0},{16,24},{1,9},{25,17},{9,1},{17,25},{2,10},{26... | collective-permute-start | bytes 1769480 | tf_op jit(solution)/shard_map/ppermute | solution.py:499
  126.6 10.1 %collective-permute-start.19 = (bf16[192,1536]{1,0:T(8,128)(2,1)S(1)}, bf16[192,1536]{1,0:T(8,128)(2,1)S(1)}, u32[]{:S(2)}, u32[]{:S(2)}) collective-permute-start(bf16[192,1536]{1,0:T(8,128)(2,1)S(1)} %shard_map.128.a_ref), channel_id=1, source_target_pairs={{8,16},{16,8},{9,17},{17,9},{10,18},{18,10},{11,19},{19,11},{12,20... | collective-permute-start | bytes 1769480 | tf_op jit(solution)/shard_map/ppermute | solution.py:484
  128.2 12.9 %collective-permute-start.16 = (bf16[96,1920]{1,0:T(8,128)(2,1)}, bf16[96,1920]{1,0:T(8,128)(2,1)S(1)}, u32[]{:S(2)}, u32[]{:S(2)}) collective-permute-start(bf16[96,1920]{1,0:T(8,128)(2,1)} %get-tuple-element.189), channel_id=1, source_target_pairs={{0,1},{1,0},{2,3},{3,2},{4,5},{5,4},{6,7},{7,6},{8,9},{9,8},{10,11... | collective-permute-start | bytes 1105928 | tf_op jit(solution)/shard_map/ppermute | solution.py:463
  131.6 16.8 %collective-permute-start.23 = (bf16[192,1536]{1,0:T(8,128)(2,1)S(1)}, bf16[192,1536]{1,0:T(8,128)(2,1)S(1)}, u32[]{:S(2)}, u32[]{:S(2)}) collective-permute-start(bf16[192,1536]{1,0:T(8,128)(2,1)S(1)} %get-tuple-element.195), channel_id=1, source_target_pairs={{0,8},{24,16},{8,0},{16,24},{1,9},{25,17},{9,1},{17,25},{2,10},{26... | collective-permute-start | bytes 1769480 | tf_op jit(solution)/shard_map/ppermute | solution.py:499
  135.4 2.8 %copy-start.19 = (bf16[576,1792]{1,0:T(8,128)(2,1)S(1)}, bf16[576,1792]{1,0:T(8,128)(2,1)}, u32[]{:S(2)}) copy-start(bf16[576,1792]{1,0:T(8,128)(2,1)} %constant_dynamic-update-slice_fusion.2) | copy-start | bytes 6193156
  135.9 13.5 %collective-permute-start.26 = (bf16[192,1536]{1,0:T(8,128)(2,1)S(1)}, bf16[192,1536]{1,0:T(8,128)(2,1)S(1)}, u32[]{:S(2)}, u32[]{:S(2)}) collective-permute-start(bf16[192,1536]{1,0:T(8,128)(2,1)S(1)} %shard_map.132.a_ref), channel_id=1, source_target_pairs={{8,16},{16,8},{9,17},{17,9},{10,18},{18,10},{11,19},{19,11},{12,20... | collective-permute-start | bytes 1769480 | tf_op jit(solution)/shard_map/ppermute | solution.py:484
  136.9 24.1 %collective-permute-start.25 = (bf16[192,1536]{1,0:T(8,128)(2,1)S(1)}, bf16[192,1536]{1,0:T(8,128)(2,1)S(1)}, u32[]{:S(2)}, u32[]{:S(2)}) collective-permute-start(bf16[192,1536]{1,0:T(8,128)(2,1)S(1)} %shard_map.133.own_ref), channel_id=1, source_target_pairs={{8,0},{16,24},{9,1},{17,25},{10,2},{18,26},{11,3},{19,27},{12,4},{... | collective-permute-start | bytes 1769480 | tf_op jit(solution)/shard_map/ppermute | solution.py:503
  138.3 2.2 %copy-start.20 = (bf16[576,1792]{1,0:T(8,128)(2,1)}, bf16[576,1792]{1,0:T(8,128)(2,1)S(1)}, u32[]{:S(2)}) copy-start(bf16[576,1792]{1,0:T(8,128)(2,1)S(1)} %constant_dynamic-update-slice_fusion) | copy-start | bytes 6193156
  138.3 3.6 %copy-start.27 = (bf16[96,192]{1,0:T(8,128)(2,1)S(1)}, bf16[96,192]{1,0:T(8,128)(2,1)}, u32[]{:S(2)}) copy-start(bf16[96,192]{1,0:T(8,128)(2,1)} %copy-done.26) | copy-start | bytes 110596
  138.3 3.6 %copy-start.29 = (bf16[96,192]{1,0:T(8,128)(2,1)S(1)}, bf16[96,192]{1,0:T(8,128)(2,1)}, u32[]{:S(2)}) copy-start(bf16[96,192]{1,0:T(8,128)(2,1)} %copy-done.28) | copy-start | bytes 110596
  140.5 29.3 %collective-permute-start.21 = (bf16[96,1920]{1,0:T(8,128)(2,1)S(1)}, bf16[96,1920]{1,0:T(8,128)(2,1)S(1)}, u32[]{:S(2)}, u32[]{:S(2)}) collective-permute-start(bf16[96,1920]{1,0:T(8,128)(2,1)S(1)} %get-tuple-element.205), channel_id=1, source_target_pairs={{0,2},{1,3},{2,0},{3,1},{4,6},{5,7},{6,4},{7,5},{8,10},{9,11},{10,... | collective-permute-start | bytes 1105928 | tf_op jit(solution)/shard_map/ppermute | solution.py:463
  141.2 28.6 %collective-permute-start.22 = (bf16[96,1920]{1,0:T(8,128)(2,1)S(1)}, bf16[96,1920]{1,0:T(8,128)(2,1)S(1)}, u32[]{:S(2)}, u32[]{:S(2)}) collective-permute-start(bf16[96,1920]{1,0:T(8,128)(2,1)S(1)} %get-tuple-element.208), channel_id=1, source_target_pairs={{0,3},{1,2},{2,1},{3,0},{4,7},{5,6},{6,5},{7,4},{8,11},{9,10},{10,... | collective-permute-start | bytes 1105928 | tf_op jit(solution)/shard_map/ppermute | solution.py:463
  148.5 19.7 %collective-permute-start.24 = (bf16[192,1536]{1,0:T(8,128)(2,1)S(1)}, bf16[192,1536]{1,0:T(8,128)(2,1)S(1)}, u32[]{:S(2)}, u32[]{:S(2)}) collective-permute-start(bf16[192,1536]{1,0:T(8,128)(2,1)S(1)} %shard_map.135.a_ref), channel_id=1, source_target_pairs={{8,16},{16,8},{9,17},{17,9},{10,18},{18,10},{11,19},{19,11},{12,20... | collective-permute-start | bytes 1769480 | tf_op jit(solution)/shard_map/ppermute | solution.py:484
  149.5 28.7 %collective-permute-start.30 = (bf16[192,1536]{1,0:T(8,128)(2,1)S(1)}, bf16[192,1536]{1,0:T(8,128)(2,1)S(1)}, u32[]{:S(2)}, u32[]{:S(2)}) collective-permute-start(bf16[192,1536]{1,0:T(8,128)(2,1)S(1)} %shard_map.136.own_ref), channel_id=1, source_target_pairs={{8,0},{16,24},{9,1},{17,25},{10,2},{18,26},{11,3},{19,27},{12,4},{... | collective-permute-start | bytes 1769480 | tf_op jit(solution)/shard_map/ppermute | solution.py:503
  163.2 1.7 copy-start.14
  163.2 1.7 copy-start.16
  163.2 1.7 copy-start.18
  163.2 26.3 %collective-permute-start.27 = (bf16[96,1920]{1,0:T(8,128)(2,1)S(1)}, bf16[96,1920]{1,0:T(8,128)(2,1)S(1)}, u32[]{:S(2)}, u32[]{:S(2)}) collective-permute-start(bf16[96,1920]{1,0:T(8,128)(2,1)S(1)} %get-tuple-element.222), channel_id=1, source_target_pairs={{0,4},{1,5},{2,6},{3,7},{4,0},{5,1},{6,2},{7,3},{8,12},{9,13},{10,... | collective-permute-start | bytes 1105928 | tf_op jit(solution)/shard_map/ppermute | solution.py:463
  168.3 1.7 copy-start.22
  168.3 1.7 copy-start.23
  168.4 17.4 %collective-permute-start.29 = (bf16[192,1536]{1,0:T(8,128)(2,1)S(1)}, bf16[192,1536]{1,0:T(8,128)(2,1)S(1)}, u32[]{:S(2)}, u32[]{:S(2)}) collective-permute-start(bf16[192,1536]{1,0:T(8,128)(2,1)S(1)} %shard_map.139.own_ref), channel_id=1, source_target_pairs={{8,0},{16,24},{9,1},{17,25},{10,2},{18,26},{11,3},{19,27},{12,4},{... | collective-permute-start | bytes 1769480 | tf_op jit(solution)/shard_map/ppermute | solution.py:503
  169.8 1.7 copy-start.21
  169.8 19.7 %collective-permute-start.28 = (bf16[96,1920]{1,0:T(8,128)(2,1)S(1)}, bf16[96,1920]{1,0:T(8,128)(2,1)S(1)}, u32[]{:S(2)}, u32[]{:S(2)}) collective-permute-start(bf16[96,1920]{1,0:T(8,128)(2,1)S(1)} %get-tuple-element.230), channel_id=1, source_target_pairs={{0,5},{1,4},{2,7},{3,6},{4,1},{5,0},{6,3},{7,2},{8,13},{9,12},{10,... | collective-permute-start | bytes 1105928 | tf_op jit(solution)/shard_map/ppermute | solution.py:463
  171.5 3.4 %copy-start.12 = (bf16[192,1024]{1,0:T(8,128)(2,1)S(1)}, bf16[192,1024]{1,0:T(8,128)(2,1)}, u32[]{:S(2)}) copy-start(bf16[192,1024]{1,0:T(8,128)(2,1)} %copy-done.11) | copy-start | bytes 1179652
  188.0 14.6 %collective-permute-start.31 = (bf16[96,1920]{1,0:T(8,128)(2,1)S(1)}, bf16[96,1920]{1,0:T(8,128)(2,1)S(1)}, u32[]{:S(2)}, u32[]{:S(2)}) collective-permute-start(bf16[96,1920]{1,0:T(8,128)(2,1)S(1)} %get-tuple-element.249), channel_id=1, source_target_pairs={{0,6},{1,7},{2,4},{3,5},{4,2},{5,3},{6,0},{7,1},{8,14},{9,15},{10,... | collective-permute-start | bytes 1105928 | tf_op jit(solution)/shard_map/ppermute | solution.py:463
  189.6 15.4 %collective-permute-start.32 = (bf16[96,1920]{1,0:T(8,128)(2,1)S(1)}, bf16[96,1920]{1,0:T(8,128)(2,1)S(1)}, u32[]{:S(2)}, u32[]{:S(2)}) collective-permute-start(bf16[96,1920]{1,0:T(8,128)(2,1)S(1)} %get-tuple-element.252), channel_id=1, source_target_pairs={{0,7},{1,6},{2,5},{3,4},{4,3},{5,2},{6,1},{7,0},{8,15},{9,14},{10,... | collective-permute-start | bytes 1105928 | tf_op jit(solution)/shard_map/ppermute | solution.py:463
  198.0 7.5 %copy-start.32 = (s32[192,2]{0,1:T(2,128)S(1)}, s32[192,2]{0,1:T(2,128)}, u32[]{:S(2)}) copy-start(s32[192,2]{0,1:T(2,128)} %param.9) | copy-start | bytes 4612
  198.0 8.2 %copy-start.24 = (bf16[96,192]{1,0:T(8,128)(2,1)S(1)}, bf16[96,192]{1,0:T(8,128)(2,1)}, u32[]{:S(2)}) copy-start(bf16[96,192]{1,0:T(8,128)(2,1)} %get-tuple-element.263) | copy-start | bytes 110596
  198.0 8.2 %copy-start.25 = (bf16[96,192]{1,0:T(8,128)(2,1)S(1)}, bf16[96,192]{1,0:T(8,128)(2,1)}, u32[]{:S(2)}) copy-start(bf16[96,192]{1,0:T(8,128)(2,1)} %get-tuple-element.264) | copy-start | bytes 110596
  (6 other events, 5.0 us)

commit v2 on v1

--- a/solution.py
+++ b/solution.py
@@ -469,8 +469,8 @@
             5: [(finish, 1)],
             6: [(finish, 2)],
             7: [(finish, 3), (take_back, chunks[0])],
-            8: [(finish, 4), (finish, 5), (add_gradient, 0)],
-            9: [(take_back, chunks[1]), (add_gradient, 1), (add_gradient, 2)],
+            8: [(finish, 4), (finish, 5)],
+            9: [(take_back, chunks[1]), (add_gradient, 0), (add_gradient, 1), (add_gradient, 2)],
         }
         compute_part(0)
         arrived[0] = lax.ppermute(part[0], "dp", inward)

time: 209 us -> 199 us (0.952)
  waiting for transfers between devices: 58.6 us -> 36.7 us
  starting transfers between devices: 49.4 us -> 56.7 us
  local copies, waits for them, and re-layouts: 13.4 us -> 16.2 us
    ppermute x5, waiting for transfers between devices: 17.5 us -> 9.43 us  [body(): arrived[t + 1] = lax.ppermute(both, 'dp', inward + outward)]
    ppermute x5, starting transfers between devices: 17.3 us -> 24.5 us  [body(): arrived[t + 1] = lax.ppermute(both, 'dp', inward + outward)]
    ppermute x1, waiting for transfers between devices: 8.88 us -> 3.16 us  [body(): arrived[1] = lax.ppermute(part[1], 'dp', inward)]
    ppermute x3, waiting for transfers between devices: 13.4 us -> 10.2 us  [body(): spread_out[k] = lax.ppermute(total[k], 'dp', outward)]
    ppermute x7, waiting for transfers between devices: 2.44 us -> 0.02 us  [finish(): one = lax.ppermute(one, 'expert', [(i, i ^ r) for i in range(groups)])]
    ppermute x3, waiting for transfers between devices: 2.17 us -> 0.01 us  [hand_on(): lax.ppermute(other, 'expert', [(i, i ^ 1) for i in range(groups)])]
    slice x4, local copies, waits for them, and re-layouts: 0.43 us -> 2.59 us  [take_back(): route_cols[r] = one[:, width]]
    unnamed x77 -> x93, local copies, waits for them, and re-layouts: 11.6 us -> 12.2 us
  transfers between devices with their start and end apart: 33 -> 33, of which waited for: 13 -> 10; matrix products, arithmetic and copies ran while one was open for 9% -> 11% of each run, Pallas kernels for 27% -> 30%
where the time goes in v2:
time: 199 us; the launch traced here: 196 us
  Pallas kernels  58.3 us (29%)
  starting transfers between devices  56.7 us (28%)
  waiting for transfers between devices  36.7 us (18%)
  matrix products  22.7 us (11%)
  local copies, waits for them, and re-layouts  16.2 us (8%)
  other arithmetic  3.84 us (2%)
    ppermute x5, starting transfers between devices, body(): arrived[t + 1] = lax.ppermute(both, 'dp', inward + outward)  24.5 us
    pallas_call x8, Pallas kernels, forward_piece(): pl.pallas_call(functools.partial(forward_kernel, len(rows), width, per_ar...  21.3 us
    pallas_call x8, Pallas kernels, backward_piece(): pl.pallas_call(functools.partial(backward_kernel, len(rows), width, half...  17.5 us
    pallas_call x3, Pallas kernels, gradient_add(): pl.pallas_call(gradient_kernel, grid=(height // BLOCK,), in_specs=[pl.Blo...  12.3 us
    unnamed x93, local copies, waits for them, and re-layouts  12.2 us
    ppermute x3, waiting for transfers between devices, body(): spread_out[k] = lax.ppermute(total[k], 'dp', outward)  10.2 us
    dot_general x3, matrix products, add_gradient(): lax.dot_general(rows_left, rows_right, over_rows, preferred_element_type=...  9.89 us
    ppermute x1, waiting for transfers between devices, body(): arrived[0] = lax.ppermute(part[0], 'dp', inward)  9.5 us
  transfers between devices with their start and end apart: 33, of which 10 were waited for; matrix products, arithmetic and copies ran while one was open for 11% of the time, Pallas kernels for 30%

profile of v2, /device:TPU:0, one launch (start us, length us, event | category | flops | bytes accessed | tf_op | source)
XLA Modules:
  0.0 196.1 jit_solution(9458244797336143985)
XLA Ops:
  4.2 3.1 %convolution_convert_fusion.2 = bf16[192,3712]{1,0:T(8,128)(2,1)} fusion(pred[192,192]{1,0:T(32,128)(4,1)S(1)} %bitcast.60, bf16[192,3]{1,0:T(8,128)(2,1)S(1)} %copy.32, bf16[192,1792]{1,0:T(8,128)(2,1)} %param.8, bf16[192,1792]{1,0:T(8,128)(2,1)} %param.7), kind=kOutput, calls=%fused_computation.2 | convolution fusion | flops 280092672 | bytes 2839680 | tf_op jit(solution)/shard_map/dot_general | solution.py:408
  7.2 1.6 convolution_convert_fusion.1
  8.9 3.0 %collective-permute-start.2 = (bf16[192,3712]{1,0:T(8,128)(2,1)}, bf16[192,3712]{1,0:T(8,128)(2,1)S(1)}, u32[]{:S(2)}, u32[]{:S(2)}) collective-permute-start(bf16[192,3712]{1,0:T(8,128)(2,1)} %convolution_convert_fusion.1), channel_id=1, source_target_pairs={{0,4},{1,5},{2,6},{3,7},{4,0},{5,1},{6,2},{7,3},{8,12},{9,13},{10,... | collective-permute-start | bytes 4276232 | tf_op jit(solution)/shard_map/ppermute | solution.py:415
  11.9 1.5 collective-permute-start.3
  14.0 2.1 %convolution_convert_fusion.4 = bf16[96,3712]{1,0:T(8,128)(2,1)} fusion(bf16[96,192]{1,0:T(8,128)(2,1)S(1)} %get-tuple-element.135, bf16[192,3]{1,0:T(8,128)(2,1)} %copy-done.35, bf16[192,1792]{1,0:T(8,128)(2,1)S(1)} %copy-done.41, bf16[192,1792]{1,0:T(8,128)(2,1)S(1)} %copy-done.43), kind=kOutput, calls=%fused_computation.4 | convolution fusion | flops 142897152 | bytes 2126976 | tf_op jit(solution)/shard_map/dot_general | solution.py:287
  16.2 1.8 convolution_convert_fusion.3.refs_0_
  18.7 2.0 %copy-done.1 = bf16[1,1792,1024]{2,1,0:T(8,128)(2,1)S(1)} copy-done((bf16[1,1792,1024]{2,1,0:T(8,128)(2,1)S(1)}, bf16[1,1792,1024]{2,1,0:T(8,128)(2,1)}, u32[]{:S(2)}) %copy-start.1) | copy-done | bytes 3670040
  20.7 2.0 %copy-done.3 = bf16[1,1024,1792]{2,1,0:T(8,128)(2,1)S(1)} copy-done((bf16[1,1024,1792]{2,1,0:T(8,128)(2,1)S(1)}, bf16[1,1024,1792]{2,1,0:T(8,128)(2,1)}, u32[]{:S(2)}) %copy-start.3) | copy-done | bytes 3670040
  22.8 3.1 %shard_map.110 = (bf16[192,1536]{1,0:T(8,128)(2,1)S(1)}, bf16[192,1792]{1,0:T(8,128)(2,1)S(1)}, bf16[192,1792]{1,0:T(8,128)(2,1)S(1)}) custom-call(s32[2]{0:T(128)S(1)} %pad_add_fusion.scalars.middle_ref, bf16[96,3712]{1,0:T(8,128)(2,1)S(1)} %convolution_convert_fusion.3.refs_0_, bf16[96,3712]{1,0:T(8,128)(2,1)} %collective-permute-done.refs_1_, ...), custom_call_target="tpu_custom_call" | custom-call | flops 1 | bytes 1 | tf_op jit(solution)/shard_map/pallas_call | solution.py:84
  25.9 0.9 copy-done.13
  26.7 3.6 %collective-permute-start.4 = (bf16[192,1536]{1,0:T(8,128)(2,1)S(1)}, bf16[192,1536]{1,0:T(8,128)(2,1)S(1)}, u32[]{:S(2)}, u32[]{:S(2)}) collective-permute-start(bf16[192,1536]{1,0:T(8,128)(2,1)S(1)} %get-tuple-element.140.a_ref), channel_id=1, source_target_pairs={{0,8},{24,16},{1,9},{25,17},{2,10},{26,18},{3,11},{27,19},{4,12},{... | collective-permute-start | bytes 1769480 | tf_op jit(solution)/shard_map/ppermute | solution.py:476
  30.4 3.1 %shard_map.111.a_ref = bf16[192,1536]{1,0:T(8,128)(2,1)S(1)} custom-call(s32[2]{0:T(128)S(1)} %pad_add_fusion.scalars.middle_ref, bf16[96,3712]{1,0:T(8,128)(2,1)S(1)} %convolution_convert_fusion.3.refs_0_, bf16[96,3712]{1,0:T(8,128)(2,1)} %collective-permute-done.refs_1_, bf16[1,1792,1024]{2,1,0:T(8,128)(2,1)S(1)} %copy-done, ...), custom_call_target="tpu_custom_call" | custom-call | flops 1 | bytes 1 | tf_op jit(solution)/shard_map/pallas_call | solution.py:84
  34.1 9.5 %collective-permute-done.4.b_ref = bf16[192,1536]{1,0:T(8,128)(2,1)S(1)} collective-permute-done((bf16[192,1536]{1,0:T(8,128)(2,1)S(1)}, bf16[192,1536]{1,0:T(8,128)(2,1)S(1)}, u32[]{:S(2)}, u32[]{:S(2)}) %collective-permute-start.4) | collective-permute-done | bytes 589856 | tf_op jit(solution)/shard_map/ppermute | solution.py:476
  43.7 1.1 collective-permute-done.3.refs_0_
  45.0 3.5 %collective-permute-start.1 = (bf16[192,1536]{1,0:T(8,128)(2,1)S(1)}, bf16[192,1536]{1,0:T(8,128)(2,1)S(1)}, u32[]{:S(2)}, u32[]{:S(2)}) collective-permute-start(bf16[192,1536]{1,0:T(8,128)(2,1)S(1)} %shard_map.111.a_ref), channel_id=1, source_target_pairs={{0,8},{24,16},{1,9},{25,17},{2,10},{26,18},{3,11},{27,19},{4,12},{... | collective-permute-start | bytes 1769480 | tf_op jit(solution)/shard_map/ppermute | solution.py:478
  48.5 2.5 %shard_map.113 = (bf16[192,1536]{1,0:T(8,128)(2,1)S(1)}, bf16[192,1792]{1,0:T(8,128)(2,1)S(1)}, bf16[192,1792]{1,0:T(8,128)(2,1)S(1)}) custom-call(s32[2]{0:T(128)S(1)} %pad_add_fusion.scalars.middle_ref, bf16[192,3712]{1,0:T(8,128)(2,1)S(1)} %collective-permute-done.3.refs_0_, bf16[96,3712]{1,0:T(8,128)(2,1)S(1)} %collective-permute-done.5.refs_1_, ...), custom_call_target="tpu_custom_call" | custom-call | flops 1 | bytes 1 | tf_op jit(solution)/shard_map/pallas_call | solution.py:84
  51.0 0.8 copy-done.15
  51.9 1.4 collective-permute-start.14
  54.0 4.9 %collective-permute-start.7 = (bf16[192,1536]{1,0:T(8,128)(2,1)S(1)}, bf16[192,1536]{1,0:T(8,128)(2,1)S(1)}, u32[]{:S(2)}, u32[]{:S(2)}) collective-permute-start(bf16[192,1536]{1,0:T(8,128)(2,1)S(1)} %get-tuple-element.152.a_ref), channel_id=1, source_target_pairs={{0,8},{24,16},{1,9},{25,17},{2,10},{26,18},{3,11},{27,19},{4,12},{... | collective-permute-start | bytes 1769480 | tf_op jit(solution)/shard_map/ppermute | solution.py:492
  58.9 3.2 %collective-permute-done.1.b_ref = bf16[192,1536]{1,0:T(8,128)(2,1)S(1)} collective-permute-done((bf16[192,1536]{1,0:T(8,128)(2,1)S(1)}, bf16[192,1536]{1,0:T(8,128)(2,1)S(1)}, u32[]{:S(2)}, u32[]{:S(2)}) %collective-permute-start.1) | collective-permute-done | bytes 589856 | tf_op jit(solution)/shard_map/ppermute | solution.py:478
  63.0 2.5 %shard_map.115.other_ref.a_ref = bf16[192,1536]{1,0:T(8,128)(2,1)S(1)} custom-call(s32[2]{0:T(128)S(1)} %pad_add_fusion.scalars.middle_ref, bf16[192,3712]{1,0:T(8,128)(2,1)S(1)} %collective-permute-done.3.refs_0_, bf16[96,3712]{1,0:T(8,128)(2,1)S(1)} %collective-permute-done.5.refs_1_, bf16[1,1792,1024]{2,1,0:T(8,128)(2,1)S(1)} %copy-done, ...), custom_call_target="tpu_custom_call" | custom-call | flops 1 | bytes 1 | tf_op jit(solution)/shard_map/pallas_call | solution.py:84
  66.4 5.6 %collective-permute-start.11 = (bf16[192,1536]{1,0:T(8,128)(2,1)S(1)}, bf16[192,1536]{1,0:T(8,128)(2,1)S(1)}, u32[]{:S(2)}, u32[]{:S(2)}) collective-permute-start(bf16[192,1536]{1,0:T(8,128)(2,1)S(1)} %get-tuple-element.156), channel_id=1, source_target_pairs={{0,8},{24,16},{8,0},{16,24},{1,9},{25,17},{9,1},{17,25},{2,10},{26... | collective-permute-start | bytes 1769480 | tf_op jit(solution)/shard_map/ppermute | solution.py:499
  72.0 2.7 %collective-permute-done.7.b_ref = bf16[192,1536]{1,0:T(8,128)(2,1)S(1)} collective-permute-done((bf16[192,1536]{1,0:T(8,128)(2,1)S(1)}, bf16[192,1536]{1,0:T(8,128)(2,1)S(1)}, u32[]{:S(2)}, u32[]{:S(2)}) %collective-permute-start.7) | collective-permute-done | bytes 589856 | tf_op jit(solution)/shard_map/ppermute | solution.py:492
  75.6 2.5 %shard_map.118 = (bf16[192,1536]{1,0:T(8,128)(2,1)S(1)}, bf16[192,1792]{1,0:T(8,128)(2,1)S(1)}, bf16[192,1792]{1,0:T(8,128)(2,1)S(1)}) custom-call(s32[2]{0:T(128)S(1)} %pad_add_fusion.scalars.middle_ref, bf16[192,3712]{1,0:T(8,128)(2,1)S(1)} %collective-permute-done.2.refs_0_, bf16[96,3712]{1,0:T(8,128)(2,1)S(1)} %collective-permute-done.9.refs_1_, ...), custom_call_target="tpu_custom_call" | custom-call | flops 1 | bytes 1 | tf_op jit(solution)/shard_map/pallas_call | solution.py:84
  78.9 5.7 %collective-permute-start.10 = (bf16[192,1536]{1,0:T(8,128)(2,1)S(1)}, bf16[192,1536]{1,0:T(8,128)(2,1)S(1)}, u32[]{:S(2)}, u32[]{:S(2)}) collective-permute-start(bf16[192,1536]{1,0:T(8,128)(2,1)S(1)} %get-tuple-element.165), channel_id=1, source_target_pairs={{0,8},{24,16},{8,0},{16,24},{1,9},{25,17},{9,1},{17,25},{2,10},{26... | collective-permute-start | bytes 1769480 | tf_op jit(solution)/shard_map/ppermute | solution.py:499
  84.6 2.7 %collective-permute-done.11.b_ref.came_ref = bf16[192,1536]{1,0:T(8,128)(2,1)S(1)} collective-permute-done((bf16[192,1536]{1,0:T(8,128)(2,1)S(1)}, bf16[192,1536]{1,0:T(8,128)(2,1)S(1)}, u32[]{:S(2)}, u32[]{:S(2)}) %collective-permute-start.11) | collective-permute-done | bytes 589856 | tf_op jit(solution)/shard_map/ppermute | solution.py:499
  87.7 0.9 collective-permute-start.12
  88.5 2.5 %shard_map.121.other_ref.a_ref = bf16[192,1536]{1,0:T(8,128)(2,1)S(1)} custom-call(s32[2]{0:T(128)S(1)} %pad_add_fusion.scalars.middle_ref, bf16[192,3712]{1,0:T(8,128)(2,1)S(1)} %collective-permute-done.2.refs_0_, bf16[96,3712]{1,0:T(8,128)(2,1)S(1)} %collective-permute-done.9.refs_1_, bf16[1,1792,1024]{2,1,0:T(8,128)(2,1)S(1)} %copy-done, ...), custom_call_target="tpu_custom_call" | custom-call | flops 1 | bytes 1 | tf_op jit(solution)/shard_map/pallas_call | solution.py:84
  91.1 1.6 shard_map.122
  92.7 5.3 %collective-permute-start.18 = (bf16[192,1536]{1,0:T(8,128)(2,1)}, bf16[192,1536]{1,0:T(8,128)(2,1)S(1)}, u32[]{:S(2)}, u32[]{:S(2)}) collective-permute-start(bf16[192,1536]{1,0:T(8,128)(2,1)} %get-tuple-element.172), channel_id=1, source_target_pairs={{0,8},{24,16},{8,0},{16,24},{1,9},{25,17},{9,1},{17,25},{2,10},{26... | collective-permute-start | bytes 1769480 | tf_op jit(solution)/shard_map/ppermute | solution.py:499
  97.9 2.5 %shard_map.123 = (bf16[192,1024]{1,0:T(8,128)(2,1)S(1)}, bf16[192,1024]{1,0:T(8,128)(2,1)S(1)}, bf16[192,1024]{1,0:T(8,128)(2,1)S(1)}, f32[192,1792]{1,0:T(8,128)S(1)}, f32[192,128]{1,0:T(8,128)S(1)}) custom-call(s32[2]{0:T(128)S(1)} %pad_add_fusion.scalars.middle_ref, bf16[192,1536]{1,0:T(8,128)(2,1)S(1)} %get-tuple-element.167.own_ref, ...), custom_call_target="tpu_custom_call" | custom-call | flops 1 | bytes 1 | tf_op jit(solution)/shard_map/pallas_call | solution.py:196
  101.3 2.5 %shard_map.125 = (bf16[192,1536]{1,0:T(8,128)(2,1)S(1)}, bf16[192,1792]{1,0:T(8,128)(2,1)S(1)}, bf16[192,1792]{1,0:T(8,128)(2,1)S(1)}) custom-call(s32[2]{0:T(128)S(1)} %pad_add_fusion.scalars.middle_ref, bf16[192,3712]{1,0:T(8,128)(2,1)S(1)} %collective-permute-done.14.refs_0_, bf16[96,3712]{1,0:T(8,128)(2,1)S(1)} %collective-permute-done.15.refs_1_, ...), custom_call_target="tpu_custom_call" | custom-call | flops 1 | bytes 1 | tf_op jit(solution)/shard_map/pallas_call | solution.py:84
  104.7 1.1 copy-done.6
  105.8 1.6 shard_map.126
  107.3 5.1 %collective-permute-start.17 = (bf16[192,1536]{1,0:T(8,128)(2,1)}, bf16[192,1536]{1,0:T(8,128)(2,1)S(1)}, u32[]{:S(2)}, u32[]{:S(2)}) collective-permute-start(bf16[192,1536]{1,0:T(8,128)(2,1)} %get-tuple-element.182), channel_id=1, source_target_pairs={{0,8},{24,16},{8,0},{16,24},{1,9},{25,17},{9,1},{17,25},{2,10},{26... | collective-permute-start | bytes 1769480 | tf_op jit(solution)/shard_map/ppermute | solution.py:499
  112.4 2.4 %shard_map.127 = (bf16[192,1024]{1,0:T(8,128)(2,1)S(1)}, bf16[192,1024]{1,0:T(8,128)(2,1)S(1)}, bf16[192,1024]{1,0:T(8,128)(2,1)S(1)}, bf16[96,1920]{1,0:T(8,128)(2,1)S(1)}, bf16[96,1920]{1,0:T(8,128)(2,1)S(1)}) custom-call(s32[2]{0:T(128)S(1)} %pad_add_fusion.scalars.middle_ref, ...), custom_call_target="tpu_custom_call", output_to_operand_aliasing={{0}: (9, {}), {1}: (10, {}), {2}: (11, {})} | custom-call | flops 1 | bytes 1 | tf_op jit(solution)/shard_map/pallas_call | solution.py:196
  117.2 2.5 %shard_map.129.other_ref.a_ref = bf16[192,1536]{1,0:T(8,128)(2,1)S(1)} custom-call(s32[2]{0:T(128)S(1)} %pad_add_fusion.scalars.middle_ref, bf16[192,3712]{1,0:T(8,128)(2,1)S(1)} %collective-permute-done.14.refs_0_, bf16[96,3712]{1,0:T(8,128)(2,1)S(1)} %collective-permute-done.15.refs_1_, bf16[1,1792,1024]{2,1,0:T(8,128)(2,1)S(1)} %copy-done, ...), custom_call_target="tpu_custom_call" | custom-call | flops 1 | bytes 1 | tf_op jit(solution)/shard_map/pallas_call | solution.py:84
  120.5 2.9 %collective-permute-start.23 = (bf16[192,1536]{1,0:T(8,128)(2,1)S(1)}, bf16[192,1536]{1,0:T(8,128)(2,1)S(1)}, u32[]{:S(2)}, u32[]{:S(2)}) collective-permute-start(bf16[192,1536]{1,0:T(8,128)(2,1)S(1)} %get-tuple-element.195), channel_id=1, source_target_pairs={{0,8},{24,16},{8,0},{16,24},{1,9},{25,17},{9,1},{17,25},{2,10},{26... | collective-permute-start | bytes 1769480 | tf_op jit(solution)/shard_map/ppermute | solution.py:499
  123.3 0.9 constant_dynamic-update-slice_fusion.2
  124.2 2.1 %shard_map.131 = (bf16[192,1024]{1,0:T(8,128)(2,1)S(1)}, bf16[192,1024]{1,0:T(8,128)(2,1)S(1)}, bf16[192,1024]{1,0:T(8,128)(2,1)S(1)}, f32[192,1792]{1,0:T(8,128)S(1)}, f32[192,128]{1,0:T(8,128)S(1)}) custom-call(s32[2]{0:T(128)S(1)} %pad_add_fusion.scalars.middle_ref, bf16[192,1536]{1,0:T(8,128)(2,1)S(1)} %get-tuple-element.192.own_ref, ...), custom_call_target="tpu_custom_call" | custom-call | flops 1 | bytes 1 | tf_op jit(solution)/shard_map/pallas_call | solution.py:196
  127.8 1.3 collective-permute-start.25
  129.2 2.1 %shard_map.134 = (bf16[192,1024]{1,0:T(8,128)(2,1)S(1)}, bf16[192,1024]{1,0:T(8,128)(2,1)S(1)}, bf16[192,1024]{1,0:T(8,128)(2,1)S(1)}, bf16[96,1920]{1,0:T(8,128)(2,1)S(1)}, bf16[96,1920]{1,0:T(8,128)(2,1)S(1)}) custom-call(s32[2]{0:T(128)S(1)} %pad_add_fusion.scalars.middle_ref, ...), custom_call_target="tpu_custom_call", output_to_operand_aliasing={{0}: (9, {}), {1}: (10, {}), {2}: (11, {})} | custom-call | flops 1 | bytes 1 | tf_op jit(solution)/shard_map/pallas_call | solution.py:196
  131.3 1.3 collective-permute-start.21
  133.3 6.2 %collective-permute-done.23.b_ref.came_ref = bf16[192,1536]{1,0:T(8,128)(2,1)S(1)} collective-permute-done((bf16[192,1536]{1,0:T(8,128)(2,1)S(1)}, bf16[192,1536]{1,0:T(8,128)(2,1)S(1)}, u32[]{:S(2)}, u32[]{:S(2)}) %collective-permute-start.23) | collective-permute-done | bytes 589856 | tf_op jit(solution)/shard_map/ppermute | solution.py:499
  141.3 1.5 collective-permute-start.30
  142.9 2.1 %shard_map.137 = (bf16[192,1024]{1,0:T(8,128)(2,1)S(1)}, bf16[192,1024]{1,0:T(8,128)(2,1)S(1)}, bf16[192,1024]{1,0:T(8,128)(2,1)S(1)}, f32[192,1792]{1,0:T(8,128)S(1)}, f32[192,128]{1,0:T(8,128)S(1)}) custom-call(s32[2]{0:T(128)S(1)} %pad_add_fusion.scalars.middle_ref, bf16[192,1536]{1,0:T(8,128)(2,1)S(1)} %get-tuple-element.210.own_ref, ...), custom_call_target="tpu_custom_call" | custom-call | flops 1 | bytes 1 | tf_op jit(solution)/shard_map/pallas_call | solution.py:196
  145.0 7.1 %collective-permute-done.25.came_ref = bf16[192,1536]{1,0:T(8,128)(2,1)S(1)} collective-permute-done((bf16[192,1536]{1,0:T(8,128)(2,1)S(1)}, bf16[192,1536]{1,0:T(8,128)(2,1)S(1)}, u32[]{:S(2)}, u32[]{:S(2)}) %collective-permute-start.25) | collective-permute-done | bytes 589856 | tf_op jit(solution)/shard_map/ppermute | solution.py:503
  152.1 2.1 %shard_map.138 = (bf16[192,1024]{1,0:T(8,128)(2,1)S(1)}, bf16[192,1024]{1,0:T(8,128)(2,1)S(1)}, bf16[192,1024]{1,0:T(8,128)(2,1)S(1)}, bf16[96,1920]{1,0:T(8,128)(2,1)S(1)}, bf16[96,1920]{1,0:T(8,128)(2,1)S(1)}) custom-call(s32[2]{0:T(128)S(1)} %pad_add_fusion.scalars.middle_ref, ...), custom_call_target="tpu_custom_call", output_to_operand_aliasing={{0}: (9, {}), {1}: (10, {}), {2}: (11, {})} | custom-call | flops 1 | bytes 1 | tf_op jit(solution)/shard_map/pallas_call | solution.py:196
  154.3 0.9 collective-permute-start.27
  155.3 1.4 collective-permute-start.29
  157.7 1.5 convolution_add_fusion.2
  159.6 3.3 %convolution_convert_fusion.7.before_ref = bf16[1024,1792]{1,0:T(8,128)(2,1)S(1)} fusion(bf16[576,1024]{1,0:T(8,128)(2,1)S(1)} %pad_maximum_fusion, bf16[192,1792]{1,0:T(8,128)(2,1)S(1)} %copy-done.18, bf16[192,1792]{1,0:T(8,128)(2,1)S(1)} %copy-done.16, bf16[192,1792]{1,0:T(8,128)(2,1)S(1)} %copy-done.14), kind=kOutput, calls=%fused_computation.7 | convolution fusion | flops 2121957376 | bytes 6914048 | tf_op jit(solution)/shard_map/dot_general | solution.py:374
  163.0 3.3 %convolution_convert_fusion.6.before_ref = bf16[1792,1024]{1,0:T(8,128)(2,1)S(1)} fusion(bf16[576,1792]{1,0:T(8,128)(2,1)S(1)} %copy-done.26, bf16[192,1024]{1,0:T(8,128)(2,1)S(1)} %get-tuple-element.237, bf16[192,1024]{1,0:T(8,128)(2,1)S(1)} %get-tuple-element.236, bf16[192,1024]{1,0:T(8,128)(2,1)S(1)} %copy-done.10), kind=kOutput, calls=%fused_computation.6 | convolution fusion | flops 2119303168 | bytes 6914048 | tf_op jit(solution)/shard_map/dot_general | solution.py:374
  166.3 0.9 slice_reduce_fusion.4
  167.2 3.3 %convolution_convert_fusion.5.before_ref = bf16[1792,1024]{1,0:T(8,128)(2,1)S(1)} fusion(bf16[576,1792]{1,0:T(8,128)(2,1)S(1)} %copy-done.26, bf16[192,1024]{1,0:T(8,128)(2,1)S(1)} %get-tuple-element.241, bf16[192,1024]{1,0:T(8,128)(2,1)S(1)} %get-tuple-element.240, bf16[192,1024]{1,0:T(8,128)(2,1)S(1)} %copy-done.12), kind=kOutput, calls=%fused_computation.5 | convolution fusion | flops 2119303168 | bytes 6914048 | tf_op jit(solution)/shard_map/dot_general | solution.py:374
  170.5 2.1 %shard_map.140 = (bf16[192,1024]{1,0:T(8,128)(2,1)S(1)}, bf16[192,1024]{1,0:T(8,128)(2,1)S(1)}, bf16[192,1024]{1,0:T(8,128)(2,1)S(1)}, f32[192,1792]{1,0:T(8,128)S(1)}, f32[192,128]{1,0:T(8,128)S(1)}) custom-call(s32[2]{0:T(128)S(1)} %pad_add_fusion.scalars.middle_ref, bf16[192,1536]{1,0:T(8,128)(2,1)S(1)} %shard_map.136.own_ref, ...), custom_call_target="tpu_custom_call" | custom-call | flops 1 | bytes 1 | tf_op jit(solution)/shard_map/pallas_call | solution.py:196
  172.6 3.0 %collective-permute-done.29.came_ref = bf16[192,1536]{1,0:T(8,128)(2,1)S(1)} collective-permute-done((bf16[192,1536]{1,0:T(8,128)(2,1)S(1)}, bf16[192,1536]{1,0:T(8,128)(2,1)S(1)}, u32[]{:S(2)}, u32[]{:S(2)}) %collective-permute-start.29) | collective-permute-done | bytes 589856 | tf_op jit(solution)/shard_map/ppermute | solution.py:503
  175.6 2.1 %shard_map.141 = (bf16[192,1024]{1,0:T(8,128)(2,1)S(1)}, bf16[192,1024]{1,0:T(8,128)(2,1)S(1)}, bf16[192,1024]{1,0:T(8,128)(2,1)S(1)}, bf16[96,1920]{1,0:T(8,128)(2,1)S(1)}, bf16[96,1920]{1,0:T(8,128)(2,1)S(1)}) custom-call(s32[2]{0:T(128)S(1)} %pad_add_fusion.scalars.middle_ref, ...), custom_call_target="tpu_custom_call", output_to_operand_aliasing={{0}: (9, {}), {1}: (10, {}), {2}: (11, {})} | custom-call | flops 1 | bytes 1 | tf_op jit(solution)/shard_map/pallas_call | solution.py:196
  177.8 1.5 collective-permute-start.31
  180.5 3.3 %shard_map.142 = bf16[1024,1792]{1,0:T(8,128)(2,1)} custom-call(bf16[192,1024]{1,0:T(8,128)(2,1)S(1)} %get-tuple-element.257.left_ref, bf16[192,1792]{1,0:T(8,128)(2,1)S(1)} %get-tuple-element.258.right_ref, bf16[1024,1792]{1,0:T(8,128)(2,1)S(1)} %convolution_convert_fusion.7.before_ref), custom_call_target="tpu_custom_call" | custom-call | flops 1 | bytes 1 | tf_op jit(solution)/shard_map/pallas_call | solution.py:219
  183.8 4.5 %shard_map.143 = bf16[1792,1024]{1,0:T(8,128)(2,1)} custom-call(bf16[192,1792]{1,0:T(8,128)(2,1)S(1)} %get-tuple-element.261.left_ref, bf16[192,1024]{1,0:T(8,128)(2,1)S(1)} %get-tuple-element.260.right_ref, bf16[1792,1024]{1,0:T(8,128)(2,1)S(1)} %convolution_convert_fusion.6.before_ref), custom_call_target="tpu_custom_call" | custom-call | flops 1 | bytes 1 | tf_op jit(solution)/shard_map/pallas_call | solution.py:219
  188.3 4.5 %shard_map.144 = bf16[1792,1024]{1,0:T(8,128)(2,1)} custom-call(bf16[192,1792]{1,0:T(8,128)(2,1)S(1)} %get-tuple-element.261.left_ref, bf16[192,1024]{1,0:T(8,128)(2,1)S(1)} %get-tuple-element.262.right_ref, bf16[1792,1024]{1,0:T(8,128)(2,1)S(1)} %convolution_convert_fusion.5.before_ref), custom_call_target="tpu_custom_call" | custom-call | flops 1 | bytes 1 | tf_op jit(solution)/shard_map/pallas_call | solution.py:219
  192.9 0.9 slice_reduce_fusion.2
  194.9 1.2 fusion.1
  (179 shorter events, 22.6 us)
Async XLA Ops:
  4.1 3.1 %copy-start.35 = (bf16[192,3]{1,0:T(8,128)(2,1)}, bf16[192,3]{1,0:T(8,128)(2,1)S(1)}, u32[]{:S(2)}) copy-start(bf16[192,3]{1,0:T(8,128)(2,1)S(1)} %copy.32) | copy-start | bytes 3460
  4.2 3.1 %copy-start.41 = (bf16[192,1792]{1,0:T(8,128)(2,1)S(1)}, bf16[192,1792]{1,0:T(8,128)(2,1)}, u32[]{:S(2)}) copy-start(bf16[192,1792]{1,0:T(8,128)(2,1)} %param.8) | copy-start | bytes 2064388
  4.2 3.1 %copy-start.43 = (bf16[192,1792]{1,0:T(8,128)(2,1)S(1)}, bf16[192,1792]{1,0:T(8,128)(2,1)}, u32[]{:S(2)}) copy-start(bf16[192,1792]{1,0:T(8,128)(2,1)} %param.7) | copy-start | bytes 2064388
  8.9 35.9 %collective-permute-start.2 = (bf16[192,3712]{1,0:T(8,128)(2,1)}, bf16[192,3712]{1,0:T(8,128)(2,1)S(1)}, u32[]{:S(2)}, u32[]{:S(2)}) collective-permute-start(bf16[192,3712]{1,0:T(8,128)(2,1)} %convolution_convert_fusion.1), channel_id=1, source_target_pairs={{0,4},{1,5},{2,6},{3,7},{4,0},{5,1},{6,2},{7,3},{8,12},{9,13},{10,... | collective-permute-start | bytes 4276232 | tf_op jit(solution)/shard_map/ppermute | solution.py:415
  11.9 32.9 %collective-permute-start.3 = (bf16[192,3712]{1,0:T(8,128)(2,1)}, bf16[192,3712]{1,0:T(8,128)(2,1)S(1)}, u32[]{:S(2)}, u32[]{:S(2)}) collective-permute-start(bf16[192,3712]{1,0:T(8,128)(2,1)} %convolution_convert_fusion.2), channel_id=1, source_target_pairs={{0,2},{1,3},{2,0},{3,1},{4,6},{5,7},{6,4},{7,5},{8,10},{9,11},{10,... | collective-permute-start | bytes 4276232 | tf_op jit(solution)/shard_map/ppermute | solution.py:415
  14.0 2.1 %copy-start.31 = (bf16[96,192]{1,0:T(8,128)(2,1)}, bf16[96,192]{1,0:T(8,128)(2,1)S(1)}, u32[]{:S(2)}) copy-start(bf16[96,192]{1,0:T(8,128)(2,1)S(1)} %get-tuple-element.135) | copy-start | bytes 110596
  14.0 2.2 %copy-start.33 = (bf16[96,192]{1,0:T(8,128)(2,1)}, bf16[96,192]{1,0:T(8,128)(2,1)S(1)}, u32[]{:S(2)}) copy-start(bf16[96,192]{1,0:T(8,128)(2,1)S(1)} %get-tuple-element.136) | copy-start | bytes 110596
  14.0 2.2 %copy-start.36 = (bf16[192,3]{1,0:T(8,128)(2,1)S(1)}, bf16[192,3]{1,0:T(8,128)(2,1)}, u32[]{:S(2)}) copy-start(bf16[192,3]{1,0:T(8,128)(2,1)} %copy-done.35) | copy-start | bytes 3460
  16.1 2.5 %collective-permute-start = (bf16[96,3712]{1,0:T(8,128)(2,1)}, bf16[96,3712]{1,0:T(8,128)(2,1)}, u32[]{:S(2)}, u32[]{:S(2)}) collective-permute-start(bf16[96,3712]{1,0:T(8,128)(2,1)} %convolution_convert_fusion.4), channel_id=1, source_target_pairs={{0,1},{1,0},{2,3},{3,2},{4,5},{5,4},{6,7},{7,6},{8,9},{9,8},{10,11... | collective-permute-start | bytes 2138120 | tf_op jit(solution)/shard_map/ppermute | solution.py:290
  16.2 2.5 %copy-start = (bf16[1,1792,1024]{2,1,0:T(8,128)(2,1)S(1)}, bf16[1,1792,1024]{2,1,0:T(8,128)(2,1)}, u32[]{:S(2)}) copy-start(bf16[1,1792,1024]{2,1,0:T(8,128)(2,1)} %refs_2_.31) | copy-start | bytes 11010052
  18.7 2.0 %copy-start.1 = (bf16[1,1792,1024]{2,1,0:T(8,128)(2,1)S(1)}, bf16[1,1792,1024]{2,1,0:T(8,128)(2,1)}, u32[]{:S(2)}) copy-start(bf16[1,1792,1024]{2,1,0:T(8,128)(2,1)} %refs_3_.31) | copy-start | bytes 11010052
  20.7 2.0 %copy-start.3 = (bf16[1,1024,1792]{2,1,0:T(8,128)(2,1)S(1)}, bf16[1,1024,1792]{2,1,0:T(8,128)(2,1)}, u32[]{:S(2)}) copy-start(bf16[1,1024,1792]{2,1,0:T(8,128)(2,1)} %refs_4_.15) | copy-start | bytes 11010052
  26.7 6.8 %copy-start.42 = (bf16[192,1792]{1,0:T(8,128)(2,1)S(1)}, bf16[192,1792]{1,0:T(8,128)(2,1)}, u32[]{:S(2)}) copy-start(bf16[192,1792]{1,0:T(8,128)(2,1)} %param.8) | copy-start | bytes 2064388
  26.7 6.8 %copy-start.44 = (bf16[192,1792]{1,0:T(8,128)(2,1)S(1)}, bf16[192,1792]{1,0:T(8,128)(2,1)}, u32[]{:S(2)}) copy-start(bf16[192,1792]{1,0:T(8,128)(2,1)} %param.7) | copy-start | bytes 2064388
  26.7 16.9 %collective-permute-start.4 = (bf16[192,1536]{1,0:T(8,128)(2,1)S(1)}, bf16[192,1536]{1,0:T(8,128)(2,1)S(1)}, u32[]{:S(2)}, u32[]{:S(2)}) collective-permute-start(bf16[192,1536]{1,0:T(8,128)(2,1)S(1)} %get-tuple-element.140.a_ref), channel_id=1, source_target_pairs={{0,8},{24,16},{1,9},{25,17},{2,10},{26,18},{3,11},{27,19},{4,12},{... | collective-permute-start | bytes 1769480 | tf_op jit(solution)/shard_map/ppermute | solution.py:476
  34.1 14.4 %copy-start.2 = (bf16[1,1792,1024]{2,1,0:T(8,128)(2,1)S(1)}, bf16[1,1792,1024]{2,1,0:T(8,128)(2,1)}, u32[]{:S(2)}) copy-start(bf16[1,1792,1024]{2,1,0:T(8,128)(2,1)} %refs_3_.31) | copy-start | bytes 11010052
  44.9 3.6 %collective-permute-start.5 = (bf16[96,3712]{1,0:T(8,128)(2,1)S(1)}, bf16[96,3712]{1,0:T(8,128)(2,1)S(1)}, u32[]{:S(2)}, u32[]{:S(2)}) collective-permute-start(bf16[96,3712]{1,0:T(8,128)(2,1)S(1)} %slice.114), channel_id=1, source_target_pairs={{0,1},{1,0},{2,3},{3,2},{4,5},{5,4},{6,7},{7,6},{8,9},{9,8},{10,11... | collective-permute-start | bytes 2138120 | tf_op jit(solution)/shard_map/ppermute | solution.py:427
  45.0 17.1 %collective-permute-start.1 = (bf16[192,1536]{1,0:T(8,128)(2,1)S(1)}, bf16[192,1536]{1,0:T(8,128)(2,1)S(1)}, u32[]{:S(2)}, u32[]{:S(2)}) collective-permute-start(bf16[192,1536]{1,0:T(8,128)(2,1)S(1)} %shard_map.111.a_ref), channel_id=1, source_target_pairs={{0,8},{24,16},{1,9},{25,17},{2,10},{26,18},{3,11},{27,19},{4,12},{... | collective-permute-start | bytes 1769480 | tf_op jit(solution)/shard_map/ppermute | solution.py:478
  51.9 35.6 %collective-permute-start.14 = (bf16[192,3712]{1,0:T(8,128)(2,1)S(1)}, bf16[192,3712]{1,0:T(8,128)(2,1)S(1)}, u32[]{:S(2)}, u32[]{:S(2)}) collective-permute-start(bf16[192,3712]{1,0:T(8,128)(2,1)S(1)} %convolution_convert_fusion), channel_id=1, source_target_pairs={{0,6},{1,7},{2,4},{3,5},{4,2},{5,3},{6,0},{7,1},{8,14},{9,15},{10,... | collective-permute-start | bytes 4276232 | tf_op jit(solution)/shard_map/ppermute | solution.py:415
  53.3 12.2 %collective-permute-start.8 = (bf16[192,1536]{1,0:T(8,128)(2,1)S(1)}, bf16[192,1536]{1,0:T(8,128)(2,1)S(1)}, u32[]{:S(2)}, u32[]{:S(2)}) collective-permute-start(bf16[192,1536]{1,0:T(8,128)(2,1)S(1)} %shard_map.112.a_ref), channel_id=1, source_target_pairs={{8,16},{16,8},{9,17},{17,9},{10,18},{18,10},{11,19},{19,11},{12,20... | collective-permute-start | bytes 1769480 | tf_op jit(solution)/shard_map/ppermute | solution.py:484
  54.0 20.7 %collective-permute-start.7 = (bf16[192,1536]{1,0:T(8,128)(2,1)S(1)}, bf16[192,1536]{1,0:T(8,128)(2,1)S(1)}, u32[]{:S(2)}, u32[]{:S(2)}) collective-permute-start(bf16[192,1536]{1,0:T(8,128)(2,1)S(1)} %get-tuple-element.152.a_ref), channel_id=1, source_target_pairs={{0,8},{24,16},{1,9},{25,17},{2,10},{26,18},{3,11},{27,19},{4,12},{... | collective-permute-start | bytes 1769480 | tf_op jit(solution)/shard_map/ppermute | solution.py:492
  62.2 13.3 %collective-permute-start.9 = (bf16[96,3712]{1,0:T(8,128)(2,1)S(1)}, bf16[96,3712]{1,0:T(8,128)(2,1)S(1)}, u32[]{:S(2)}, u32[]{:S(2)}) collective-permute-start(bf16[96,3712]{1,0:T(8,128)(2,1)S(1)} %slice.115), channel_id=1, source_target_pairs={{0,1},{1,0},{2,3},{3,2},{4,5},{5,4},{6,7},{7,6},{8,9},{9,8},{10,11... | collective-permute-start | bytes 2138120 | tf_op jit(solution)/shard_map/ppermute | solution.py:427
  62.3 15.8 %collective-permute-start.6 = (bf16[192,1536]{1,0:T(8,128)(2,1)S(1)}, bf16[192,1536]{1,0:T(8,128)(2,1)S(1)}, u32[]{:S(2)}, u32[]{:S(2)}) collective-permute-start(bf16[192,1536]{1,0:T(8,128)(2,1)S(1)} %shard_map.114.a_ref), channel_id=1, source_target_pairs={{8,16},{16,8},{9,17},{17,9},{10,18},{18,10},{11,19},{19,11},{12,20... | collective-permute-start | bytes 1769480 | tf_op jit(solution)/shard_map/ppermute | solution.py:484
  66.4 21.0 %collective-permute-start.11 = (bf16[192,1536]{1,0:T(8,128)(2,1)S(1)}, bf16[192,1536]{1,0:T(8,128)(2,1)S(1)}, u32[]{:S(2)}, u32[]{:S(2)}) collective-permute-start(bf16[192,1536]{1,0:T(8,128)(2,1)S(1)} %get-tuple-element.156), channel_id=1, source_target_pairs={{0,8},{24,16},{8,0},{16,24},{1,9},{25,17},{9,1},{17,25},{2,10},{26... | collective-permute-start | bytes 1769480 | tf_op jit(solution)/shard_map/ppermute | solution.py:499
  74.9 16.2 %collective-permute-start.13 = (bf16[192,1536]{1,0:T(8,128)(2,1)S(1)}, bf16[192,1536]{1,0:T(8,128)(2,1)S(1)}, u32[]{:S(2)}, u32[]{:S(2)}) collective-permute-start(bf16[192,1536]{1,0:T(8,128)(2,1)S(1)} %shard_map.117.a_ref), channel_id=1, source_target_pairs={{8,16},{16,8},{9,17},{17,9},{10,18},{18,10},{11,19},{19,11},{12,20... | collective-permute-start | bytes 1769480 | tf_op jit(solution)/shard_map/ppermute | solution.py:484
  78.1 9.5 %copy-start.17 = (bf16[192,1792]{1,0:T(8,128)(2,1)}, bf16[192,1792]{1,0:T(8,128)(2,1)S(1)}, u32[]{:S(2)}) copy-start(bf16[192,1792]{1,0:T(8,128)(2,1)S(1)} %get-tuple-element.233) | copy-start | bytes 2064388
  78.9 21.5 %collective-permute-start.10 = (bf16[192,1536]{1,0:T(8,128)(2,1)S(1)}, bf16[192,1536]{1,0:T(8,128)(2,1)S(1)}, u32[]{:S(2)}, u32[]{:S(2)}) collective-permute-start(bf16[192,1536]{1,0:T(8,128)(2,1)S(1)} %get-tuple-element.165), channel_id=1, source_target_pairs={{0,8},{24,16},{8,0},{16,24},{1,9},{25,17},{9,1},{17,25},{2,10},{26... | collective-permute-start | bytes 1769480 | tf_op jit(solution)/shard_map/ppermute | solution.py:499
  87.6 13.7 %collective-permute-start.15 = (bf16[96,3712]{1,0:T(8,128)(2,1)S(1)}, bf16[96,3712]{1,0:T(8,128)(2,1)S(1)}, u32[]{:S(2)}, u32[]{:S(2)}) collective-permute-start(bf16[96,3712]{1,0:T(8,128)(2,1)S(1)} %slice.116), channel_id=1, source_target_pairs={{0,1},{1,0},{2,3},{3,2},{4,5},{5,4},{6,7},{7,6},{8,9},{9,8},{10,11... | collective-permute-start | bytes 2138120 | tf_op jit(solution)/shard_map/ppermute | solution.py:427
  87.7 16.2 %collective-permute-start.12 = (bf16[192,1536]{1,0:T(8,128)(2,1)S(1)}, bf16[192,1536]{1,0:T(8,128)(2,1)S(1)}, u32[]{:S(2)}, u32[]{:S(2)}) collective-permute-start(bf16[192,1536]{1,0:T(8,128)(2,1)S(1)} %shard_map.120.a_ref), channel_id=1, source_target_pairs={{8,16},{16,8},{9,17},{17,9},{10,18},{18,10},{11,19},{19,11},{12,20... | collective-permute-start | bytes 1769480 | tf_op jit(solution)/shard_map/ppermute | solution.py:484
  92.7 23.6 %collective-permute-start.18 = (bf16[192,1536]{1,0:T(8,128)(2,1)}, bf16[192,1536]{1,0:T(8,128)(2,1)S(1)}, u32[]{:S(2)}, u32[]{:S(2)}) collective-permute-start(bf16[192,1536]{1,0:T(8,128)(2,1)} %get-tuple-element.172), channel_id=1, source_target_pairs={{0,8},{24,16},{8,0},{16,24},{1,9},{25,17},{9,1},{17,25},{2,10},{26... | collective-permute-start | bytes 1769480 | tf_op jit(solution)/shard_map/ppermute | solution.py:499
  97.9 3.4 %copy-start.4 = (bf16[1,1024,1792]{2,1,0:T(8,128)(2,1)S(1)}, bf16[1,1024,1792]{2,1,0:T(8,128)(2,1)}, u32[]{:S(2)}) copy-start(bf16[1,1024,1792]{2,1,0:T(8,128)(2,1)} %refs_4_.15) | copy-start | bytes 11010052
  100.6 19.1 %collective-permute-start.20 = (bf16[192,1536]{1,0:T(8,128)(2,1)S(1)}, bf16[192,1536]{1,0:T(8,128)(2,1)S(1)}, u32[]{:S(2)}, u32[]{:S(2)}) collective-permute-start(bf16[192,1536]{1,0:T(8,128)(2,1)S(1)} %shard_map.124.a_ref), channel_id=1, source_target_pairs={{8,16},{16,8},{9,17},{17,9},{10,18},{18,10},{11,19},{19,11},{12,20... | collective-permute-start | bytes 1769480 | tf_op jit(solution)/shard_map/ppermute | solution.py:484
  101.3 11.1 %copy-start.8 = (bf16[192,1024]{1,0:T(8,128)(2,1)S(1)}, bf16[192,1024]{1,0:T(8,128)(2,1)}, u32[]{:S(2)}) copy-start(bf16[192,1024]{1,0:T(8,128)(2,1)} %copy-done.7) | copy-start | bytes 1179652
  107.3 19.5 %collective-permute-start.17 = (bf16[192,1536]{1,0:T(8,128)(2,1)}, bf16[192,1536]{1,0:T(8,128)(2,1)S(1)}, u32[]{:S(2)}, u32[]{:S(2)}) collective-permute-start(bf16[192,1536]{1,0:T(8,128)(2,1)} %get-tuple-element.182), channel_id=1, source_target_pairs={{0,8},{24,16},{8,0},{16,24},{1,9},{25,17},{9,1},{17,25},{2,10},{26... | collective-permute-start | bytes 1769480 | tf_op jit(solution)/shard_map/ppermute | solution.py:499
  116.5 11.2 %collective-permute-start.19 = (bf16[192,1536]{1,0:T(8,128)(2,1)S(1)}, bf16[192,1536]{1,0:T(8,128)(2,1)S(1)}, u32[]{:S(2)}, u32[]{:S(2)}) collective-permute-start(bf16[192,1536]{1,0:T(8,128)(2,1)S(1)} %shard_map.128.a_ref), channel_id=1, source_target_pairs={{8,16},{16,8},{9,17},{17,9},{10,18},{18,10},{11,19},{19,11},{12,20... | collective-permute-start | bytes 1769480 | tf_op jit(solution)/shard_map/ppermute | solution.py:484
  120.5 19.0 %collective-permute-start.23 = (bf16[192,1536]{1,0:T(8,128)(2,1)S(1)}, bf16[192,1536]{1,0:T(8,128)(2,1)S(1)}, u32[]{:S(2)}, u32[]{:S(2)}) collective-permute-start(bf16[192,1536]{1,0:T(8,128)(2,1)S(1)} %get-tuple-element.195), channel_id=1, source_target_pairs={{0,8},{24,16},{8,0},{16,24},{1,9},{25,17},{9,1},{17,25},{2,10},{26... | collective-permute-start | bytes 1769480 | tf_op jit(solution)/shard_map/ppermute | solution.py:499
  123.3 9.3 %collective-permute-start.16 = (bf16[96,1920]{1,0:T(8,128)(2,1)S(1)}, bf16[96,1920]{1,0:T(8,128)(2,1)S(1)}, u32[]{:S(2)}, u32[]{:S(2)}) collective-permute-start(bf16[96,1920]{1,0:T(8,128)(2,1)S(1)} %get-tuple-element.189), channel_id=1, source_target_pairs={{0,1},{1,0},{2,3},{3,2},{4,5},{5,4},{6,7},{7,6},{8,9},{9,8},{10,11... | collective-permute-start | bytes 1105928 | tf_op jit(solution)/shard_map/ppermute | solution.py:463
  127.0 14.2 %collective-permute-start.26 = (bf16[192,1536]{1,0:T(8,128)(2,1)S(1)}, bf16[192,1536]{1,0:T(8,128)(2,1)S(1)}, u32[]{:S(2)}, u32[]{:S(2)}) collective-permute-start(bf16[192,1536]{1,0:T(8,128)(2,1)S(1)} %shard_map.132.a_ref), channel_id=1, source_target_pairs={{8,16},{16,8},{9,17},{17,9},{10,18},{18,10},{11,19},{19,11},{12,20... | collective-permute-start | bytes 1769480 | tf_op jit(solution)/shard_map/ppermute | solution.py:484
  127.8 24.3 %collective-permute-start.25 = (bf16[192,1536]{1,0:T(8,128)(2,1)S(1)}, bf16[192,1536]{1,0:T(8,128)(2,1)S(1)}, u32[]{:S(2)}, u32[]{:S(2)}) collective-permute-start(bf16[192,1536]{1,0:T(8,128)(2,1)S(1)} %shard_map.133.own_ref), channel_id=1, source_target_pairs={{8,0},{16,24},{9,1},{17,25},{10,2},{18,26},{11,3},{19,27},{12,4},{... | collective-permute-start | bytes 1769480 | tf_op jit(solution)/shard_map/ppermute | solution.py:503
  129.1 3.7 %copy-start.32 = (bf16[96,192]{1,0:T(8,128)(2,1)S(1)}, bf16[96,192]{1,0:T(8,128)(2,1)}, u32[]{:S(2)}) copy-start(bf16[96,192]{1,0:T(8,128)(2,1)} %copy-done.31) | copy-start | bytes 110596
  129.2 3.7 %copy-start.34 = (bf16[96,192]{1,0:T(8,128)(2,1)S(1)}, bf16[96,192]{1,0:T(8,128)(2,1)}, u32[]{:S(2)}) copy-start(bf16[96,192]{1,0:T(8,128)(2,1)} %copy-done.33) | copy-start | bytes 110596
  131.3 25.5 %collective-permute-start.21 = (bf16[96,1920]{1,0:T(8,128)(2,1)S(1)}, bf16[96,1920]{1,0:T(8,128)(2,1)S(1)}, u32[]{:S(2)}, u32[]{:S(2)}) collective-permute-start(bf16[96,1920]{1,0:T(8,128)(2,1)S(1)} %get-tuple-element.205), channel_id=1, source_target_pairs={{0,2},{1,3},{2,0},{3,1},{4,6},{5,7},{6,4},{7,5},{8,10},{9,11},{10,... | collective-permute-start | bytes 1105928 | tf_op jit(solution)/shard_map/ppermute | solution.py:463
  132.7 7.7 %copy-start.24 = (bf16[576,1792]{1,0:T(8,128)(2,1)S(1)}, bf16[576,1792]{1,0:T(8,128)(2,1)}, u32[]{:S(2)}) copy-start(bf16[576,1792]{1,0:T(8,128)(2,1)} %constant_dynamic-update-slice_fusion.2) | copy-start | bytes 6193156
  132.7 24.1 %collective-permute-start.22 = (bf16[96,1920]{1,0:T(8,128)(2,1)S(1)}, bf16[96,1920]{1,0:T(8,128)(2,1)S(1)}, u32[]{:S(2)}, u32[]{:S(2)}) collective-permute-start(bf16[96,1920]{1,0:T(8,128)(2,1)S(1)} %get-tuple-element.208), channel_id=1, source_target_pairs={{0,3},{1,2},{2,1},{3,0},{4,7},{5,6},{6,5},{7,4},{8,11},{9,10},{10,... | collective-permute-start | bytes 1105928 | tf_op jit(solution)/shard_map/ppermute | solution.py:463
  139.6 15.6 %collective-permute-start.24 = (bf16[192,1536]{1,0:T(8,128)(2,1)S(1)}, bf16[192,1536]{1,0:T(8,128)(2,1)S(1)}, u32[]{:S(2)}, u32[]{:S(2)}) collective-permute-start(bf16[192,1536]{1,0:T(8,128)(2,1)S(1)} %shard_map.135.a_ref), channel_id=1, source_target_pairs={{8,16},{16,8},{9,17},{17,9},{10,18},{18,10},{11,19},{19,11},{12,20... | collective-permute-start | bytes 1769480 | tf_op jit(solution)/shard_map/ppermute | solution.py:484
  140.4 2.4 %copy-start.25 = (bf16[576,1792]{1,0:T(8,128)(2,1)}, bf16[576,1792]{1,0:T(8,128)(2,1)S(1)}, u32[]{:S(2)}) copy-start(bf16[576,1792]{1,0:T(8,128)(2,1)S(1)} %constant_dynamic-update-slice_fusion) | copy-start | bytes 6193156
  141.3 29.1 %collective-permute-start.30 = (bf16[192,1536]{1,0:T(8,128)(2,1)S(1)}, bf16[192,1536]{1,0:T(8,128)(2,1)S(1)}, u32[]{:S(2)}, u32[]{:S(2)}) collective-permute-start(bf16[192,1536]{1,0:T(8,128)(2,1)S(1)} %shard_map.136.own_ref), channel_id=1, source_target_pairs={{8,0},{16,24},{9,1},{17,25},{10,2},{18,26},{11,3},{19,27},{12,4},{... | collective-permute-start | bytes 1769480 | tf_op jit(solution)/shard_map/ppermute | solution.py:503
  154.3 25.0 %collective-permute-start.27 = (bf16[96,1920]{1,0:T(8,128)(2,1)S(1)}, bf16[96,1920]{1,0:T(8,128)(2,1)S(1)}, u32[]{:S(2)}, u32[]{:S(2)}) collective-permute-start(bf16[96,1920]{1,0:T(8,128)(2,1)S(1)} %get-tuple-element.219), channel_id=1, source_target_pairs={{0,4},{1,5},{2,6},{3,7},{4,0},{5,1},{6,2},{7,3},{8,12},{9,13},{10,... | collective-permute-start | bytes 1105928 | tf_op jit(solution)/shard_map/ppermute | solution.py:463
  155.3 2.4 %copy-start.27 = (bf16[96,192]{1,0:T(8,128)(2,1)S(1)}, bf16[96,192]{1,0:T(8,128)(2,1)}, u32[]{:S(2)}) copy-start(bf16[96,192]{1,0:T(8,128)(2,1)} %get-tuple-element.267) | copy-start | bytes 110596
  155.3 2.4 %copy-start.28 = (bf16[96,192]{1,0:T(8,128)(2,1)S(1)}, bf16[96,192]{1,0:T(8,128)(2,1)}, u32[]{:S(2)}) copy-start(bf16[96,192]{1,0:T(8,128)(2,1)} %get-tuple-element.268) | copy-start | bytes 110596
  155.3 20.3 %collective-permute-start.29 = (bf16[192,1536]{1,0:T(8,128)(2,1)S(1)}, bf16[192,1536]{1,0:T(8,128)(2,1)S(1)}, u32[]{:S(2)}, u32[]{:S(2)}) collective-permute-start(bf16[192,1536]{1,0:T(8,128)(2,1)S(1)} %shard_map.139.own_ref), channel_id=1, source_target_pairs={{8,0},{16,24},{9,1},{17,25},{10,2},{18,26},{11,3},{19,27},{12,4},{... | collective-permute-start | bytes 1769480 | tf_op jit(solution)/shard_map/ppermute | solution.py:503
  156.8 2.4 %copy-start.21 = (bf16[96,1920]{1,0:T(8,128)(2,1)}, bf16[96,1920]{1,0:T(8,128)(2,1)S(1)}, u32[]{:S(2)}) copy-start(bf16[96,1920]{1,0:T(8,128)(2,1)S(1)} %collective-permute-done.21) | copy-start | bytes 1105924
  156.9 22.4 %collective-permute-start.28 = (bf16[96,1920]{1,0:T(8,128)(2,1)S(1)}, bf16[96,1920]{1,0:T(8,128)(2,1)S(1)}, u32[]{:S(2)}, u32[]{:S(2)}) collective-permute-start(bf16[96,1920]{1,0:T(8,128)(2,1)S(1)} %get-tuple-element.223), channel_id=1, source_target_pairs={{0,5},{1,4},{2,7},{3,6},{4,1},{5,0},{6,3},{7,2},{8,13},{9,12},{10,... | collective-permute-start | bytes 1105928 | tf_op jit(solution)/shard_map/ppermute | solution.py:463
  159.6 3.3 %copy-start.10 = (bf16[192,1024]{1,0:T(8,128)(2,1)S(1)}, bf16[192,1024]{1,0:T(8,128)(2,1)}, u32[]{:S(2)}) copy-start(bf16[192,1024]{1,0:T(8,128)(2,1)} %copy-done.9) | copy-start | bytes 1179652
  159.6 3.3 %copy-start.26 = (bf16[576,1792]{1,0:T(8,128)(2,1)S(1)}, bf16[576,1792]{1,0:T(8,128)(2,1)}, u32[]{:S(2)}) copy-start(bf16[576,1792]{1,0:T(8,128)(2,1)} %copy-done.25) | copy-start | bytes 6193156
  163.0 4.2 %copy-start.12 = (bf16[192,1024]{1,0:T(8,128)(2,1)S(1)}, bf16[192,1024]{1,0:T(8,128)(2,1)}, u32[]{:S(2)}) copy-start(bf16[192,1024]{1,0:T(8,128)(2,1)} %copy-done.11) | copy-start | bytes 1179652
  177.8 2.4 %copy-start.19 = (f32[192,1792]{1,0:T(8,128)S(1)}, f32[192,1792]{1,0:T(8,128)}, u32[]{:S(2)}) copy-start(f32[192,1792]{1,0:T(8,128)} %convolution_add_fusion.2) | copy-start | bytes 4128772
  177.8 16.0 %collective-permute-start.31 = (bf16[96,1920]{1,0:T(8,128)(2,1)S(1)}, bf16[96,1920]{1,0:T(8,128)(2,1)S(1)}, u32[]{:S(2)}, u32[]{:S(2)}) collective-permute-start(bf16[96,1920]{1,0:T(8,128)(2,1)S(1)} %get-tuple-element.249), channel_id=1, source_target_pairs={{0,6},{1,7},{2,4},{3,5},{4,2},{5,3},{6,0},{7,1},{8,14},{9,15},{10,... | collective-permute-start | bytes 1105928 | tf_op jit(solution)/shard_map/ppermute | solution.py:463
  179.4 14.4 %collective-permute-start.32 = (bf16[96,1920]{1,0:T(8,128)(2,1)S(1)}, bf16[96,1920]{1,0:T(8,128)(2,1)S(1)}, u32[]{:S(2)}, u32[]{:S(2)}) collective-permute-start(bf16[96,1920]{1,0:T(8,128)(2,1)S(1)} %get-tuple-element.252), channel_id=1, source_target_pairs={{0,7},{1,6},{2,5},{3,4},{4,3},{5,2},{6,1},{7,0},{8,15},{9,14},{10,... | collective-permute-start | bytes 1105928 | tf_op jit(solution)/shard_map/ppermute | solution.py:463
  188.3 5.6 %copy-start.38 = (bf16[96]{0:T(256)(128)(2,1)S(1)}, bf16[96]{0:T(256)(128)(2,1)}, u32[]{:S(2)}) copy-start(bf16[96]{0:T(256)(128)(2,1)} %get-tuple-element.276) | copy-start | bytes 580
  188.3 5.9 %copy-start.37 = (s32[192,2]{0,1:T(2,128)S(1)}, s32[192,2]{0,1:T(2,128)}, u32[]{:S(2)}) copy-start(s32[192,2]{0,1:T(2,128)} %param.9) | copy-start | bytes 4612
  188.3 5.9 %copy-start.40 = (s32[8]{0:T(128)S(1)}, s32[8]{0:T(128)}, u32[]{:S(2)}) copy-start(s32[8]{0:T(128)} %copy-done.39) | copy-start | bytes 100
  188.3 6.6 %copy-start.29 = (bf16[96,192]{1,0:T(8,128)(2,1)S(1)}, bf16[96,192]{1,0:T(8,128)(2,1)}, u32[]{:S(2)}) copy-start(bf16[96,192]{1,0:T(8,128)(2,1)} %get-tuple-element.263) | copy-start | bytes 110596
  188.3 6.6 %copy-start.30 = (bf16[96,192]{1,0:T(8,128)(2,1)S(1)}, bf16[96,192]{1,0:T(8,128)(2,1)}, u32[]{:S(2)}) copy-start(bf16[96,192]{1,0:T(8,128)(2,1)} %get-tuple-element.264) | copy-start | bytes 110596
  (14 other events, 14.8 us)

commit v3 on v2

--- a/solution.py
+++ b/solution.py
@@ -249,7 +249,7 @@
     choose = routes.shape[1]
     capacity = 2 * tokens * choose // groups
     per_chunk = max(1, groups // 4)
-    offsets = list(range(groups))
+    offsets = [0, 1, 3, 5, 6, 7, 2, 4] if groups == 8 else list(range(groups))
     chunks = [offsets[i : i + per_chunk] for i in range(0, groups, per_chunk)]
 
     partner = me ^ jnp.arange(groups, dtype=jnp.int32)
@@ -427,10 +427,12 @@
                 lax.ppermute(other, "expert", [(i, i ^ 1) for i in range(groups)]),
             ]
 
+        def fetch_last(c):
+            rows[c] = [fetch(r) for r in chunks[c]]
+
         rows = {}
-        fetch_pair(1)
-        fetch_pair(2)
         from_core = fetch(1)
+        rows[1] = [fetch(r) for r in chunks[1]]
         rows[0] = [fetch(0), from_core]
 
         def compute_part(k):
@@ -464,7 +466,9 @@
                 returned[r] = one
 
         work = {
-            1: [(fetch_pair, 3)],
+            1: [(fetch_pair, 2)],
+            2: [(split, 2), (hand_on, 2)],
+            3: [(fetch_last, 3)],
             4: [(finish, 0)],
             5: [(finish, 1)],
             6: [(finish, 2)],
@@ -476,16 +480,12 @@
         arrived[0] = lax.ppermute(part[0], "dp", inward)
         compute_part(1)
         arrived[1] = lax.ppermute(part[1], "dp", inward)
-        pick_pair(3)
+        pick_pair(2)
         for t in range(1, pieces + 2):
             if t <= pieces:
                 (came,) = gate(arrived[t - 1])
                 partly[t - 1] = mark(add_pieces(part[t - 1], came))
                 crossed[t - 1] = lax.ppermute(partly[t - 1], "dp", across)
-            for c in {1: (1, 2), 4: (3,)}.get(t, ()):
-                split(c)
-            if t in (1, 2, 4):
-                hand_on({1: 1, 2: 2, 4: 3}[t])
             if t + 1 < pieces:
                 compute_part(t + 1)
             if t == 1:

time: 199 us -> 217 us (1.090)
  waiting for transfers between devices: 36.7 us -> 68.7 us
  starting transfers between devices: 56.7 us -> 50.6 us
  local copies, waits for them, and re-layouts: 16.2 us -> 13 us
    ppermute x3 -> x1, waiting for transfers between devices: 1.06 us -> 13.3 us  [fetch_pair(): pairs[c] = lax.ppermute(sent, 'expert', [(i, i ^ r) for i in range(groups)])]
    ppermute x1, waiting for transfers between devices: 3.16 us -> 11.4 us  [body(): arrived[1] = lax.ppermute(part[1], 'dp', inward)]
    ppermute x1, waiting for transfers between devices: 2.72 us -> 10.7 us  [body(): arrived[2] = lax.ppermute(part[2], 'dp', inward)]
    ppermute x3 -> x1, starting transfers between devices: 5.89 us -> 0.55 us  [fetch_pair(): pairs[c] = lax.ppermute(sent, 'expert', [(i, i ^ r) for i in range(groups)])]
    ppermute x1 -> x5, starting transfers between devices: 0.01 us -> 5.19 us  [fetch(): rows = lax.ppermute(rows, 'expert', [(i, i ^ r) for i in range(groups)])]
    ppermute x5, starting transfers between devices: 24.5 us -> 19.4 us  [body(): arrived[t + 1] = lax.ppermute(both, 'dp', inward + outward)]
    dot_general x3 -> x1, matrix products: 5.25 us -> 0.54 us  [pick_pair(): jnp.dot(both, packed, preferred_element_type=F32).astype(BF16)]
    dot_general x2 -> x6, matrix products: 3.9 us -> 7.87 us  [fetch(): rows = jnp.dot(one, packed, preferred_element_type=F32).astype(BF16)]
  transfers between devices with their start and end apart: 33 -> 33, of which waited for: 10 -> 11; matrix products, arithmetic and copies ran while one was open for 11% -> 11% of each run, Pallas kernels for 30% -> 25%
where the time goes in v3:
time: 217 us; the launch traced here: 216 us
  waiting for transfers between devices  68.7 us (32%)
  Pallas kernels  56.3 us (26%)
  starting transfers between devices  50.6 us (23%)
  matrix products  22 us (10%)
  local copies, waits for them, and re-layouts  13 us (6%)
  other arithmetic  3.84 us (2%)
    pallas_call x8, Pallas kernels, forward_piece(): pl.pallas_call(functools.partial(forward_kernel, len(rows), width, per_ar...  20.2 us
    ppermute x5, starting transfers between devices, body(): arrived[t + 1] = lax.ppermute(both, 'dp', inward + outward)  19.4 us
    pallas_call x8, Pallas kernels, backward_piece(): pl.pallas_call(functools.partial(backward_kernel, len(rows), width, half...  17.7 us
    ppermute x1, waiting for transfers between devices, fetch_pair(): pairs[c] = lax.ppermute(sent, 'expert', [(i, i ^ r) for i in range(groups)])  13.3 us
    pallas_call x3, Pallas kernels, gradient_add(): pl.pallas_call(gradient_kernel, grid=(height // BLOCK,), in_specs=[pl.Blo...  12.3 us
    ppermute x3, waiting for transfers between devices, body(): spread_out[k] = lax.ppermute(total[k], 'dp', outward)  11.9 us
    ppermute x1, waiting for transfers between devices, body(): arrived[1] = lax.ppermute(part[1], 'dp', inward)  11.4 us
    ppermute x1, waiting for transfers between devices, body(): arrived[2] = lax.ppermute(part[2], 'dp', inward)  10.7 us
  transfers between devices with their start and end apart: 33, of which 11 were waited for; matrix products, arithmetic and copies ran while one was open for 11% of the time, Pallas kernels for 25%

profile of v3, /device:TPU:0, one launch (start us, length us, event | category | flops | bytes accessed | tf_op | source)
XLA Modules:
  0.0 216.0 jit_solution(12561134540634151561)
XLA Ops:
  4.1 2.6 %convolution_convert_fusion.6 = bf16[96,3712]{1,0:T(8,128)(2,1)} fusion(pred[8,96,192]{2,1,0:T(32,128)(4,1)S(1)} %get-tuple-element.263, bf16[192,3]{1,0:T(8,128)(2,1)S(1)} %copy.32, bf16[192,1792]{1,0:T(8,128)(2,1)} %param.8, bf16[192,1792]{1,0:T(8,128)(2,1)} %param.7), kind=kOutput, calls=%fused_computation.6 | convolution fusion | flops 142897152 | bytes 2162688 | tf_op jit(solution)/shard_map/dot_general | solution.py:287
  7.9 1.2 convolution_convert_fusion.5
  9.1 2.6 %collective-permute-start.3 = (bf16[96,3712]{1,0:T(8,128)(2,1)}, bf16[96,3712]{1,0:T(8,128)(2,1)S(1)}, u32[]{:S(2)}, u32[]{:S(2)}) collective-permute-start(bf16[96,3712]{1,0:T(8,128)(2,1)} %convolution_convert_fusion.5), channel_id=1, source_target_pairs={{0,3},{1,2},{2,1},{3,0},{4,7},{5,6},{6,5},{7,4},{8,11},{9,10},{10,... | collective-permute-start | bytes 2138120 | tf_op jit(solution)/shard_map/ppermute | solution.py:290
  11.7 1.2 convolution_convert_fusion.4
  12.9 1.1 collective-permute-start.4
  14.5 2.0 copy-done
  16.6 2.0 copy-done.2
  18.6 2.0 copy-done.4
  20.6 2.5 %shard_map.110 = (bf16[192,1536]{1,0:T(8,128)(2,1)S(1)}, bf16[192,1792]{1,0:T(8,128)(2,1)S(1)}, bf16[192,1792]{1,0:T(8,128)(2,1)S(1)}) custom-call(s32[2]{0:T(128)S(1)} %pad_add_fusion.scalars.middle_ref, bf16[96,3712]{1,0:T(8,128)(2,1)S(1)} %convolution_convert_fusion.3.refs_0_, bf16[96,3712]{1,0:T(8,128)(2,1)S(1)} %collective-permute-done.refs_1_, ...), custom_call_target="tpu_custom_call" | custom-call | flops 1 | bytes 1 | tf_op jit(solution)/shard_map/pallas_call | solution.py:84
  23.2 3.5 %collective-permute-start.2 = (bf16[192,1536]{1,0:T(8,128)(2,1)S(1)}, bf16[192,1536]{1,0:T(8,128)(2,1)S(1)}, u32[]{:S(2)}, u32[]{:S(2)}) collective-permute-start(bf16[192,1536]{1,0:T(8,128)(2,1)S(1)} %get-tuple-element.136.a_ref), channel_id=1, source_target_pairs={{0,8},{24,16},{1,9},{25,17},{2,10},{26,18},{3,11},{27,19},{4,12},{... | collective-permute-start | bytes 1769480 | tf_op jit(solution)/shard_map/ppermute | solution.py:480
  26.7 2.5 %shard_map.111.a_ref = bf16[192,1536]{1,0:T(8,128)(2,1)S(1)} custom-call(s32[2]{0:T(128)S(1)} %pad_add_fusion.scalars.middle_ref, bf16[96,3712]{1,0:T(8,128)(2,1)S(1)} %convolution_convert_fusion.3.refs_0_, bf16[96,3712]{1,0:T(8,128)(2,1)S(1)} %collective-permute-done.refs_1_, bf16[1,1792,1024]{2,1,0:T(8,128)(2,1)S(1)} %copy-done, ...), custom_call_target="tpu_custom_call" | custom-call | flops 1 | bytes 1 | tf_op jit(solution)/shard_map/pallas_call | solution.py:84
  29.8 10.0 %collective-permute-done.2.b_ref = bf16[192,1536]{1,0:T(8,128)(2,1)S(1)} collective-permute-done((bf16[192,1536]{1,0:T(8,128)(2,1)S(1)}, bf16[192,1536]{1,0:T(8,128)(2,1)S(1)}, u32[]{:S(2)}, u32[]{:S(2)}) %collective-permute-start.2) | collective-permute-done | bytes 589856 | tf_op jit(solution)/shard_map/ppermute | solution.py:480
  40.1 2.5 %shard_map.113 = (bf16[192,1536]{1,0:T(8,128)(2,1)S(1)}, bf16[192,1792]{1,0:T(8,128)(2,1)S(1)}, bf16[192,1792]{1,0:T(8,128)(2,1)S(1)}) custom-call(s32[2]{0:T(128)S(1)} %pad_add_fusion.scalars.middle_ref, bf16[96,3712]{1,0:T(8,128)(2,1)S(1)} %collective-permute-done.3.refs_0_, bf16[96,3712]{1,0:T(8,128)(2,1)S(1)} %collective-permute-done.4.refs_1_, ...), custom_call_target="tpu_custom_call" | custom-call | flops 1 | bytes 1 | tf_op jit(solution)/shard_map/pallas_call | solution.py:84
  43.2 4.4 %collective-permute-start.1 = (bf16[192,1536]{1,0:T(8,128)(2,1)S(1)}, bf16[192,1536]{1,0:T(8,128)(2,1)S(1)}, u32[]{:S(2)}, u32[]{:S(2)}) collective-permute-start(bf16[192,1536]{1,0:T(8,128)(2,1)S(1)} %shard_map.111.a_ref), channel_id=1, source_target_pairs={{0,8},{24,16},{1,9},{25,17},{2,10},{26,18},{3,11},{27,19},{4,12},{... | collective-permute-start | bytes 1769480 | tf_op jit(solution)/shard_map/ppermute | solution.py:482
  48.3 11.4 %collective-permute-done.1.b_ref = bf16[192,1536]{1,0:T(8,128)(2,1)S(1)} collective-permute-done((bf16[192,1536]{1,0:T(8,128)(2,1)S(1)}, bf16[192,1536]{1,0:T(8,128)(2,1)S(1)}, u32[]{:S(2)}, u32[]{:S(2)}) %collective-permute-start.1) | collective-permute-done | bytes 589856 | tf_op jit(solution)/shard_map/ppermute | solution.py:482
  59.9 2.5 %shard_map.115.other_ref.a_ref = bf16[192,1536]{1,0:T(8,128)(2,1)S(1)} custom-call(s32[2]{0:T(128)S(1)} %pad_add_fusion.scalars.middle_ref, bf16[96,3712]{1,0:T(8,128)(2,1)S(1)} %collective-permute-done.3.refs_0_, bf16[96,3712]{1,0:T(8,128)(2,1)S(1)} %collective-permute-done.4.refs_1_, bf16[1,1792,1024]{2,1,0:T(8,128)(2,1)S(1)} %copy-done.1, ...), custom_call_target="tpu_custom_call" | custom-call | flops 1 | bytes 1 | tf_op jit(solution)/shard_map/pallas_call | solution.py:84
  62.4 0.8 shard_map.116
  63.2 13.3 %collective-permute-done.7.refs_0_ = bf16[192,3712]{1,0:T(8,128)(2,1)S(1)} collective-permute-done((bf16[192,3712]{1,0:T(8,128)(2,1)S(1)}, bf16[192,3712]{1,0:T(8,128)(2,1)S(1)}, u32[]{:S(2)}, u32[]{:S(2)}) %collective-permute-start.7) | collective-permute-done | bytes 1425440 | tf_op jit(solution)/shard_map/ppermute | solution.py:415
  76.6 4.4 %collective-permute-start.6 = (bf16[192,1536]{1,0:T(8,128)(2,1)S(1)}, bf16[192,1536]{1,0:T(8,128)(2,1)S(1)}, u32[]{:S(2)}, u32[]{:S(2)}) collective-permute-start(bf16[192,1536]{1,0:T(8,128)(2,1)S(1)} %get-tuple-element.143.a_ref), channel_id=1, source_target_pairs={{0,8},{24,16},{1,9},{25,17},{2,10},{26,18},{3,11},{27,19},{4,12},{... | collective-permute-start | bytes 1769480 | tf_op jit(solution)/shard_map/ppermute | solution.py:492
  81.7 2.2 %collective-permute-start.11 = (bf16[192,1536]{1,0:T(8,128)(2,1)S(1)}, bf16[192,1536]{1,0:T(8,128)(2,1)S(1)}, u32[]{:S(2)}, u32[]{:S(2)}) collective-permute-start(bf16[192,1536]{1,0:T(8,128)(2,1)S(1)} %get-tuple-element.148), channel_id=1, source_target_pairs={{0,8},{24,16},{8,0},{16,24},{1,9},{25,17},{9,1},{17,25},{2,10},{26... | collective-permute-start | bytes 1769480 | tf_op jit(solution)/shard_map/ppermute | solution.py:499
  83.9 10.7 %collective-permute-done.6.b_ref = bf16[192,1536]{1,0:T(8,128)(2,1)S(1)} collective-permute-done((bf16[192,1536]{1,0:T(8,128)(2,1)S(1)}, bf16[192,1536]{1,0:T(8,128)(2,1)S(1)}, u32[]{:S(2)}, u32[]{:S(2)}) %collective-permute-start.6) | collective-permute-done | bytes 589856 | tf_op jit(solution)/shard_map/ppermute | solution.py:492
  94.8 0.8 collective-permute-start.13
  95.6 2.5 %shard_map.118 = (bf16[192,1536]{1,0:T(8,128)(2,1)S(1)}, bf16[192,1792]{1,0:T(8,128)(2,1)S(1)}, bf16[192,1792]{1,0:T(8,128)(2,1)S(1)}) custom-call(s32[2]{0:T(128)S(1)} %pad_add_fusion.scalars.middle_ref, bf16[192,3712]{1,0:T(8,128)(2,1)S(1)} %collective-permute-done.7.refs_0_, bf16[96,3712]{1,0:T(8,128)(2,1)S(1)} %collective-permute-done.9.refs_1_, ...), custom_call_target="tpu_custom_call" | custom-call | flops 1 | bytes 1 | tf_op jit(solution)/shard_map/pallas_call | solution.py:84
  99.0 5.3 %collective-permute-start.10 = (bf16[192,1536]{1,0:T(8,128)(2,1)S(1)}, bf16[192,1536]{1,0:T(8,128)(2,1)S(1)}, u32[]{:S(2)}, u32[]{:S(2)}) collective-permute-start(bf16[192,1536]{1,0:T(8,128)(2,1)S(1)} %get-tuple-element.158), channel_id=1, source_target_pairs={{0,8},{24,16},{8,0},{16,24},{1,9},{25,17},{9,1},{17,25},{2,10},{26... | collective-permute-start | bytes 1769480 | tf_op jit(solution)/shard_map/ppermute | solution.py:499
  104.3 1.2 convolution_convert_fusion.2
  105.6 1.2 convolution_convert_fusion.1
  107.9 0.9 collective-permute-start.12
  108.8 2.5 %shard_map.121.other_ref.a_ref = bf16[192,1536]{1,0:T(8,128)(2,1)S(1)} custom-call(s32[2]{0:T(128)S(1)} %pad_add_fusion.scalars.middle_ref, bf16[192,3712]{1,0:T(8,128)(2,1)S(1)} %collective-permute-done.7.refs_0_, bf16[96,3712]{1,0:T(8,128)(2,1)S(1)} %collective-permute-done.9.refs_1_, bf16[1,1792,1024]{2,1,0:T(8,128)(2,1)S(1)} %copy-done.1, ...), custom_call_target="tpu_custom_call" | custom-call | flops 1 | bytes 1 | tf_op jit(solution)/shard_map/pallas_call | solution.py:84
  112.2 4.8 %collective-permute-start.18 = (bf16[192,1536]{1,0:T(8,128)(2,1)S(1)}, bf16[192,1536]{1,0:T(8,128)(2,1)S(1)}, u32[]{:S(2)}, u32[]{:S(2)}) collective-permute-start(bf16[192,1536]{1,0:T(8,128)(2,1)S(1)} %get-tuple-element.165), channel_id=1, source_target_pairs={{0,8},{24,16},{8,0},{16,24},{1,9},{25,17},{9,1},{17,25},{2,10},{26... | collective-permute-start | bytes 1769480 | tf_op jit(solution)/shard_map/ppermute | solution.py:499
  117.0 2.1 shard_map.123
  119.1 0.8 collective-permute-done.10.b_ref.came_ref
  120.7 2.9 %collective-permute-done.15.refs_1_ = bf16[96,3712]{1,0:T(8,128)(2,1)S(1)} collective-permute-done((bf16[96,3712]{1,0:T(8,128)(2,1)}, bf16[96,3712]{1,0:T(8,128)(2,1)S(1)}, u32[]{:S(2)}, u32[]{:S(2)}) %collective-permute-start.15) | collective-permute-done | bytes 712736 | tf_op jit(solution)/shard_map/ppermute | solution.py:290
  123.8 2.5 %shard_map.125 = (bf16[192,1536]{1,0:T(8,128)(2,1)S(1)}, bf16[192,1792]{1,0:T(8,128)(2,1)S(1)}, bf16[192,1792]{1,0:T(8,128)(2,1)S(1)}) custom-call(s32[2]{0:T(128)S(1)} %pad_add_fusion.scalars.middle_ref, bf16[96,3712]{1,0:T(8,128)(2,1)S(1)} %collective-permute-done.14.refs_0_, bf16[96,3712]{1,0:T(8,128)(2,1)S(1)} %collective-permute-done.15.refs_1_, ...), custom_call_target="tpu_custom_call" | custom-call | flops 1 | bytes 1 | tf_op jit(solution)/shard_map/pallas_call | solution.py:84
  126.3 1.6 shard_map.126
  127.9 2.2 %collective-permute-start.17 = (bf16[192,1536]{1,0:T(8,128)(2,1)}, bf16[192,1536]{1,0:T(8,128)(2,1)S(1)}, u32[]{:S(2)}, u32[]{:S(2)}) collective-permute-start(bf16[192,1536]{1,0:T(8,128)(2,1)} %get-tuple-element.174), channel_id=1, source_target_pairs={{0,8},{24,16},{8,0},{16,24},{1,9},{25,17},{9,1},{17,25},{2,10},{26... | collective-permute-start | bytes 1769480 | tf_op jit(solution)/shard_map/ppermute | solution.py:499
  130.1 2.9 %shard_map.127 = (bf16[192,1024]{1,0:T(8,128)(2,1)S(1)}, bf16[192,1024]{1,0:T(8,128)(2,1)S(1)}, bf16[192,1024]{1,0:T(8,128)(2,1)S(1)}, bf16[96,1920]{1,0:T(8,128)(2,1)S(1)}, bf16[96,1920]{1,0:T(8,128)(2,1)}) custom-call(s32[2]{0:T(128)S(1)} %pad_add_fusion.scalars.middle_ref, ...), custom_call_target="tpu_custom_call", output_to_operand_aliasing={{0}: (9, {}), {1}: (10, {}), {2}: (11, {})} | custom-call | flops 1 | bytes 1 | tf_op jit(solution)/shard_map/pallas_call | solution.py:196
  133.9 2.5 %shard_map.129.other_ref.a_ref = bf16[192,1536]{1,0:T(8,128)(2,1)S(1)} custom-call(s32[2]{0:T(128)S(1)} %pad_add_fusion.scalars.middle_ref, bf16[96,3712]{1,0:T(8,128)(2,1)S(1)} %collective-permute-done.14.refs_0_, bf16[96,3712]{1,0:T(8,128)(2,1)S(1)} %collective-permute-done.15.refs_1_, bf16[1,1792,1024]{2,1,0:T(8,128)(2,1)S(1)} %copy-done.1, ...), custom_call_target="tpu_custom_call" | custom-call | flops 1 | bytes 1 | tf_op jit(solution)/shard_map/pallas_call | solution.py:84
  136.4 0.8 shard_map.130
  137.2 4.9 %collective-permute-start.23 = (bf16[192,1536]{1,0:T(8,128)(2,1)S(1)}, bf16[192,1536]{1,0:T(8,128)(2,1)S(1)}, u32[]{:S(2)}, u32[]{:S(2)}) collective-permute-start(bf16[192,1536]{1,0:T(8,128)(2,1)S(1)} %get-tuple-element.187), channel_id=1, source_target_pairs={{0,8},{24,16},{8,0},{16,24},{1,9},{25,17},{9,1},{17,25},{2,10},{26... | collective-permute-start | bytes 1769480 | tf_op jit(solution)/shard_map/ppermute | solution.py:499
  142.0 0.9 constant_dynamic-update-slice_fusion.2
  142.9 2.1 shard_map.131
  146.3 1.3 collective-permute-start.25
  147.6 2.1 shard_map.134
  150.2 7.2 %collective-permute-done.23.b_ref.came_ref = bf16[192,1536]{1,0:T(8,128)(2,1)S(1)} collective-permute-done((bf16[192,1536]{1,0:T(8,128)(2,1)S(1)}, bf16[192,1536]{1,0:T(8,128)(2,1)S(1)}, u32[]{:S(2)}, u32[]{:S(2)}) %collective-permute-start.23) | collective-permute-done | bytes 589856 | tf_op jit(solution)/shard_map/ppermute | solution.py:499
  159.5 1.5 collective-permute-start.30
  161.0 2.1 shard_map.137
  163.1 6.0 %collective-permute-done.25.came_ref = bf16[192,1536]{1,0:T(8,128)(2,1)S(1)} collective-permute-done((bf16[192,1536]{1,0:T(8,128)(2,1)S(1)}, bf16[192,1536]{1,0:T(8,128)(2,1)S(1)}, u32[]{:S(2)}, u32[]{:S(2)}) %collective-permute-start.25) | collective-permute-done | bytes 589856 | tf_op jit(solution)/shard_map/ppermute | solution.py:503
  169.0 2.1 shard_map.138
  171.4 0.9 collective-permute-start.27
  172.4 1.3 collective-permute-start.29
  175.3 3.3 %convolution_convert_fusion.9.before_ref = bf16[1024,1792]{1,0:T(8,128)(2,1)S(1)} fusion(bf16[576,1024]{1,0:T(8,128)(2,1)S(1)} %pad_maximum_fusion, bf16[192,1792]{1,0:T(8,128)(2,1)S(1)} %copy-done.13, bf16[192,1792]{1,0:T(8,128)(2,1)S(1)} %copy-done.11, bf16[192,1792]{1,0:T(8,128)(2,1)S(1)} %copy-done.9), kind=kOutput, calls=%fused_computation.9 | convolution fusion | flops 2121957376 | bytes 6914048 | tf_op jit(solution)/shard_map/dot_general | solution.py:374
  178.6 3.3 %convolution_convert_fusion.8.before_ref = bf16[1792,1024]{1,0:T(8,128)(2,1)S(1)} fusion(bf16[576,1792]{1,0:T(8,128)(2,1)S(1)} %copy-done.17, bf16[192,1024]{1,0:T(8,128)(2,1)S(1)} %get-tuple-element.229, bf16[192,1024]{1,0:T(8,128)(2,1)S(1)} %get-tuple-element.228, bf16[192,1024]{1,0:T(8,128)(2,1)S(1)} %get-tuple-element.227), kind=kOutput, calls=%fused_computation.8 | convolution fusion | flops 2119303168 | bytes 6914048 | tf_op jit(solution)/shard_map/dot_general | solution.py:374
  182.0 3.3 %convolution_convert_fusion.7.before_ref = bf16[1792,1024]{1,0:T(8,128)(2,1)S(1)} fusion(bf16[576,1792]{1,0:T(8,128)(2,1)S(1)} %copy-done.17, bf16[192,1024]{1,0:T(8,128)(2,1)S(1)} %get-tuple-element.233, bf16[192,1024]{1,0:T(8,128)(2,1)S(1)} %copy-done.7, bf16[192,1024]{1,0:T(8,128)(2,1)S(1)} %get-tuple-element.231), kind=kOutput, calls=%fused_computation.7 | convolution fusion | flops 2119303168 | bytes 6914048 | tf_op jit(solution)/shard_map/dot_general | solution.py:374
  185.4 2.1 shard_map.140
  187.5 6.0 %collective-permute-done.29.came_ref = bf16[192,1536]{1,0:T(8,128)(2,1)S(1)} collective-permute-done((bf16[192,1536]{1,0:T(8,128)(2,1)S(1)}, bf16[192,1536]{1,0:T(8,128)(2,1)S(1)}, u32[]{:S(2)}, u32[]{:S(2)}) %collective-permute-start.29) | collective-permute-done | bytes 589856 | tf_op jit(solution)/shard_map/ppermute | solution.py:503
  193.4 2.1 shard_map.141
  196.1 1.0 slice.118
  197.1 1.0 slice.119
  198.9 1.5 convolution_add_fusion.1
  200.4 3.3 %shard_map.142 = bf16[1024,1792]{1,0:T(8,128)(2,1)} custom-call(bf16[192,1024]{1,0:T(8,128)(2,1)S(1)} %get-tuple-element.249.left_ref, bf16[192,1792]{1,0:T(8,128)(2,1)S(1)} %get-tuple-element.250.right_ref, bf16[1024,1792]{1,0:T(8,128)(2,1)S(1)} %convolution_convert_fusion.9.before_ref), custom_call_target="tpu_custom_call" | custom-call | flops 1 | bytes 1 | tf_op jit(solution)/shard_map/pallas_call | solution.py:219
  203.6 4.5 %shard_map.143 = bf16[1792,1024]{1,0:T(8,128)(2,1)} custom-call(bf16[192,1792]{1,0:T(8,128)(2,1)S(1)} %get-tuple-element.253.left_ref, bf16[192,1024]{1,0:T(8,128)(2,1)S(1)} %get-tuple-element.252.right_ref, bf16[1792,1024]{1,0:T(8,128)(2,1)S(1)} %convolution_convert_fusion.8.before_ref), custom_call_target="tpu_custom_call" | custom-call | flops 1 | bytes 1 | tf_op jit(solution)/shard_map/pallas_call | solution.py:219
  208.2 4.5 %shard_map.144 = bf16[1792,1024]{1,0:T(8,128)(2,1)} custom-call(bf16[192,1792]{1,0:T(8,128)(2,1)S(1)} %get-tuple-element.253.left_ref, bf16[192,1024]{1,0:T(8,128)(2,1)S(1)} %get-tuple-element.254.right_ref, bf16[1792,1024]{1,0:T(8,128)(2,1)S(1)} %convolution_convert_fusion.7.before_ref), custom_call_target="tpu_custom_call" | custom-call | flops 1 | bytes 1 | tf_op jit(solution)/shard_map/pallas_call | solution.py:219
  212.7 1.0 slice_reduce_fusion
  214.8 1.2 fusion.1
  (164 shorter events, 20.7 us)
Async XLA Ops:
  4.1 3.8 %copy-start.32 = (bf16[192,1792]{1,0:T(8,128)(2,1)S(1)}, bf16[192,1792]{1,0:T(8,128)(2,1)}, u32[]{:S(2)}) copy-start(bf16[192,1792]{1,0:T(8,128)(2,1)} %param.8) | copy-start | bytes 2064388
  4.1 3.8 %copy-start.35 = (bf16[192,1792]{1,0:T(8,128)(2,1)S(1)}, bf16[192,1792]{1,0:T(8,128)(2,1)}, u32[]{:S(2)}) copy-start(bf16[192,1792]{1,0:T(8,128)(2,1)} %param.7) | copy-start | bytes 2064388
  6.7 7.8 %collective-permute-start = (bf16[96,3712]{1,0:T(8,128)(2,1)}, bf16[96,3712]{1,0:T(8,128)(2,1)S(1)}, u32[]{:S(2)}, u32[]{:S(2)}) collective-permute-start(bf16[96,3712]{1,0:T(8,128)(2,1)} %convolution_convert_fusion.6), channel_id=1, source_target_pairs={{0,1},{1,0},{2,3},{3,2},{4,5},{5,4},{6,7},{7,6},{8,9},{9,8},{10,11... | collective-permute-start | bytes 2138120 | tf_op jit(solution)/shard_map/ppermute | solution.py:290
  7.8 3.9 %copy-start.22 = (bf16[96,192]{1,0:T(8,128)(2,1)}, bf16[96,192]{1,0:T(8,128)(2,1)S(1)}, u32[]{:S(2)}) copy-start(bf16[96,192]{1,0:T(8,128)(2,1)S(1)} %get-tuple-element.131) | copy-start | bytes 110596
  7.8 6.2 %copy-start.29 = (bf16[96,192]{1,0:T(8,128)(2,1)}, bf16[96,192]{1,0:T(8,128)(2,1)S(1)}, u32[]{:S(2)}) copy-start(bf16[96,192]{1,0:T(8,128)(2,1)S(1)} %get-tuple-element.132) | copy-start | bytes 110596
  7.8 96.5 %copy-start.24 = (bf16[96,192]{1,0:T(8,128)(2,1)}, bf16[96,192]{1,0:T(8,128)(2,1)S(1)}, u32[]{:S(2)}) copy-start(bf16[96,192]{1,0:T(8,128)(2,1)S(1)} %get-tuple-element.159) | copy-start | bytes 110596
  7.9 97.7 %copy-start.26 = (bf16[96,192]{1,0:T(8,128)(2,1)}, bf16[96,192]{1,0:T(8,128)(2,1)S(1)}, u32[]{:S(2)}) copy-start(bf16[96,192]{1,0:T(8,128)(2,1)S(1)} %get-tuple-element.160) | copy-start | bytes 110596
  9.1 30.9 %collective-permute-start.3 = (bf16[96,3712]{1,0:T(8,128)(2,1)}, bf16[96,3712]{1,0:T(8,128)(2,1)S(1)}, u32[]{:S(2)}, u32[]{:S(2)}) collective-permute-start(bf16[96,3712]{1,0:T(8,128)(2,1)} %convolution_convert_fusion.5), channel_id=1, source_target_pairs={{0,3},{1,2},{2,1},{3,0},{4,7},{5,6},{6,5},{7,4},{8,11},{9,10},{10,... | collective-permute-start | bytes 2138120 | tf_op jit(solution)/shard_map/ppermute | solution.py:290
  12.9 27.1 %collective-permute-start.4 = (bf16[96,3712]{1,0:T(8,128)(2,1)}, bf16[96,3712]{1,0:T(8,128)(2,1)S(1)}, u32[]{:S(2)}, u32[]{:S(2)}) collective-permute-start(bf16[96,3712]{1,0:T(8,128)(2,1)} %convolution_convert_fusion.4), channel_id=1, source_target_pairs={{0,5},{1,4},{2,7},{3,6},{4,1},{5,0},{6,3},{7,2},{8,13},{9,12},{10,... | collective-permute-start | bytes 2138120 | tf_op jit(solution)/shard_map/ppermute | solution.py:290
  14.5 2.0 copy-start
  16.6 2.0 copy-start.2
  23.1 6.1 %copy-start.8 = (bf16[192,1792]{1,0:T(8,128)(2,1)}, bf16[192,1792]{1,0:T(8,128)(2,1)S(1)}, u32[]{:S(2)}) copy-start(bf16[192,1792]{1,0:T(8,128)(2,1)S(1)} %get-tuple-element.223) | copy-start | bytes 2064388
  23.2 16.7 %collective-permute-start.2 = (bf16[192,1536]{1,0:T(8,128)(2,1)S(1)}, bf16[192,1536]{1,0:T(8,128)(2,1)S(1)}, u32[]{:S(2)}, u32[]{:S(2)}) collective-permute-start(bf16[192,1536]{1,0:T(8,128)(2,1)S(1)} %get-tuple-element.136.a_ref), channel_id=1, source_target_pairs={{0,8},{24,16},{1,9},{25,17},{2,10},{26,18},{3,11},{27,19},{4,12},{... | collective-permute-start | bytes 1769480 | tf_op jit(solution)/shard_map/ppermute | solution.py:480
  26.7 2.6 %copy-start.33 = (bf16[192,1792]{1,0:T(8,128)(2,1)S(1)}, bf16[192,1792]{1,0:T(8,128)(2,1)}, u32[]{:S(2)}) copy-start(bf16[192,1792]{1,0:T(8,128)(2,1)} %param.8) | copy-start | bytes 2064388
  26.7 2.6 %copy-start.36 = (bf16[192,1792]{1,0:T(8,128)(2,1)S(1)}, bf16[192,1792]{1,0:T(8,128)(2,1)}, u32[]{:S(2)}) copy-start(bf16[192,1792]{1,0:T(8,128)(2,1)} %param.7) | copy-start | bytes 2064388
  26.7 13.3 %copy-start.5 = (bf16[1,1024,1792]{2,1,0:T(8,128)(2,1)S(1)}, bf16[1,1024,1792]{2,1,0:T(8,128)(2,1)}, u32[]{:S(2)}) copy-start(bf16[1,1024,1792]{2,1,0:T(8,128)(2,1)} %refs_4_.15) | copy-start | bytes 11010052
  29.3 10.8 %copy-start.1 = (bf16[1,1792,1024]{2,1,0:T(8,128)(2,1)S(1)}, bf16[1,1792,1024]{2,1,0:T(8,128)(2,1)}, u32[]{:S(2)}) copy-start(bf16[1,1792,1024]{2,1,0:T(8,128)(2,1)} %refs_2_.31) | copy-start | bytes 11010052
  29.3 10.8 %copy-start.3 = (bf16[1,1792,1024]{2,1,0:T(8,128)(2,1)S(1)}, bf16[1,1792,1024]{2,1,0:T(8,128)(2,1)}, u32[]{:S(2)}) copy-start(bf16[1,1792,1024]{2,1,0:T(8,128)(2,1)} %refs_3_.31) | copy-start | bytes 11010052
  42.6 19.8 %copy-start.10 = (bf16[192,1792]{1,0:T(8,128)(2,1)}, bf16[192,1792]{1,0:T(8,128)(2,1)S(1)}, u32[]{:S(2)}) copy-start(bf16[192,1792]{1,0:T(8,128)(2,1)S(1)} %get-tuple-element.224) | copy-start | bytes 2064388
  42.6 33.8 %collective-permute-start.7 = (bf16[192,3712]{1,0:T(8,128)(2,1)S(1)}, bf16[192,3712]{1,0:T(8,128)(2,1)S(1)}, u32[]{:S(2)}, u32[]{:S(2)}) collective-permute-start(bf16[192,3712]{1,0:T(8,128)(2,1)S(1)} %convolution_convert_fusion), channel_id=1, source_target_pairs={{0,6},{1,7},{2,4},{3,5},{4,2},{5,3},{6,0},{7,1},{8,14},{9,15},{10,... | collective-permute-start | bytes 4276232 | tf_op jit(solution)/shard_map/ppermute | solution.py:415
  43.2 16.6 %collective-permute-start.1 = (bf16[192,1536]{1,0:T(8,128)(2,1)S(1)}, bf16[192,1536]{1,0:T(8,128)(2,1)S(1)}, u32[]{:S(2)}, u32[]{:S(2)}) collective-permute-start(bf16[192,1536]{1,0:T(8,128)(2,1)S(1)} %shard_map.111.a_ref), channel_id=1, source_target_pairs={{0,8},{24,16},{1,9},{25,17},{2,10},{26,18},{3,11},{27,19},{4,12},{... | collective-permute-start | bytes 1769480 | tf_op jit(solution)/shard_map/ppermute | solution.py:482
  47.6 14.8 %collective-permute-start.8 = (bf16[192,1536]{1,0:T(8,128)(2,1)S(1)}, bf16[192,1536]{1,0:T(8,128)(2,1)S(1)}, u32[]{:S(2)}, u32[]{:S(2)}) collective-permute-start(bf16[192,1536]{1,0:T(8,128)(2,1)S(1)} %shard_map.112.a_ref), channel_id=1, source_target_pairs={{8,16},{16,8},{9,17},{17,9},{10,18},{18,10},{11,19},{19,11},{12,20... | collective-permute-start | bytes 1769480 | tf_op jit(solution)/shard_map/ppermute | solution.py:488
  76.5 19.1 %collective-permute-start.9 = (bf16[96,3712]{1,0:T(8,128)(2,1)S(1)}, bf16[96,3712]{1,0:T(8,128)(2,1)S(1)}, u32[]{:S(2)}, u32[]{:S(2)}) collective-permute-start(bf16[96,3712]{1,0:T(8,128)(2,1)S(1)} %slice.109), channel_id=1, source_target_pairs={{0,1},{1,0},{2,3},{3,2},{4,5},{5,4},{6,7},{7,6},{8,9},{9,8},{10,11... | collective-permute-start | bytes 2138120 | tf_op jit(solution)/shard_map/ppermute | solution.py:427
  76.6 18.0 %collective-permute-start.6 = (bf16[192,1536]{1,0:T(8,128)(2,1)S(1)}, bf16[192,1536]{1,0:T(8,128)(2,1)S(1)}, u32[]{:S(2)}, u32[]{:S(2)}) collective-permute-start(bf16[192,1536]{1,0:T(8,128)(2,1)S(1)} %get-tuple-element.143.a_ref), channel_id=1, source_target_pairs={{0,8},{24,16},{1,9},{25,17},{2,10},{26,18},{3,11},{27,19},{4,12},{... | collective-permute-start | bytes 1769480 | tf_op jit(solution)/shard_map/ppermute | solution.py:492
  81.0 17.2 %collective-permute-start.5 = (bf16[192,1536]{1,0:T(8,128)(2,1)S(1)}, bf16[192,1536]{1,0:T(8,128)(2,1)S(1)}, u32[]{:S(2)}, u32[]{:S(2)}) collective-permute-start(bf16[192,1536]{1,0:T(8,128)(2,1)S(1)} %shard_map.114.a_ref), channel_id=1, source_target_pairs={{8,16},{16,8},{9,17},{17,9},{10,18},{18,10},{11,19},{19,11},{12,20... | collective-permute-start | bytes 1769480 | tf_op jit(solution)/shard_map/ppermute | solution.py:488
  81.7 26.1 %collective-permute-start.11 = (bf16[192,1536]{1,0:T(8,128)(2,1)S(1)}, bf16[192,1536]{1,0:T(8,128)(2,1)S(1)}, u32[]{:S(2)}, u32[]{:S(2)}) collective-permute-start(bf16[192,1536]{1,0:T(8,128)(2,1)S(1)} %get-tuple-element.148), channel_id=1, source_target_pairs={{0,8},{24,16},{8,0},{16,24},{1,9},{25,17},{9,1},{17,25},{2,10},{26... | collective-permute-start | bytes 1769480 | tf_op jit(solution)/shard_map/ppermute | solution.py:499
  94.8 9.6 %copy-start.34 = (bf16[192,1792]{1,0:T(8,128)(2,1)S(1)}, bf16[192,1792]{1,0:T(8,128)(2,1)}, u32[]{:S(2)}) copy-start(bf16[192,1792]{1,0:T(8,128)(2,1)} %param.8) | copy-start | bytes 2064388
  94.8 9.6 %copy-start.37 = (bf16[192,1792]{1,0:T(8,128)(2,1)S(1)}, bf16[192,1792]{1,0:T(8,128)(2,1)}, u32[]{:S(2)}) copy-start(bf16[192,1792]{1,0:T(8,128)(2,1)} %param.7) | copy-start | bytes 2064388
  94.8 16.6 %collective-permute-start.13 = (bf16[192,1536]{1,0:T(8,128)(2,1)S(1)}, bf16[192,1536]{1,0:T(8,128)(2,1)S(1)}, u32[]{:S(2)}, u32[]{:S(2)}) collective-permute-start(bf16[192,1536]{1,0:T(8,128)(2,1)S(1)} %shard_map.117.a_ref), channel_id=1, source_target_pairs={{8,16},{16,8},{9,17},{17,9},{10,18},{18,10},{11,19},{19,11},{12,20... | collective-permute-start | bytes 1769480 | tf_op jit(solution)/shard_map/ppermute | solution.py:488
  99.0 20.9 %collective-permute-start.10 = (bf16[192,1536]{1,0:T(8,128)(2,1)S(1)}, bf16[192,1536]{1,0:T(8,128)(2,1)S(1)}, u32[]{:S(2)}, u32[]{:S(2)}) collective-permute-start(bf16[192,1536]{1,0:T(8,128)(2,1)S(1)} %get-tuple-element.158), channel_id=1, source_target_pairs={{0,8},{24,16},{8,0},{16,24},{1,9},{25,17},{9,1},{17,25},{2,10},{26... | collective-permute-start | bytes 1769480 | tf_op jit(solution)/shard_map/ppermute | solution.py:499
  106.8 16.8 %collective-permute-start.15 = (bf16[96,3712]{1,0:T(8,128)(2,1)}, bf16[96,3712]{1,0:T(8,128)(2,1)S(1)}, u32[]{:S(2)}, u32[]{:S(2)}) collective-permute-start(bf16[96,3712]{1,0:T(8,128)(2,1)} %convolution_convert_fusion.1), channel_id=1, source_target_pairs={{0,4},{1,5},{2,6},{3,7},{4,0},{5,1},{6,2},{7,3},{8,12},{9,13},{10,... | collective-permute-start | bytes 2138120 | tf_op jit(solution)/shard_map/ppermute | solution.py:290
  107.3 16.5 %collective-permute-start.14 = (bf16[96,3712]{1,0:T(8,128)(2,1)}, bf16[96,3712]{1,0:T(8,128)(2,1)S(1)}, u32[]{:S(2)}, u32[]{:S(2)}) collective-permute-start(bf16[96,3712]{1,0:T(8,128)(2,1)} %convolution_convert_fusion.2), channel_id=1, source_target_pairs={{0,2},{1,3},{2,0},{3,1},{4,6},{5,7},{6,4},{7,5},{8,10},{9,11},{10,... | collective-permute-start | bytes 2138120 | tf_op jit(solution)/shard_map/ppermute | solution.py:290
  107.9 18.4 %collective-permute-start.12 = (bf16[192,1536]{1,0:T(8,128)(2,1)S(1)}, bf16[192,1536]{1,0:T(8,128)(2,1)S(1)}, u32[]{:S(2)}, u32[]{:S(2)}) collective-permute-start(bf16[192,1536]{1,0:T(8,128)(2,1)S(1)} %shard_map.120.a_ref), channel_id=1, source_target_pairs={{8,16},{16,8},{9,17},{17,9},{10,18},{18,10},{11,19},{19,11},{12,20... | collective-permute-start | bytes 1769480 | tf_op jit(solution)/shard_map/ppermute | solution.py:488
  112.2 20.9 %collective-permute-start.18 = (bf16[192,1536]{1,0:T(8,128)(2,1)S(1)}, bf16[192,1536]{1,0:T(8,128)(2,1)S(1)}, u32[]{:S(2)}, u32[]{:S(2)}) collective-permute-start(bf16[192,1536]{1,0:T(8,128)(2,1)S(1)} %get-tuple-element.165), channel_id=1, source_target_pairs={{0,8},{24,16},{8,0},{16,24},{1,9},{25,17},{9,1},{17,25},{2,10},{26... | collective-permute-start | bytes 1769480 | tf_op jit(solution)/shard_map/ppermute | solution.py:499
  120.0 16.4 %collective-permute-start.20 = (bf16[192,1536]{1,0:T(8,128)(2,1)S(1)}, bf16[192,1536]{1,0:T(8,128)(2,1)S(1)}, u32[]{:S(2)}, u32[]{:S(2)}) collective-permute-start(bf16[192,1536]{1,0:T(8,128)(2,1)S(1)} %shard_map.124.a_ref), channel_id=1, source_target_pairs={{8,16},{16,8},{9,17},{17,9},{10,18},{18,10},{11,19},{19,11},{12,20... | collective-permute-start | bytes 1769480 | tf_op jit(solution)/shard_map/ppermute | solution.py:488
  127.9 17.4 %collective-permute-start.17 = (bf16[192,1536]{1,0:T(8,128)(2,1)}, bf16[192,1536]{1,0:T(8,128)(2,1)S(1)}, u32[]{:S(2)}, u32[]{:S(2)}) collective-permute-start(bf16[192,1536]{1,0:T(8,128)(2,1)} %get-tuple-element.174), channel_id=1, source_target_pairs={{0,8},{24,16},{8,0},{16,24},{1,9},{25,17},{9,1},{17,25},{2,10},{26... | collective-permute-start | bytes 1769480 | tf_op jit(solution)/shard_map/ppermute | solution.py:499
  133.2 13.0 %collective-permute-start.19 = (bf16[192,1536]{1,0:T(8,128)(2,1)S(1)}, bf16[192,1536]{1,0:T(8,128)(2,1)S(1)}, u32[]{:S(2)}, u32[]{:S(2)}) collective-permute-start(bf16[192,1536]{1,0:T(8,128)(2,1)S(1)} %shard_map.128.a_ref), channel_id=1, source_target_pairs={{8,16},{16,8},{9,17},{17,9},{10,18},{18,10},{11,19},{19,11},{12,20... | collective-permute-start | bytes 1769480 | tf_op jit(solution)/shard_map/ppermute | solution.py:488
  137.2 20.2 %collective-permute-start.23 = (bf16[192,1536]{1,0:T(8,128)(2,1)S(1)}, bf16[192,1536]{1,0:T(8,128)(2,1)S(1)}, u32[]{:S(2)}, u32[]{:S(2)}) collective-permute-start(bf16[192,1536]{1,0:T(8,128)(2,1)S(1)} %get-tuple-element.187), channel_id=1, source_target_pairs={{0,8},{24,16},{8,0},{16,24},{1,9},{25,17},{9,1},{17,25},{2,10},{26... | collective-permute-start | bytes 1769480 | tf_op jit(solution)/shard_map/ppermute | solution.py:499
  142.0 7.7 %collective-permute-start.16 = (bf16[96,1920]{1,0:T(8,128)(2,1)}, bf16[96,1920]{1,0:T(8,128)(2,1)S(1)}, u32[]{:S(2)}, u32[]{:S(2)}) collective-permute-start(bf16[96,1920]{1,0:T(8,128)(2,1)} %get-tuple-element.181), channel_id=1, source_target_pairs={{0,1},{1,0},{2,3},{3,2},{4,5},{5,4},{6,7},{7,6},{8,9},{9,8},{10,11... | collective-permute-start | bytes 1105928 | tf_op jit(solution)/shard_map/ppermute | solution.py:465
  145.4 13.9 %collective-permute-start.26 = (bf16[192,1536]{1,0:T(8,128)(2,1)S(1)}, bf16[192,1536]{1,0:T(8,128)(2,1)S(1)}, u32[]{:S(2)}, u32[]{:S(2)}) collective-permute-start(bf16[192,1536]{1,0:T(8,128)(2,1)S(1)} %shard_map.132.a_ref), channel_id=1, source_target_pairs={{8,16},{16,8},{9,17},{17,9},{10,18},{18,10},{11,19},{19,11},{12,20... | collective-permute-start | bytes 1769480 | tf_op jit(solution)/shard_map/ppermute | solution.py:488
  146.3 22.8 %collective-permute-start.25 = (bf16[192,1536]{1,0:T(8,128)(2,1)S(1)}, bf16[192,1536]{1,0:T(8,128)(2,1)S(1)}, u32[]{:S(2)}, u32[]{:S(2)}) collective-permute-start(bf16[192,1536]{1,0:T(8,128)(2,1)S(1)} %shard_map.133.own_ref), channel_id=1, source_target_pairs={{8,0},{16,24},{9,1},{17,25},{10,2},{18,26},{11,3},{19,27},{12,4},{... | collective-permute-start | bytes 1769480 | tf_op jit(solution)/shard_map/ppermute | solution.py:503
  147.6 2.3 %copy-start.28 = (bf16[96,192]{1,0:T(8,128)(2,1)S(1)}, bf16[96,192]{1,0:T(8,128)(2,1)}, u32[]{:S(2)}) copy-start(bf16[96,192]{1,0:T(8,128)(2,1)} %get-tuple-element.261) | copy-start | bytes 110596
  147.6 2.3 %copy-start.30 = (bf16[96,192]{1,0:T(8,128)(2,1)S(1)}, bf16[96,192]{1,0:T(8,128)(2,1)}, u32[]{:S(2)}) copy-start(bf16[96,192]{1,0:T(8,128)(2,1)} %copy-done.29) | copy-start | bytes 110596
  149.7 7.8 %copy-start.6 = (bf16[192,1024]{1,0:T(8,128)(2,1)}, bf16[192,1024]{1,0:T(8,128)(2,1)S(1)}, u32[]{:S(2)}) copy-start(bf16[192,1024]{1,0:T(8,128)(2,1)S(1)} %get-tuple-element.232) | copy-start | bytes 1179652
  149.8 8.4 %copy-start.15 = (bf16[576,1792]{1,0:T(8,128)(2,1)S(1)}, bf16[576,1792]{1,0:T(8,128)(2,1)}, u32[]{:S(2)}) copy-start(bf16[576,1792]{1,0:T(8,128)(2,1)} %constant_dynamic-update-slice_fusion.2) | copy-start | bytes 6193156
  157.6 13.8 %collective-permute-start.24 = (bf16[192,1536]{1,0:T(8,128)(2,1)S(1)}, bf16[192,1536]{1,0:T(8,128)(2,1)S(1)}, u32[]{:S(2)}, u32[]{:S(2)}) collective-permute-start(bf16[192,1536]{1,0:T(8,128)(2,1)S(1)} %shard_map.135.a_ref), channel_id=1, source_target_pairs={{8,16},{16,8},{9,17},{17,9},{10,18},{18,10},{11,19},{19,11},{12,20... | collective-permute-start | bytes 1769480 | tf_op jit(solution)/shard_map/ppermute | solution.py:488
  158.3 15.4 %collective-permute-start.21 = (bf16[96,1920]{1,0:T(8,128)(2,1)S(1)}, bf16[96,1920]{1,0:T(8,128)(2,1)S(1)}, u32[]{:S(2)}, u32[]{:S(2)}) collective-permute-start(bf16[96,1920]{1,0:T(8,128)(2,1)S(1)} %get-tuple-element.197), channel_id=1, source_target_pairs={{0,3},{1,2},{2,1},{3,0},{4,7},{5,6},{6,5},{7,4},{8,11},{9,10},{10,... | collective-permute-start | bytes 1105928 | tf_op jit(solution)/shard_map/ppermute | solution.py:465
  158.4 14.0 %collective-permute-start.22 = (bf16[96,1920]{1,0:T(8,128)(2,1)S(1)}, bf16[96,1920]{1,0:T(8,128)(2,1)S(1)}, u32[]{:S(2)}, u32[]{:S(2)}) collective-permute-start(bf16[96,1920]{1,0:T(8,128)(2,1)S(1)} %get-tuple-element.200), channel_id=1, source_target_pairs={{0,5},{1,4},{2,7},{3,6},{4,1},{5,0},{6,3},{7,2},{8,13},{9,12},{10,... | collective-permute-start | bytes 1105928 | tf_op jit(solution)/shard_map/ppermute | solution.py:465
  159.5 25.9 %collective-permute-start.30 = (bf16[192,1536]{1,0:T(8,128)(2,1)S(1)}, bf16[192,1536]{1,0:T(8,128)(2,1)S(1)}, u32[]{:S(2)}, u32[]{:S(2)}) collective-permute-start(bf16[192,1536]{1,0:T(8,128)(2,1)S(1)} %shard_map.136.own_ref), channel_id=1, source_target_pairs={{8,0},{16,24},{9,1},{17,25},{10,2},{18,26},{11,3},{19,27},{12,4},{... | collective-permute-start | bytes 1769480 | tf_op jit(solution)/shard_map/ppermute | solution.py:503
  171.2 25.0 %collective-permute-start.28 = (bf16[96,1920]{1,0:T(8,128)(2,1)S(1)}, bf16[96,1920]{1,0:T(8,128)(2,1)}, u32[]{:S(2)}, u32[]{:S(2)}) collective-permute-start(bf16[96,1920]{1,0:T(8,128)(2,1)S(1)} %get-tuple-element.215), channel_id=1, source_target_pairs={{0,7},{1,6},{2,5},{3,4},{4,3},{5,2},{6,1},{7,0},{8,15},{9,14},{10,... | collective-permute-start | bytes 1105928 | tf_op jit(solution)/shard_map/ppermute | solution.py:465
  171.3 2.5 %copy-start.21 = (bf16[96,192]{1,0:T(8,128)(2,1)S(1)}, bf16[96,192]{1,0:T(8,128)(2,1)}, u32[]{:S(2)}) copy-start(bf16[96,192]{1,0:T(8,128)(2,1)} %copy-done.20) | copy-start | bytes 110596
  171.3 2.5 %copy-start.23 = (bf16[96,192]{1,0:T(8,128)(2,1)S(1)}, bf16[96,192]{1,0:T(8,128)(2,1)}, u32[]{:S(2)}) copy-start(bf16[96,192]{1,0:T(8,128)(2,1)} %copy-done.22) | copy-start | bytes 110596
  171.4 24.8 %collective-permute-start.27 = (bf16[96,1920]{1,0:T(8,128)(2,1)S(1)}, bf16[96,1920]{1,0:T(8,128)(2,1)}, u32[]{:S(2)}, u32[]{:S(2)}) collective-permute-start(bf16[96,1920]{1,0:T(8,128)(2,1)S(1)} %get-tuple-element.211), channel_id=1, source_target_pairs={{0,6},{1,7},{2,4},{3,5},{4,2},{5,3},{6,0},{7,1},{8,14},{9,15},{10,... | collective-permute-start | bytes 1105928 | tf_op jit(solution)/shard_map/ppermute | solution.py:465
  172.4 21.0 %collective-permute-start.29 = (bf16[192,1536]{1,0:T(8,128)(2,1)S(1)}, bf16[192,1536]{1,0:T(8,128)(2,1)S(1)}, u32[]{:S(2)}, u32[]{:S(2)}) collective-permute-start(bf16[192,1536]{1,0:T(8,128)(2,1)S(1)} %shard_map.139.own_ref), channel_id=1, source_target_pairs={{8,0},{16,24},{9,1},{17,25},{10,2},{18,26},{11,3},{19,27},{12,4},{... | collective-permute-start | bytes 1769480 | tf_op jit(solution)/shard_map/ppermute | solution.py:503
  175.3 3.3 %copy-start.17 = (bf16[576,1792]{1,0:T(8,128)(2,1)S(1)}, bf16[576,1792]{1,0:T(8,128)(2,1)}, u32[]{:S(2)}) copy-start(bf16[576,1792]{1,0:T(8,128)(2,1)} %copy-done.16) | copy-start | bytes 6193156
  178.6 3.4 %copy-start.7 = (bf16[192,1024]{1,0:T(8,128)(2,1)S(1)}, bf16[192,1024]{1,0:T(8,128)(2,1)}, u32[]{:S(2)}) copy-start(bf16[192,1024]{1,0:T(8,128)(2,1)} %copy-done.6) | copy-start | bytes 1179652
  193.4 5.5 %copy-start.18 = (bf16[96,192]{1,0:T(8,128)(2,1)S(1)}, bf16[96,192]{1,0:T(8,128)(2,1)}, u32[]{:S(2)}) copy-start(bf16[96,192]{1,0:T(8,128)(2,1)} %get-tuple-element.255) | copy-start | bytes 110596
  193.4 5.5 %copy-start.19 = (bf16[96,192]{1,0:T(8,128)(2,1)S(1)}, bf16[96,192]{1,0:T(8,128)(2,1)}, u32[]{:S(2)}) copy-start(bf16[96,192]{1,0:T(8,128)(2,1)} %get-tuple-element.256) | copy-start | bytes 110596
  195.6 18.1 %collective-permute-start.31 = (bf16[96,1920]{1,0:T(8,128)(2,1)S(1)}, bf16[96,1920]{1,0:T(8,128)(2,1)S(1)}, u32[]{:S(2)}, u32[]{:S(2)}) collective-permute-start(bf16[96,1920]{1,0:T(8,128)(2,1)S(1)} %get-tuple-element.241), channel_id=1, source_target_pairs={{0,2},{1,3},{2,0},{3,1},{4,6},{5,7},{6,4},{7,5},{8,10},{9,11},{10,... | collective-permute-start | bytes 1105928 | tf_op jit(solution)/shard_map/ppermute | solution.py:465
  198.1 15.5 %collective-permute-start.32 = (bf16[96,1920]{1,0:T(8,128)(2,1)S(1)}, bf16[96,1920]{1,0:T(8,128)(2,1)S(1)}, u32[]{:S(2)}, u32[]{:S(2)}) collective-permute-start(bf16[96,1920]{1,0:T(8,128)(2,1)S(1)} %get-tuple-element.244), channel_id=1, source_target_pairs={{0,4},{1,5},{2,6},{3,7},{4,0},{5,1},{6,2},{7,3},{8,12},{9,13},{10,... | collective-permute-start | bytes 1105928 | tf_op jit(solution)/shard_map/ppermute | solution.py:465
  208.2 6.0 %copy-start.31 = (s32[192,2]{0,1:T(2,128)S(1)}, s32[192,2]{0,1:T(2,128)}, u32[]{:S(2)}) copy-start(s32[192,2]{0,1:T(2,128)} %param.9) | copy-start | bytes 4612
  208.2 6.6 %copy-start.25 = (bf16[96,192]{1,0:T(8,128)(2,1)S(1)}, bf16[96,192]{1,0:T(8,128)(2,1)}, u32[]{:S(2)}) copy-start(bf16[96,192]{1,0:T(8,128)(2,1)} %copy-done.24) | copy-start | bytes 110596
  208.2 6.6 %copy-start.27 = (bf16[96,192]{1,0:T(8,128)(2,1)S(1)}, bf16[96,192]{1,0:T(8,128)(2,1)}, u32[]{:S(2)}) copy-start(bf16[96,192]{1,0:T(8,128)(2,1)} %copy-done.26) | copy-start | bytes 110596
  212.7 2.1 copy-start.14
  (7 other events, 9.9 us)
